TPU v7x, 32 devices: a whole 2x2x4 slice. The times are simulated.
32 devices in a mesh: item: 4 (over y, x), row: 4 (over z), pair: 2 (over core).
Axes of the slice: x: 2, y: 2, z: 4, core: 2. Of those that a mesh axis runs over, the one named last changes fastest.
Arguments:
- image: bfloat16 [4, 32, 512, 128], P('item', 'row', 'pair'), may hold values from -6 to 6
- land_mask: int32 [4, 32, 512], P('item', 'row', 'pair'), may hold values 0 or 1
- embedding: bfloat16 [4, 512], P('item'), may hold values from -6 to 6
- input_gain: float32 [128], replicated, may hold values from 0.5 to 1.5
- input_shift: float32 [128], replicated, may hold values from -3 to 3
- first_kernel: bfloat16 [3, 3, 128, 256], replicated, may hold values from -0.1875 to 0.1875
- first_bias: float32 [256], replicated, may hold values from -3 to 3
- film_weight: bfloat16 [512, 512], replicated, may hold values from -0.125 to 0.125
- film_bias: float32 [512], replicated, may hold values from -1.75 to 1.75
- middle_gain: float32 [256], replicated, may hold values from 0.5 to 1.5
- middle_shift: float32 [256], replicated, may hold values from -3 to 3
- second_kernel: bfloat16 [3, 3, 256, 256], replicated, may hold values from -0.125 to 0.125
- second_bias: float32 [256], replicated, may hold values from -3 to 3
- skip_weight: bfloat16 [128, 256], replicated, may hold values from -0.5 to 0.5
- skip_bias: float32 [256], replicated, may hold values from -3 to 3
- features: bfloat16 [4, 64, 64, 256], P('item', 'row', 'pair'), may hold values from -6 to 6
- token_land: int32 [4, 64, 64], P('item', 'row', 'pair'), may hold values 0 or 1
- attend_gain: float32 [256], replicated, may hold values from 0.5 to 1.5
- attend_shift: float32 [256], replicated, may hold values from -3 to 3
- mixing_weight: bfloat16 [256, 768], replicated, may hold values from -0.375 to 0.375
- mixing_bias: float32 [512], replicated, may hold values from -1.75 to 1.75
- output_weight: bfloat16 [256, 256], replicated, may hold values from -6 to 6
- output_bias: float32 [256], replicated, may hold values from -1.75 to 1.75
- grad_pooled: bfloat16 [4, 16, 256, 256], P('item', 'row', 'pair'), may hold values from -6 to 6
- grad_result: bfloat16 [4, 64, 64, 256], P('item', 'row', 'pair'), may hold values from -6 to 6
Outputs:
- pooled: bfloat16 [4, 16, 256, 256], P('item', 'row', 'pair')
- result: bfloat16 [4, 64, 64, 256], P('item', 'row', 'pair')
- image_grad: bfloat16 [4, 32, 512, 128], P('item', 'row', 'pair')
- features_grad: bfloat16 [4, 64, 64, 256], P('item', 'row', 'pair')
- input_gain_grad: float32 [128], replicated
- input_shift_grad: float32 [128], replicated
- first_kernel_grad: float32 [3, 3, 128, 256], replicated
- first_bias_grad: float32 [256], replicated
- film_weight_grad: float32 [512, 512], replicated
- film_bias_grad: float32 [512], replicated
- middle_gain_grad: float32 [256], replicated
- middle_shift_grad: float32 [256], replicated
- second_kernel_grad: float32 [3, 3, 256, 256], replicated
- second_bias_grad: float32 [256], replicated
- skip_weight_grad: float32 [128, 256], replicated
- skip_bias_grad: float32 [256], replicated
- attend_gain_grad: float32 [256], replicated
- attend_shift_grad: float32 [256], replicated
- mixing_weight_grad: float32 [256, 768], replicated
- mixing_bias_grad: float32 [512], replicated
- output_weight_grad: float32 [256, 256], replicated
- output_bias_grad: float32 [256], replicated
- rms_values: float32 [5], replicated
All inputs are finite; a program needn't handle non-finite values. No bound on the sum of `land_mask` or of `token_land` on one device may be relied on, other than what follows from the above.
Results may differ from a plain program's by a relative error of at most 0.012.
The roundings to bfloat16 on the way count: a program that leaves them out, or rounds other values in their place, can miss the bound.
Values may be sent and summed in bfloat16 or wider, within the bound.
A program may use at most 128 MiB of HBM per device.

v0:
```python
import functools
import math
from types import SimpleNamespace

import jax
import jax.numpy as jnp
from jax import lax
from jax.experimental import pallas as pl
from jax.experimental.pallas import tpu as pltpu
from jax.sharding import PartitionSpec as P

GROUPS = 32
EPS = 1e-05
MASKED = -1000000000.0
LOG2E = 1.4426950408889634
F32 = jnp.float32
BF16 = jnp.bfloat16
MESH = pl.DeviceIdType.MESH
HIGHEST = lax.Precision.HIGHEST


def mm(left, right):
    return jnp.dot(left, right, preferred_element_type=F32)


def mm_t(left, right):
    return lax.dot_general(left, right, (((1,), (1,)), ((), ())), preferred_element_type=F32)


def iota(shape, dim):
    return lax.broadcasted_iota(jnp.int32, shape, dim)


def fold(value):
    rows, width = value.shape
    return jnp.sum(value.reshape(rows // 8, 8, width), axis=0)


def total(value):
    return jnp.sum(value, axis=0, keepdims=True)


def group_total(rows, width):
    channels = rows.shape[-1]
    left = jnp.floor(iota((channels, channels), 0).astype(F32) * (1.0 / width))
    right = jnp.floor(iota((channels, channels), 1).astype(F32) * (1.0 / width))
    same = (left == right).astype(F32)
    padded = jnp.concatenate([rows, jnp.zeros((8 - rows.shape[0], channels), F32)], axis=0)
    return jnp.dot(padded, same, precision=HIGHEST, preferred_element_type=F32)


def sigmoid(value):
    return 0.5 * jnp.tanh(0.5 * value) + 0.5


INPUTS = (
    "image", "land", "embedding", "gain1", "shift1", "kernel1", "bias1", "film_w", "film_b",
    "gain2", "shift2", "kernel2", "bias2", "skip_w", "skip_b", "features", "token", "gain3",
    "shift3", "mix_w", "mix_b", "out_w", "out_b", "gpool", "gres",
)
RESULTS = ("pooled", "result", "image_grad", "features_grad", "sum_a", "sum_b", "sum_c", "vectors")


class Links:
    def __init__(self, ref, n_item, n_row):
        self.ref = ref
        self.n_item, self.n_row, self.n_group = n_item, n_row, n_row * 2
        self.item, self.row, self.pair = (lax.axis_index(a) for a in ("item", "row", "pair"))
        self.sibling = 1 - self.pair
        self.slot = self.row * 2 + self.pair
        self.sends = 0
        self.recvs = 0
        self.pending = []

    def new_send(self):
        self.sends += 1
        return self.sends - 1

    def new_recv(self, count=1):
        self.recvs += count
        return self.recvs - count

    def send(self, source, target, device, recv, when=None):
        index = self.new_send()

        def make():
            return pltpu.make_async_remote_copy(
                src_ref=source,
                dst_ref=target,
                send_sem=self.ref.send_sem.at[index],
                recv_sem=self.ref.recv_sem.at[recv],
                device_id=device,
                device_id_type=MESH,
            )

        if when is None:
            make().start()
        else:
            pl.when(when)(lambda: make().start())
        self.pending.append((make, when))

    def arrived(self, target, recv, when=None):
        def wait():
            pltpu.make_async_remote_copy(
                src_ref=target,
                dst_ref=target,
                send_sem=self.ref.send_sem.at[0],
                recv_sem=self.ref.recv_sem.at[recv],
                device_id=(self.item, self.row, self.sibling),
                device_id_type=MESH,
            ).wait_recv()

        if when is None:
            wait()
        else:
            pl.when(when)(wait)

    def finish(self):
        for make, when in self.pending:
            if when is None:
                make().wait_send()
            else:
                pl.when(when)(lambda make=make: make().wait_send())

    def barrier(self):
        sem = pltpu.get_barrier_semaphore()
        count = 0
        for step in range(1, self.n_group):
            other = lax.rem(self.slot + step, self.n_group)
            device = (self.item, lax.div(other, 2), lax.rem(other, 2))
            pl.semaphore_signal(sem, inc=1, device_id=device, device_id_type=MESH)
            count += 1
        for step in range(1, self.n_item):
            device = (lax.rem(self.item + step, self.n_item), self.row, self.pair)
            pl.semaphore_signal(sem, inc=1, device_id=device, device_id_type=MESH)
            count += 1
        pl.semaphore_wait(sem, count)

    def share(self, slots, source=None):
        base = self.new_recv(self.n_group)
        mine = slots.at[self.slot]
        for step in range(1, self.n_group):
            other = lax.rem(self.slot + step, self.n_group)
            device = (self.item, lax.div(other, 2), lax.rem(other, 2))
            self.send(mine if source is None else source, mine, device, base + self.slot)

        def wait():
            for step in range(1, self.n_group):
                other = lax.rem(self.slot + step, self.n_group)
                self.arrived(slots.at[other], base + other)

        return wait

    def edge_rows(self, first, last, above, below):
        has_above, has_below = self.row > 0, self.row < self.n_row - 1
        from_above, from_below = self.new_recv(), self.new_recv()
        self.send(first, below, (self.item, self.row - 1, self.pair), from_below, has_above)
        self.send(last, above, (self.item, self.row + 1, self.pair), from_above, has_below)

        def wait():
            self.arrived(above, from_above, has_above)
            self.arrived(below, from_below, has_below)

            @pl.when(self.row == 0)
            def _():
                above[...] = jnp.zeros(above.shape, above.dtype)

            @pl.when(self.row == self.n_row - 1)
            def _():
                below[...] = jnp.zeros(below.shape, below.dtype)

        return wait

    def edge_columns(self, column, columns):
        has_above, has_below = self.row > 0, self.row < self.n_row - 1
        base = self.new_recv(3)
        self.send(column, columns.at[1], (self.item, self.row, self.sibling), base + 1)
        self.send(column, columns.at[2], (self.item, self.row - 1, self.sibling), base + 2, has_above)
        self.send(column, columns.at[0], (self.item, self.row + 1, self.sibling), base, has_below)

        def wait():
            self.arrived(columns.at[1], base + 1)
            self.arrived(columns.at[0], base, has_above)
            self.arrived(columns.at[2], base + 2, has_below)

            @pl.when(self.row == 0)
            def _():
                columns[0] = jnp.zeros(columns.shape[1:], columns.dtype)

            @pl.when(self.row == self.n_row - 1)
            def _():
                columns[2] = jnp.zeros(columns.shape[1:], columns.dtype)

        return wait

    def all_sum(self, part, recv1, sum1, recv2, recv3, out):
        blocks = part.shape[0]
        half = blocks // 2
        quarter = half // self.n_item
        chunk = quarter // self.n_row
        item_at, row_at = self.item * quarter, self.row * chunk
        own = self.pair * half + item_at + row_at

        def span(ref, start, size):
            return ref.at[pl.ds(start, size)]

        def stage1():
            sem = self.new_recv()
            self.send(span(part, self.sibling * half, half), recv1, (self.item, self.row, self.sibling), sem)

            def stage2():
                self.arrived(recv1, sem)
                sum1[...] = (part[pl.ds(self.pair * half, half)].astype(F32) + recv1[...].astype(F32)).astype(BF16)
                base = self.new_recv(self.n_item - 1)
                for step in range(1, self.n_item):
                    other = lax.rem(self.item + step, self.n_item)
                    self.send(
                        span(sum1, other * quarter, quarter), recv2.at[step - 1],
                        (other, self.row, self.pair), base + step - 1,
                    )

                def stage3():
                    value = sum1[pl.ds(item_at, quarter)].astype(F32)
                    for step in range(1, self.n_item):
                        self.arrived(recv2.at[step - 1], base + step - 1)
                        value = value + recv2[step - 1].astype(F32)
                    sum1[pl.ds(item_at, quarter)] = value.astype(BF16)
                    base3 = self.new_recv(self.n_row - 1)
                    for step in range(1, self.n_row):
                        other = lax.rem(self.row + step, self.n_row)
                        self.send(
                            span(sum1, item_at + other * chunk, chunk), recv3.at[step - 1],
                            (self.item, other, self.pair), base3 + step - 1,
                        )

                    def stage4():
                        value = sum1[pl.ds(item_at + row_at, chunk)].astype(F32)
                        for step in range(1, self.n_row):
                            self.arrived(recv3.at[step - 1], base3 + step - 1)
                            value = value + recv3[step - 1].astype(F32)
                        out[pl.ds(own, chunk)] = value.astype(BF16)
                        base4 = self.new_recv(self.n_row)
                        for step in range(1, self.n_row):
                            other = lax.rem(self.row + step, self.n_row)
                            self.send(
                                span(out, own, chunk), span(out, own, chunk),
                                (self.item, other, self.pair), base4 + self.row,
                            )

                        def stage5():
                            for step in range(1, self.n_row):
                                other = lax.rem(self.row + step, self.n_row)
                                self.arrived(
                                    span(out, self.pair * half + item_at + other * chunk, chunk), base4 + other
                                )
                            base5 = self.new_recv(self.n_item)
                            mine = span(out, self.pair * half + item_at, quarter)
                            for step in range(1, self.n_item):
                                other = lax.rem(self.item + step, self.n_item)
                                self.send(mine, mine, (other, self.row, self.pair), base5 + self.item)

                            def stage6():
                                for step in range(1, self.n_item):
                                    other = lax.rem(self.item + step, self.n_item)
                                    self.arrived(
                                        span(out, self.pair * half + other * quarter, quarter), base5 + other
                                    )
                                sem6 = self.new_recv()
                                whole = span(out, self.pair * half, half)
                                self.send(whole, whole, (self.item, self.row, self.sibling), sem6)

                                def stage7():
                                    self.arrived(span(out, self.sibling * half, half), sem6)

                                return stage7

                            return stage6

                        return stage5

                    return stage4

                return stage3

            return stage2

        return stage1()


def norm_terms(sums, squares, count, width):
    size = jnp.maximum(count, 1.0) * width
    grouped = group_total(jnp.concatenate([sums, squares], axis=0), width)
    mean = grouped[0:1] / size
    return mean, lax.rsqrt(grouped[1:2] / size - mean * mean + EPS), size


def main_kernel(n_item, n_row, *refs):
    names = INPUTS + RESULTS + SCRATCH
    ref = SimpleNamespace(**dict(zip(names, refs)))
    link = Links(ref, n_item, n_row)
    height, span, c_in = ref.image.shape
    channels = ref.bias1.shape[-1]
    half = span // 2
    tokens = ref.features.shape[0]
    n_group = link.n_group
    low, high = height // 2, half
    side = link.pair.astype(F32)
    width1, width2 = c_in // GROUPS, channels // GROUPS
    slot = link.slot
    factor = channels ** (-0.5)

    link.barrier()

    wait_token = link.share(ref.flags, ref.token)
    wait_image_rows = link.edge_rows(ref.image.at[0], ref.image.at[height - 1], ref.image_up, ref.image_down)
    wait_pool_rows = link.edge_rows(ref.gpool.at[0], ref.gpool.at[low - 1], ref.pool_up, ref.pool_down)
    feature_sem = link.new_recv(n_group)
    link.send(ref.features, ref.raw.at[slot], (link.item, link.row, link.sibling), feature_sem + slot)
    for step in range(1, n_row):
        other = lax.rem(link.row + step, n_row)
        link.send(ref.features, ref.raw.at[slot], (link.item, other, link.pair), feature_sem + slot)
    ref.flags[slot] = ref.token[...]
    ref.raw[slot] = ref.features[...]

    ones = jnp.ones((span, 128), BF16)
    place = iota((span, span), 0)
    place = jnp.where(place < half, 2 * place, 2 * (place - half) + 1)
    spread = place == iota((span, span), 1)

    def land_row(y, carry):
        line = jnp.broadcast_to(ref.land[pl.ds(y, 1), :].astype(F32), (span, span))
        ref.mask[y] = mm(jnp.where(spread, line, 0.0).astype(BF16), ones)
        return carry

    lax.fori_loop(0, height, land_row, 0)

    rows_t, cols_t = ref.token.shape

    def token_mask(flags):
        pick = iota((rows_t, cols_t, rows_t), 0) == iota((rows_t, cols_t, rows_t), 2)
        lines = mm(pick.reshape(tokens, rows_t).astype(BF16), flags.astype(F32).astype(BF16))
        keep = (iota((rows_t, cols_t, cols_t), 1) == iota((rows_t, cols_t, cols_t), 2)).reshape(tokens, cols_t)
        return mm(jnp.where(keep, lines, 0.0).astype(BF16), jnp.ones((cols_t, 128), BF16))

    ref.token_mask[...] = token_mask(ref.token[...])

    def split_row(y, row):
        ref.line[...] = row.astype(F32)
        even = ref.line[pl.ds(0, half, stride=2), :]
        odd = ref.line[pl.ds(1, half, stride=2), :]
        ref.normed1[y, 0:half] = even
        ref.normed1[y, half:span] = odd
        return even, odd

    def image_row(y, carry):
        sums, squares, count = carry
        even, odd = split_row(y + 1, ref.image[y])
        value = jnp.concatenate([even, odd], axis=0)
        ref.image_low[y] = value.astype(BF16)
        ref.column1[pl.ds(y, 1), :] = jnp.where(side > 0.5, even[0:1], odd[half - 1 : half])
        mask = ref.mask[y]
        masked = value * mask
        return sums + fold(masked), squares + fold(masked * value), count + fold(mask)

    zero1 = jnp.zeros((8, c_in), F32)
    zero2 = jnp.zeros((8, channels), F32)
    sums1, squares1, count1 = lax.fori_loop(0, height, image_row, (zero1, zero1, jnp.zeros((8, 128), F32)))
    wait_image_columns = link.edge_columns(ref.column1, ref.columns1)
    raw = ref.features[...].astype(F32)
    tmask = ref.token_mask[...]
    tmask2 = jnp.concatenate([tmask] * (channels // 128), axis=1)
    masked = raw * tmask2
    ref.stats1[slot] = jnp.zeros((8, channels), F32)
    ref.stats1[slot, 0:1, 0:c_in] = total(sums1)
    ref.stats1[slot, 0:1, c_in:channels] = total(squares1)
    ref.stats1[slot, 1:2, :] = total(masked)
    ref.stats1[slot, 2:3, :] = total(masked * raw)
    ref.stats1[slot, 3:4, 0:128] = total(count1)
    ref.stats1[slot, 3:4, 128:256] = total(tmask)
    wait_stats1 = link.share(ref.stats1)

    for i in range(low):
        value = (ref.gpool[i].astype(F32) * 0.25 * math.sqrt(0.5)).astype(BF16)
        ref.gpre[i] = value
        ref.gpre_t[:, i * half : (i + 1) * half] = value.T
        wide = value.astype(F32)
        ref.column2[i : i + 1, :] = jnp.where(side > 0.5, wide[0:1], wide[half - 1 : half])
    wait_pool_columns = link.edge_columns(ref.column2, ref.columns2)
    gpre_sum = zero2
    for i in range(low):
        gpre_sum = gpre_sum + fold(ref.gpre[i].astype(F32))

    coarse = ref.probs if n_group >= 8 and tokens >= 2 * channels else ref.coarse

    upper, lower = {0: (2,), 1: (1, 2)}, {0: (0, 1), 1: (0,)}
    for u in range(2):
        for line, row_taps in enumerate((upper[u], lower[u])):
            tall = []
            for b in range(3):
                tile = sum(ref.kernel2[a, b * channels : (b + 1) * channels, :].astype(F32) for a in row_taps)
                tall.append(tile)
            for v in range(2):
                for place_x, column_taps in enumerate((upper[v], lower[v])):
                    tile = sum(tall[b] for b in column_taps)
                    coarse[u * 4 + v * 2 + line, 0:channels, place_x * channels : (place_x + 1) * channels] = tile.astype(BF16)

    wait_pool_rows()
    wait_pool_columns()
    first_row = iota((half, channels), 0) == 0
    last_row = iota((half, channels), 0) == half - 1
    for i in range(low + 2):
        if i == 0:
            value, edge = ref.pool_up[...], ref.columns2[0, low - 1 : low, :]
        elif i == low + 1:
            value, edge = ref.pool_down[...], ref.columns2[2, 0:1, :]
        else:
            value, edge = ref.gpre[i - 1], ref.columns2[1, i - 1 : i, :]
        if i in (0, low + 1):
            value = (value.astype(F32) * 0.25 * math.sqrt(0.5)).astype(BF16)
        wide = value.astype(F32)
        left = jnp.where(first_row, edge * side, pltpu.roll(wide, 1, 0))
        right = jnp.where(last_row, edge * (1.0 - side), pltpu.roll(wide, half - 1, 0))
        ref.padded_g[i, :, 0:channels] = left.astype(BF16)
        ref.padded_g[i, :, channels : 2 * channels] = value
        ref.padded_g[i, :, 2 * channels : 3 * channels] = right.astype(BF16)
    for u in range(2):
        for v in range(2):
            value = 0.0
            for line in range(2):
                rows = ref.padded_g[u + line : u + line + low, :, v * channels : (v + 2) * channels]
                value = value + mm_t(rows.reshape(low * half, 2 * channels), coarse[u * 4 + v * 2 + line, 0:channels, 0 : 2 * channels])
            for i in range(low):
                ref.grad2[2 * i + u, v * half : (v + 1) * half, :] = value[i * half : (i + 1) * half]

    wait_image_rows()
    wait_image_columns()
    wait_stats1()
    stats = ref.stats1[0]
    for other in range(1, n_group):
        stats = stats + ref.stats1[other]
    count_land = jnp.concatenate([stats[3:4, 0:128]] * (channels // 128), axis=1)
    count_token = jnp.concatenate([stats[3:4, 128:256]] * (channels // 128), axis=1)
    mean1, inv1, size1 = norm_terms(stats[0:1, 0:c_in], stats[0:1, c_in:channels], count_land[:, 0:c_in], width1)
    mean3, inv3, size3 = norm_terms(stats[1:2], stats[2:3], count_token, width2)
    split_row(0, ref.image_up[...])
    split_row(height + 1, ref.image_down[...])
    gain1, shift1 = ref.gain1[...], ref.shift1[...]

    def write_shifted(target, y, even, odd, edge, size):
        top = iota((half, size), 0) == 0
        end = iota((half, size), 0) == half - 1
        before = jnp.where(top, edge * side, pltpu.roll(odd, 1, 0)).astype(BF16)
        after = jnp.where(end, edge * (1.0 - side), pltpu.roll(even, half - 1, 0)).astype(BF16)
        even, odd = even.astype(BF16), odd.astype(BF16)
        target[y, 0:half, 0:size] = before
        target[y, 0:half, size : 2 * size] = even
        target[y, 0:half, 2 * size : 3 * size] = odd
        target[y, half:span, 0:size] = even
        target[y, half:span, size : 2 * size] = odd
        target[y, half:span, 2 * size : 3 * size] = after

    def act1(value):
        normed = (value - mean1) * inv1
        affine = normed * gain1 + shift1
        gate = sigmoid(affine)
        return normed, affine, gate

    def edge_act(rows):
        _, affine, gate = act1(rows)
        return affine * gate

    has_up = (link.row > 0).astype(F32)
    has_down = (link.row < n_row - 1).astype(F32)
    ref.columns1[0] = edge_act(ref.columns1[0]) * has_up
    ref.columns1[1] = edge_act(ref.columns1[1])
    ref.columns1[2] = edge_act(ref.columns1[2]) * has_down

    def act1_edge_row(y, edge, exists):
        _, affine, gate = act1(ref.normed1[y])
        act = affine * gate * exists
        write_shifted(ref.padded1, y, act[0:half], act[half:span], edge, c_in)

    act1_edge_row(0, ref.columns1[0, height - 1 : height, :], has_up)
    act1_edge_row(height + 1, ref.columns1[2, 0:1, :], has_down)

    def act1_row(y, carry):
        normed, affine, gate = act1(ref.normed1[y + 1])
        act = affine * gate
        ref.normed1[y + 1] = normed
        ref.slope1[y] = gate * (1.0 + affine * (1.0 - gate))
        write_shifted(ref.padded1, y + 1, act[0:half], act[half:span], ref.columns1[1, pl.ds(y, 1), :], c_in)
        return carry

    lax.fori_loop(0, height, act1_row, 0)

    def wide_mask(y):
        mask = ref.mask[y]
        return jnp.concatenate([mask] * (channels // 128), axis=1)

    def conv1_row(y, carry):
        sums, squares = carry
        value = mm(ref.padded1[y], ref.kernel1[0])
        value = value + mm(ref.padded1[y + 1], ref.kernel1[1])
        value = value + mm(ref.padded1[y + 2], ref.kernel1[2])
        value = value + ref.bias1[...]
        ref.hidden[y] = value
        masked = value * wide_mask(y)
        return sums + fold(masked), squares + fold(masked * value)

    sums2, squares2 = lax.fori_loop(0, height, conv1_row, (zero2, zero2))
    ref.stats2[slot] = jnp.zeros((8, channels), F32)
    ref.stats2[slot, 0:1, :] = total(sums2)
    ref.stats2[slot, 1:2, :] = total(squares2)
    wait_stats2 = link.share(ref.stats2)

    gain3, shift3 = ref.gain3[...], ref.shift3[...]
    scale3 = inv3 * gain3

    def normalize(index):
        value = ((ref.raw[index].astype(F32) - mean3) * scale3 + shift3).astype(BF16)
        ref.tokens[index] = value
        ref.tokens_t[index] = value.T

    normalize(slot)
    mine = ref.tokens[slot]
    w_query = ref.mix_w[:, 0:channels]
    w_key = ref.mix_w[:, channels : 2 * channels]
    w_value = ref.mix_w[:, 2 * channels : 3 * channels]
    ref.query[...] = (mm(mine, w_query) + ref.mix_b[:, 0:channels]).astype(BF16)
    ref.query_t[...] = (mm_t(w_key, ref.query[...]) * (factor * LOG2E)).astype(BF16)
    alive = (count_token > 0.0).astype(F32) * factor
    ref.query_k[...] = (mm_t(ref.query[...], w_key) * alive).astype(BF16)
    ref.grad_att[...] = mm_t(ref.gres[...], ref.out_w[...]).astype(BF16)
    ref.grad_t[...] = mm_t(w_value, ref.grad_att[...])

    lines = jnp.broadcast_to(ref.embedding[...], (8, ref.embedding.shape[-1]))
    film = mm(lines, ref.film_w[...])[0:1] + ref.film_b[...]
    film_scale = 1.0 + film[:, 0:channels]
    film_shift = film[:, channels:]

    wait_stats2()
    stats = ref.stats2[0]
    for other in range(1, n_group):
        stats = stats + ref.stats2[other]
    mean2, inv2, size2 = norm_terms(stats[0:1], stats[1:2], count_land, width2)
    slope_m = ref.gain2[...] * film_scale
    shift_m = ref.shift2[...] * film_scale + film_shift

    def mid_row(y, carry):
        grad_sum, grad_dot = carry
        normed = (ref.hidden[y] - mean2) * inv2
        affine = normed * slope_m + shift_m
        gate = sigmoid(affine)
        act = affine * gate
        grad = ref.grad2[y] * (gate * (1.0 + affine * (1.0 - gate)))
        ref.hidden[y] = normed
        ref.grad2[y] = grad
        ref.act2[y] = act.astype(BF16)
        edge = jnp.where(side > 0.5, act[0:1], act[span - 1 : span])
        ref.column3[pl.ds(y, 1), :] = edge
        return grad_sum + fold(grad), grad_dot + fold(grad * normed)

    grad_sum2, grad_dot2 = lax.fori_loop(0, height, mid_row, (zero2, zero2))
    ref.stats3[slot] = jnp.zeros((8, channels), F32)
    ref.stats3[slot, 0:1, :] = total(grad_sum2)
    ref.stats3[slot, 1:2, :] = total(grad_dot2)
    wait_stats3 = link.share(ref.stats3)
    wait_act_rows = link.edge_rows(ref.act2.at[0], ref.act2.at[height - 1], ref.act_up, ref.act_down)
    wait_act_columns = link.edge_columns(ref.column3, ref.columns3)

    for a in range(3):
        for b in range(3):
            ref.kernel1_t[2 - a, :, (2 - b) * channels : (3 - b) * channels] = ref.kernel1[
                a, b * c_in : (b + 1) * c_in, :
            ]

    wait_stats3()
    stats = ref.stats3[0]
    for other in range(1, n_group):
        stats = stats + ref.stats3[other]
    grad_sum2, grad_dot2 = stats[0:1], stats[1:2]
    grouped = group_total(jnp.concatenate([grad_sum2 * slope_m, grad_dot2 * slope_m], axis=0), width2)
    first2, second2 = grouped[0:1] / size2, grouped[1:2] / size2

    def hidden_row(y, carry):
        normed = ref.hidden[y]
        grad = ref.grad2[y] * slope_m - wide_mask(y) * (first2 + normed * second2)
        grad = (grad * inv2).astype(BF16)
        ref.grad_hidden[y] = grad
        ref.grad_hidden_t[y] = grad.T
        wide = grad.astype(F32)
        ref.column4[pl.ds(y, 1), :] = jnp.where(side > 0.5, wide[0:1], wide[span - 1 : span])
        return carry + fold(wide)

    bias1_sum = lax.fori_loop(0, height, hidden_row, zero2)
    wait_hidden_rows = link.edge_rows(
        ref.grad_hidden.at[0], ref.grad_hidden.at[height - 1], ref.hidden_up, ref.hidden_down
    )
    wait_hidden_columns = link.edge_columns(ref.column4, ref.columns4)

    def pad_rows(target, source, up, down, columns):
        def edge_row(y, row, edge):
            row = row.astype(F32)
            write_shifted(target, y, row[0:half], row[half:span], edge, channels)

        edge_row(0, up[...], columns[0, height - 1 : height, :])
        edge_row(height + 1, down[...], columns[2, 0:1, :])

        def body(y, carry):
            edge_row(y + 1, source[y], columns[1, pl.ds(y, 1), :])
            return carry

        lax.fori_loop(0, height, body, 0)

    wait_act_rows()
    wait_act_columns()
    pad_rows(ref.padded2, ref.act2, ref.act_up, ref.act_down, ref.columns3)

    def box_row(i, carry):
        for a in range(3):
            value = 0.0
            for dy in range(2):
                for side_x in range(2):
                    row = ref.padded2[2 * i + a + dy, side_x * half : (side_x + 1) * half, :]
                    value = value + row.astype(F32)
            ref.boxes[a, i] = value.astype(BF16)
        value = 0.0
        for dy in range(2):
            for side_x in range(2):
                value = value + ref.image_low[2 * i + dy, side_x * half : (side_x + 1) * half, :].astype(F32)
        ref.image_box[i] = value.astype(BF16)
        return carry

    lax.fori_loop(0, low, box_row, 0)

    def kernel2_grad(a, carry):
        value = mm(ref.gpre_t[...], ref.boxes[a].reshape(low * half, 3 * channels)).T
        rows = 3 * channels // 16
        for lane in range(channels // 128):
            piece = value[:, lane * 128 : (lane + 1) * 128].astype(BF16).reshape(rows, 16, 128)
            ref.part_a[pl.ds(lane * 3 * rows + a * rows, rows)] = piece
        return carry

    lax.fori_loop(0, 3, kernel2_grad, 0)
    next_a = link.all_sum(ref.part_a, ref.recv1_a, ref.sum1_a, ref.recv2_a, ref.recv3_a, ref.sum_a)

    rows_c = 10 * c_in // 16

    def kernel1_grad(a, carry):
        value = 0.0
        for y in range(height):
            value = value + mm(ref.grad_hidden_t[y], ref.padded1[a + y])
        value = value.T
        rows = 3 * c_in // 16
        for lane in range(channels // 128):
            piece = value[:, lane * 128 : (lane + 1) * 128].astype(BF16).reshape(rows, 16, 128)
            ref.part_c[pl.ds(lane * rows_c + a * rows, rows)] = piece
        return carry

    lax.fori_loop(0, 3, kernel1_grad, 0)
    value = mm(ref.gpre_t[...], ref.image_box[...].reshape(low * half, c_in)).T
    for lane in range(channels // 128):
        piece = value[:, lane * 128 : (lane + 1) * 128].astype(BF16).reshape(c_in // 16, 16, 128)
        ref.part_c[pl.ds(lane * rows_c + 9 * c_in // 16, c_in // 16)] = piece
    next_c = link.all_sum(ref.part_c, ref.recv1_c, ref.sum1_c, ref.recv2_c, ref.recv3_c, ref.sum_c)

    def conv2_rows(i, carry):
        branch_sum, stream_sum = carry
        pooled = 0.0
        for u in range(2):
            y = 2 * i + u
            branch = mm(ref.padded2[y], ref.kernel2[0])
            branch = branch + mm(ref.padded2[y + 1], ref.kernel2[1])
            branch = branch + mm(ref.padded2[y + 2], ref.kernel2[2])
            branch = branch + ref.bias2[...]
            stream = (branch + mm(ref.image_low[y], ref.skip_w[...]) + ref.skip_b[...]) * math.sqrt(0.5)
            mask = wide_mask(y)
            branch_sum = branch_sum + fold(branch * branch * mask)
            stream_sum = stream_sum + fold(stream * stream * mask)
            pooled = pooled + stream[0:half] + stream[half:span]
        ref.pooled[i] = (pooled * 0.25).astype(BF16)
        return branch_sum, stream_sum

    branch_sum, stream_sum = lax.fori_loop(0, low, conv2_rows, (zero2, zero2))

    wait_hidden_rows()
    wait_hidden_columns()
    pad_rows(ref.padded2, ref.grad_hidden, ref.hidden_up, ref.hidden_down, ref.columns4)

    def back1_row(y, carry):
        grad_sum, grad_dot = carry
        value = mm_t(ref.padded2[y], ref.kernel1_t[0])
        value = value + mm_t(ref.padded2[y + 1], ref.kernel1_t[1])
        value = value + mm_t(ref.padded2[y + 2], ref.kernel1_t[2])
        value = value * ref.slope1[y]
        ref.slope1[y] = value
        return grad_sum + fold(value), grad_dot + fold(value * ref.normed1[y + 1])

    grad_sum1, grad_dot1 = lax.fori_loop(0, height, back1_row, (zero1, zero1))
    ref.stats4[slot] = jnp.zeros((8, channels), F32)
    ref.stats4[slot, 0:1, 0:c_in] = total(grad_sum1)
    ref.stats4[slot, 0:1, c_in:channels] = total(grad_dot1)
    wait_stats4 = link.share(ref.stats4)
    next_a = next_a()
    next_c = next_c()

    for step in range(1, n_row):
        other = lax.rem(link.row + step, n_row) * 2 + link.pair
        link.arrived(ref.raw.at[other], feature_sem + other)
        link.send(ref.raw.at[other], ref.raw.at[other], (link.item, link.row, link.sibling), feature_sem + other)
    wait_token()

    next_a = next_a()
    next_c = next_c()

    wait_stats4()
    stats = ref.stats4[0]
    for other in range(1, n_group):
        stats = stats + ref.stats4[other]
    grad_sum1, grad_dot1 = stats[0:1, 0:c_in], stats[0:1, c_in:channels]
    grouped = group_total(jnp.concatenate([grad_sum1 * gain1, grad_dot1 * gain1], axis=0), width1)
    first1, second1 = grouped[0:1] / size1, grouped[1:2] / size1

    def image_grad_rows(i, carry):
        skip = mm_t(ref.gpre[i], ref.skip_w[...])
        skip = jnp.concatenate([skip, skip], axis=0)
        for u in range(2):
            y = 2 * i + u
            value = ref.slope1[y] * gain1 - ref.mask[y] * (first1 + ref.normed1[y + 1] * second1)
            value = value * inv1 + skip
            ref.line[pl.ds(0, half, stride=2), :] = value[0:half]
            ref.line[pl.ds(1, half, stride=2), :] = value[half:span]
            ref.image_grad[y] = ref.line[...].astype(BF16)
        return carry

    lax.fori_loop(0, low, image_grad_rows, 0)
    next_a = next_a()
    next_c = next_c()

    for step in range(n_row):
        other = lax.rem(link.row + step, n_row) * 2 + link.sibling
        link.arrived(ref.raw.at[other], feature_sem + other)

    def score_block(index, carry):
        normalize(index)
        mask = token_mask(ref.flags[index])
        mask = jnp.concatenate([mask] * (tokens // 128), axis=1) if tokens > 128 else mask[:, 0:tokens]
        scores = mm(ref.tokens[index], ref.query_t[...])
        scores = jnp.where(mask > 0.5, scores, MASKED * LOG2E)
        ref.scores[index] = scores
        return jnp.maximum(carry, jnp.max(scores.reshape(tokens // 8, 8, tokens), axis=0))

    top = lax.fori_loop(0, n_group, score_block, jnp.full((8, tokens), -3e38, F32))
    top = jnp.max(top, axis=0, keepdims=True)
    ref.mixed_t[...] = jnp.zeros((channels, tokens), F32)

    def probs_block(index, carry):
        probs = jnp.exp2(ref.scores[index] - top)
        low_probs = probs.astype(BF16)
        ref.probs[index] = low_probs
        ref.mixed_t[...] += mm(ref.tokens_t[index], low_probs)
        return carry + fold(probs)

    norm = lax.fori_loop(0, n_group, probs_block, jnp.zeros((8, tokens), F32))
    norm = 1.0 / total(norm)
    next_a = next_a()
    next_c = next_c()
    mixed_t = ref.mixed_t[...] * norm
    ref.mixed_t[...] = mixed_t
    attended = (mm(mixed_t.T.astype(BF16), w_value) + ref.mix_b[:, channels:]).astype(BF16)
    update = mm(attended, ref.out_w[...]) + ref.out_b[...]
    result = ref.features[...].astype(F32) + update
    ref.result[...] = result.astype(BF16)
    tmask2 = jnp.concatenate([ref.token_mask[...]] * (channels // 128), axis=1)
    update_sum = fold(update * update * tmask2)
    result_sum = fold(result * result * tmask2)

    def part_b(lane, value):
        for tile in range(channels // 128):
            piece = value[:, tile * 128 : (tile + 1) * 128].astype(BF16)
            ref.part_b[pl.ds((lane + tile) * (channels // 16), channels // 16)] = piece.reshape(channels // 16, 16, 128)

    part_b(6, mm(attended.T, ref.gres[...]))
    part_b(4, mm(mixed_t.astype(BF16), ref.grad_att[...]))

    grad_t = (ref.grad_t[...] * norm).astype(BF16)
    delta = total(grad_t.astype(F32) * mixed_t)
    ref.grad_low_t[...] = grad_t
    ref.grad_low[...] = grad_t.T
    ref.grad_query_t[...] = jnp.zeros((channels, tokens), F32)

    def back_block(index, carry):
        grad_sum, grad_dot = carry
        probs = ref.probs[index]
        grad = mm(ref.tokens[index], ref.grad_low_t[...])
        grad = (probs.astype(F32) * (grad - delta)).astype(BF16)
        value = mm(grad, ref.query_k[...]) + mm(probs, ref.grad_low[...])
        ref.grad_tokens[index] = value.astype(BF16)
        ref.grad_query_t[...] += mm(ref.tokens_t[index], grad)
        return grad_sum + fold(value), grad_dot + fold(value * ref.raw[index].astype(F32))

    grad_sum3, grad_dot3 = zero2, zero2
    pair_sem = link.new_recv(n_row)
    order = [lax.rem(link.row + step, n_row) for step in range(1, n_row)] + [link.row]
    for step, other in enumerate(order):
        grad_sum3, grad_dot3 = back_block(other * 2 + link.sibling, (grad_sum3, grad_dot3))
        link.send(
            ref.grad_tokens.at[other * 2 + link.sibling], ref.pair_grad.at[step],
            (link.item, link.row, link.sibling), pair_sem + step,
        )
        grad_sum3, grad_dot3 = back_block(other * 2 + link.pair, (grad_sum3, grad_dot3))
    row_sem = link.new_recv(n_row)
    for step, other in enumerate(order[:-1]):
        link.arrived(ref.pair_grad.at[step], pair_sem + step)
        value = ref.pair_grad[step].astype(F32) + ref.grad_tokens[other * 2 + link.pair].astype(F32)
        ref.chip_grad[step] = value.astype(BF16)
        link.send(ref.chip_grad.at[step], ref.row_grad.at[step], (link.item, other, link.pair), row_sem + step)

    grad_query_t = (ref.grad_query_t[...] * alive[0:1, 0:1]).astype(BF16)
    grad_query = mm(grad_query_t.T, w_key).astype(BF16)
    part_b(0, mm(ref.tokens_t[slot], grad_query))
    part_b(2, mm(grad_query_t, ref.query[...]))
    next_b = link.all_sum(ref.part_b, ref.recv1_b, ref.sum1_b, ref.recv2_b, ref.recv3_b, ref.sum_b)
    own_grad = mm_t(grad_query, w_query)
    raw = ref.features[...].astype(F32)
    grad_sum3 = total(grad_sum3 + fold(own_grad))
    grad_dot3 = total(grad_dot3 + fold(own_grad * raw))
    ref.stats5[slot] = jnp.zeros((16, channels), F32)
    for index, value in enumerate((
        grad_sum3,
        (grad_dot3 - mean3 * grad_sum3) * inv3,
        total(bias1_sum),
        4.0 * total(gpre_sum),
        total(fold(ref.gres[...].astype(F32))),
        total(fold(grad_query.astype(F32))),
        total(fold(ref.grad_att[...].astype(F32))),
        total(branch_sum),
        total(stream_sum),
        total(update_sum),
        total(result_sum),
    )):
        ref.stats5[slot, index : index + 1, :] = value
    wait_stats5 = link.share(ref.stats5)
    next_a = next_a()
    next_c = next_c()
    next_b = next_b()

    last = n_row - 1
    link.arrived(ref.pair_grad.at[last], pair_sem + last)
    own_grad = own_grad + ref.pair_grad[last].astype(F32) + ref.grad_tokens[slot].astype(F32)
    wait_stats5()
    stats = ref.stats5[0]
    for other in range(1, n_group):
        stats = stats + ref.stats5[other]
    item = link.item
    ref.vectors[item, 0:16, :] = stats
    ref.vectors[item, 16:24, :] = jnp.zeros((8, channels), F32)
    ref.vectors[item, 11:12, 0:c_in] = grad_dot1
    ref.vectors[item, 11:12, c_in:channels] = grad_sum1
    ref.vectors[item, 12:13, :] = grad_dot2 * film_scale
    ref.vectors[item, 13:14, :] = grad_sum2 * film_scale
    ref.vectors[item, 14:15, :] = grad_dot2 * ref.gain2[...] + grad_sum2 * ref.shift2[...]
    ref.vectors[item, 15:16, :] = grad_sum2
    ref.vectors[item, 16:17, :] = ref.embedding[:, 0:channels].astype(F32)
    ref.vectors[item, 17:18, :] = ref.embedding[:, channels : 2 * channels].astype(F32)
    stats1 = ref.stats1[0]
    for other in range(1, n_group):
        stats1 = stats1 + ref.stats1[other]
    ref.vectors[item, 18:19, 0:c_in] = stats1[0:1, c_in:channels]
    ref.vectors[item, 19:20, :] = stats1[3:4]
    item_sem = link.new_recv(n_item)
    for step in range(1, n_item):
        other = lax.rem(item + step, n_item)
        link.send(ref.vectors.at[item], ref.vectors.at[item], (other, link.row, link.pair), item_sem + item)

    grouped = group_total(jnp.concatenate([stats[0:1] * gain3, stats[1:2] * gain3], axis=0), width2)
    first3, second3 = grouped[0:1] / size3, grouped[1:2] / size3
    for step in range(n_row - 1):
        link.arrived(ref.row_grad.at[step], row_sem + step)
        own_grad = own_grad + ref.row_grad[step].astype(F32)
    normed = (raw - mean3) * inv3
    value = (own_grad * gain3 - tmask2 * (first3 + normed * second3)) * inv3
    ref.features_grad[...] = (ref.gres[...].astype(F32) + value).astype(BF16)
    next_a = next_a()
    next_c = next_c()
    for _ in range(5):
        next_b = next_b()
    for step in range(1, n_item):
        other = lax.rem(item + step, n_item)
        link.arrived(ref.vectors.at[other], item_sem + other)
    link.finish()
    assert link.sends <= ref.send_sem.shape[0] and link.recvs <= ref.recv_sem.shape[0]


SCRATCH = (
    "send_sem", "recv_sem", "flags", "raw", "image_up", "image_down", "pool_up", "pool_down", "mask",
    "token_mask", "line", "normed1", "image_low", "column1", "columns1", "stats1", "gpre", "gpre_t",
    "column2", "columns2", "coarse", "padded_g", "grad2", "slope1", "padded1", "hidden", "stats2",
    "tokens", "tokens_t", "query", "query_t", "query_k", "grad_att", "grad_t", "act2", "column3",
    "columns3", "stats3", "act_up", "act_down", "kernel1_t", "grad_hidden", "grad_hidden_t", "column4",
    "columns4", "hidden_up", "hidden_down", "padded2", "boxes", "image_box", "part_a", "recv1_a",
    "sum1_a", "recv2_a", "recv3_a", "part_b", "recv1_b", "sum1_b", "recv2_b", "recv3_b", "part_c",
    "recv1_c", "sum1_c", "recv2_c", "recv3_c", "stats4", "scores", "probs", "mixed_t",
    "grad_low_t", "grad_low", "grad_query_t", "grad_tokens", "pair_grad", "chip_grad", "row_grad", "stats5",
)


def last_kernel(n_item, *refs):
    (pooled, result, image_grad, features_grad, sum_a, sum_b, sum_c, vectors) = refs[:8]
    (o_pooled, o_result, o_image, o_features, o_gain1, o_shift1, o_kernel1, o_bias1, o_film_w, o_film_b,
     o_gain2, o_shift2, o_kernel2, o_bias2, o_skip_w, o_skip_b, o_gain3, o_shift3, o_mix_w, o_mix_b,
     o_out_w, o_out_b, o_rms) = refs[8:]
    o_pooled[...] = pooled[...]
    o_result[...] = result[...]
    o_image[...] = image_grad[...]
    o_features[...] = features_grad[...]
    channels = o_bias1.shape[-1]
    c_in = o_gain1.shape[-1]

    def blocks(ref, start, count):
        return ref[start : start + count].reshape(count * 16, 128).astype(F32)

    lanes = channels // 128
    n_a, n_c, n_k = 9 * channels // 16, 10 * c_in // 16, 9 * c_in // 16
    for lane in range(lanes):
        at = slice(lane * 128, (lane + 1) * 128)
        o_kernel2[:, at] = blocks(sum_a, lane * n_a, n_a)
        o_kernel1[:, at] = blocks(sum_c, lane * n_c, n_k)
        o_skip_w[:, at] = blocks(sum_c, lane * n_c + n_k, n_c - n_k)
    n_b = channels // 16
    for lane in range(3 * lanes):
        o_mix_w[:, lane * 128 : (lane + 1) * 128] = blocks(sum_b, lane * n_b, n_b)
    for lane in range(lanes):
        o_out_w[:, lane * 128 : (lane + 1) * 128] = blocks(sum_b, (3 * lanes + lane) * n_b, n_b)
    value = vectors[0]
    for item in range(1, n_item):
        value = value + vectors[item]
    o_shift3[...] = value[0:1]
    o_gain3[...] = value[1:2]
    o_bias1[...] = value[2:3]
    o_bias2[...] = value[3:4]
    o_skip_b[...] = value[3:4]
    o_out_b[...] = value[4:5]
    o_mix_b[:, 0:channels] = value[5:6]
    o_mix_b[:, channels:] = value[6:7]
    o_gain1[...] = value[11:12, 0:c_in]
    o_shift1[...] = value[11:12, c_in:channels]
    o_gain2[...] = value[12:13]
    o_shift2[...] = value[13:14]
    o_film_b[:, 0:channels] = value[14:15]
    o_film_b[:, channels:] = value[15:16]
    pad = jnp.zeros((8 - n_item, 2 * channels), F32)
    embedding = jnp.concatenate(
        [jnp.concatenate([vectors[i, 16:17, :], vectors[i, 17:18, :]], axis=1) for i in range(n_item)] + [pad], axis=0
    )
    grads = jnp.concatenate(
        [jnp.concatenate([vectors[i, 14:15, :], vectors[i, 15:16, :]], axis=1) for i in range(n_item)] + [pad], axis=0
    )
    o_film_w[...] = lax.dot_general(
        embedding, grads, (((0,), (0,)), ((), ())), precision=HIGHEST, preferred_element_type=F32
    )

    def lane_sum(row):
        return jnp.sum(row, axis=1, keepdims=True)

    land = jnp.maximum(value[19:20, 0:1], 1.0)
    token = jnp.maximum(value[19:20, 128:129], 1.0)
    place = iota((1, 5), 1)
    rms = jnp.zeros((1, 5), F32)
    for index, (square, count) in enumerate((
        (lane_sum(value[18:19, 0:c_in]), land * c_in),
        (lane_sum(value[7:8]), land * channels),
        (lane_sum(value[8:9]), land * channels),
        (lane_sum(value[9:10]), token * channels),
        (lane_sum(value[10:11]), token * channels),
    )):
        rms = jnp.where(place == index, jnp.sqrt(square / count), rms)
    o_rms[...] = rms


def on_device(mesh_shape, *args):
    names = INPUTS
    arg = SimpleNamespace(**dict(zip(names, args)))
    n_item, n_row = mesh_shape["item"], mesh_shape["row"]
    n_group = 2 * n_row
    _, height, span, c_in = arg.image.shape
    channels = arg.bias1.shape[-1]
    _, rows_t, cols_t, _ = arg.features.shape
    tokens = rows_t * cols_t
    low, half = height // 2, span // 2
    inputs = [
        arg.image.reshape(height, span, c_in),
        arg.land_mask.reshape(height, span) if hasattr(arg, "land_mask") else arg.land.reshape(height, span),
        arg.embedding,
        arg.gain1.reshape(1, c_in),
        arg.shift1.reshape(1, c_in),
        arg.kernel1.reshape(3, 3 * c_in, channels),
        arg.bias1.reshape(1, channels),
        arg.film_w,
        arg.film_b.reshape(1, 2 * channels),
        arg.gain2.reshape(1, channels),
        arg.shift2.reshape(1, channels),
        arg.kernel2.reshape(3, 3 * channels, channels),
        arg.bias2.reshape(1, channels),
        arg.skip_w,
        arg.skip_b.reshape(1, channels),
        arg.features.reshape(tokens, channels),
        arg.token.reshape(rows_t, cols_t),
        arg.gain3.reshape(1, channels),
        arg.shift3.reshape(1, channels),
        arg.mix_w,
        arg.mix_b.reshape(1, 2 * channels),
        arg.out_w,
        arg.out_b.reshape(1, channels),
        arg.gpool.reshape(low, half, channels),
        arg.gres.reshape(tokens, channels),
    ]
    share = 2 * n_item * n_row
    blocks_a = -(-9 * channels * channels // 2048 // share) * share
    blocks_b = -(-4 * channels * channels // 2048 // share) * share
    blocks_c = -(-10 * c_in * channels // 2048 // share) * share
    vmem = pltpu.VMEM

    def sums(blocks):
        unit = blocks // 2 // n_item
        return [
            vmem((blocks, 16, 128), BF16),
            vmem((blocks // 2, 16, 128), BF16),
            vmem((blocks // 2, 16, 128), BF16),
            vmem((n_item - 1, unit, 16, 128), BF16),
            vmem((n_row - 1, unit // n_row, 16, 128), BF16),
        ]

    scratch = [
        pltpu.SemaphoreType.DMA((100 + 12 * n_group,)),
        pltpu.SemaphoreType.DMA((100 + 12 * n_group,)),
        vmem((n_group, rows_t, cols_t), jnp.int32),
        vmem((n_group, tokens, channels), BF16),
        vmem((span, c_in), BF16),
        vmem((span, c_in), BF16),
        vmem((half, channels), BF16),
        vmem((half, channels), BF16),
        vmem((height, span, 128), F32),
        vmem((tokens, 128), F32),
        vmem((span, c_in), F32),
        vmem((height + 2, span, c_in), F32),
        vmem((height, span, c_in), BF16),
        vmem((8, c_in), F32),
        vmem((3, 8, c_in), F32),
        vmem((n_group, 8, channels), F32),
        vmem((low, half, channels), BF16),
        vmem((channels, low * half), BF16),
        vmem((8, channels), F32),
        vmem((3, 8, channels), F32),
        vmem((8, channels, 2 * channels) if n_group < 8 or tokens < 2 * channels else (8, 16, 128), BF16),
        vmem((low + 2, half, 3 * channels), BF16),
        vmem((height, span, channels), F32),
        vmem((height, span, c_in), F32),
        vmem((height + 2, span, 3 * c_in), BF16),
        vmem((height, span, channels), F32),
        vmem((n_group, 8, channels), F32),
        vmem((n_group, tokens, channels), BF16),
        vmem((n_group, channels, tokens), BF16),
        vmem((tokens, channels), BF16),
        vmem((channels, tokens), BF16),
        vmem((tokens, channels), BF16),
        vmem((tokens, channels), BF16),
        vmem((channels, tokens), F32),
        vmem((height, span, channels), BF16),
        vmem((8, channels), F32),
        vmem((3, 8, channels), F32),
        vmem((n_group, 8, channels), F32),
        vmem((span, channels), BF16),
        vmem((span, channels), BF16),
        vmem((3, c_in, 3 * channels), BF16),
        vmem((height, span, channels), BF16),
        vmem((height, channels, span), BF16),
        vmem((8, channels), F32),
        vmem((3, 8, channels), F32),
        vmem((span, channels), BF16),
        vmem((span, channels), BF16),
        vmem((height + 2, span, 3 * channels), BF16),
        vmem((3, low, half, 3 * channels), BF16),
        vmem((low, half, c_in), BF16),
        *sums(blocks_a),
        *sums(blocks_b),
        *sums(blocks_c),
        vmem((n_group, 8, channels), F32),
        vmem((n_group, tokens, tokens), F32),
        vmem((n_group, tokens, tokens), BF16),
        vmem((channels, tokens), F32),
        vmem((channels, tokens), BF16),
        vmem((tokens, channels), BF16),
        vmem((channels, tokens), F32),
        vmem((n_group, tokens, channels), BF16),
        vmem((n_row, tokens, channels), BF16),
        vmem((n_row - 1, tokens, channels), BF16),
        vmem((n_row - 1, tokens, channels), BF16),
        vmem((n_group, 16, channels), F32),
    ]
    shape = jax.ShapeDtypeStruct
    mid = [
        shape((low, half, channels), BF16),
        shape((tokens, channels), BF16),
        shape((height, span, c_in), BF16),
        shape((tokens, channels), BF16),
        shape((blocks_a, 16, 128), BF16),
        shape((blocks_b, 16, 128), BF16),
        shape((blocks_c, 16, 128), BF16),
        shape((n_item, 24, channels), F32),
    ]
    in_vmem = pl.BlockSpec(memory_space=vmem)
    parts = pl.pallas_call(
        functools.partial(main_kernel, n_item, n_row),
        out_shape=mid,
        in_specs=[in_vmem] * len(inputs),
        out_specs=[in_vmem] * len(mid),
        scratch_shapes=scratch,
        compiler_params=pltpu.CompilerParams(
            collective_id=0, has_side_effects=True, vmem_limit_bytes=int(63.9 * 1024 * 1024)
        ),
    )(*inputs)
    emb = arg.embedding.shape[-1]
    final = [
        *mid[:4],
        shape((1, c_in), F32),
        shape((1, c_in), F32),
        shape((9 * c_in, channels), F32),
        shape((1, channels), F32),
        shape((emb, 2 * channels), F32),
        shape((1, 2 * channels), F32),
        shape((1, channels), F32),
        shape((1, channels), F32),
        shape((9 * channels, channels), F32),
        shape((1, channels), F32),
        shape((c_in, channels), F32),
        shape((1, channels), F32),
        shape((1, channels), F32),
        shape((1, channels), F32),
        shape((channels, 3 * channels), F32),
        shape((1, 2 * channels), F32),
        shape((channels, channels), F32),
        shape((1, channels), F32),
        shape((1, 5), F32),
    ]
    outs = pl.pallas_call(
        functools.partial(last_kernel, n_item),
        out_shape=final,
        in_specs=[in_vmem] * len(mid),
        out_specs=[in_vmem] * len(final),
        compiler_params=pltpu.CompilerParams(vmem_limit_bytes=48 * 1024 * 1024),
    )(*parts)
    shapes = (
        (1, low, half, channels),
        (1, rows_t, cols_t, channels),
        (1, height, span, c_in),
        (1, rows_t, cols_t, channels),
        (c_in,),
        (c_in,),
        (3, 3, c_in, channels),
        (channels,),
        (emb, 2 * channels),
        (2 * channels,),
        (channels,),
        (channels,),
        (3, 3, channels, channels),
        (channels,),
        (c_in, channels),
        (channels,),
        (channels,),
        (channels,),
        (channels, 3 * channels),
        (2 * channels,),
        (channels, channels),
        (channels,),
        (5,),
    )
    return tuple(out.reshape(to) for out, to in zip(outs, shapes))


def solution(mesh):
    tiled = P("item", "row", "pair", None)
    mask = P("item", "row", "pair")
    in_specs = [P()] * len(INPUTS)
    for name in ("image", "features", "gpool", "gres"):
        in_specs[INPUTS.index(name)] = tiled
    for name in ("land", "token"):
        in_specs[INPUTS.index(name)] = mask
    in_specs[INPUTS.index("embedding")] = P("item", None)
    return jax.shard_map(
        functools.partial(on_device, dict(mesh.shape)),
        mesh=mesh,
        in_specs=tuple(in_specs),
        out_specs=(tiled,) * 4 + (P(),) * 19,
        check_vma=False,
    )
```

profile of v0, /device:TPU:0, one launch (start us, length us, event | category | flops | bytes accessed | tf_op | source)
XLA Modules:
  0.0 153.7 jit_solution(1790286817593261592)
XLA Ops:
  0.7 140.9 %shard_map.416 = (bf16[4,128,256]{2,1,0:T(8,128)(2,1)}, bf16[512,256]{1,0:T(8,128)(2,1)}, bf16[8,256,128]{2,1,0:T(8,128)(2,1)}, bf16[512,256]{1,0:T(8,128)(2,1)}...) custom-call(bf16[8,256,128]{2,1,0:T(8,128)(2,1)} %bitcast.41, ...), custom_call_target="tpu_custom_call" | custom-call | tf_op jit(solution)/shard_map/pallas_call | solution.py:1113
  141.6 0.0 copy-start
  141.6 1.3 copy-done
  142.8 0.0 copy-start.1
  142.8 1.1 copy-done.1
  143.9 0.0 copy-start.2
  143.9 1.0 copy-done.2
  145.0 0.0 copy-start.3
  145.0 1.0 copy-done.3
  146.0 0.0 copy-start.4
  146.0 0.9 copy-done.4
  147.0 0.0 copy-start.5
  147.0 0.9 copy-done.5
  147.9 0.0 copy-start.6
  147.9 0.9 copy-done.6
  148.9 0.0 copy-start.7
  148.9 0.9 copy-done.7
  149.8 3.9 %shard_map.417 = (bf16[4,128,256]{2,1,0:T(8,128)(2,1)}, bf16[512,256]{1,0:T(8,128)(2,1)}, bf16[8,256,128]{2,1,0:T(8,128)(2,1)}, bf16[512,256]{1,0:T(8,128)(2,1)}...) custom-call(bf16[4,128,256]{2,1,0:T(8,128)(2,1)S(1)} %copy-done.4, ...), custom_call_target="tpu_custom_call" | custom-call | tf_op jit(solution)/shard_map/pallas_call | solution.py:1146
Async XLA Ops:
  141.6 1.3 copy-start
  142.8 1.1 copy-start.1
  143.9 1.0 copy-start.2
  145.0 1.0 copy-start.3
  146.0 0.9 copy-start.4
  147.0 0.9 copy-start.5
  147.9 0.9 copy-start.6
  148.9 0.9 copy-start.7
where the time goes:
time: 154 us
  Pallas kernels  145 us (94%)
  local copies, waits for them, and re-layouts  8.17 us (5%)
    pallas_call x1, Pallas kernels, on_device(): pl.pallas_call(functools.partial(main_kernel, n_item, n_row), out_shape=m...  141 us
    unnamed x16, local copies, waits for them, and re-layouts  8.17 us
    pallas_call x1, Pallas kernels, on_device(): pl.pallas_call(functools.partial(last_kernel, n_item), out_shape=final, i...  3.92 us

commit v1 on v0

v1 whole, which is shorter than its diff:
```python
import functools
import math
from types import SimpleNamespace

import jax
import jax.numpy as jnp
from jax import lax
from jax.experimental import pallas as pl
from jax.experimental.pallas import tpu as pltpu
from jax.sharding import PartitionSpec as P

GROUPS = 32
EPS = 1e-05
MASKED = -1000000000.0
LOG2E = 1.4426950408889634
F32 = jnp.float32
BF16 = jnp.bfloat16
MESH = pl.DeviceIdType.MESH
HIGHEST = lax.Precision.HIGHEST


def mm(left, right):
    return jnp.dot(left, right, preferred_element_type=F32)


def mm_t(left, right):
    return lax.dot_general(left, right, (((1,), (1,)), ((), ())), preferred_element_type=F32)


def iota(shape, dim):
    return lax.broadcasted_iota(jnp.int32, shape, dim)


def fold(value):
    rows, width = value.shape
    return jnp.sum(value.reshape(rows // 8, 8, width), axis=0)


def total(value):
    return jnp.sum(value, axis=0, keepdims=True)


def group_total(rows, width):
    channels = rows.shape[-1]
    left = jnp.floor(iota((channels, channels), 0).astype(F32) * (1.0 / width))
    right = jnp.floor(iota((channels, channels), 1).astype(F32) * (1.0 / width))
    same = (left == right).astype(F32)
    padded = jnp.concatenate([rows, jnp.zeros((8 - rows.shape[0], channels), F32)], axis=0)
    return jnp.dot(padded, same, precision=HIGHEST, preferred_element_type=F32)


def sigmoid(value):
    return 0.5 * jnp.tanh(0.5 * value) + 0.5


INPUTS = (
    "image", "land", "embedding", "gain1", "shift1", "kernel1", "bias1", "film_w", "film_b",
    "gain2", "shift2", "kernel2", "bias2", "skip_w", "skip_b", "features", "token", "gain3",
    "shift3", "mix_w", "mix_b", "out_w", "out_b", "gpool", "gres",
)
RESULTS = ("pooled", "result", "image_grad", "features_grad", "sum_a", "sum_b", "sum_c", "vectors")


class Links:
    def __init__(self, ref, n_item, n_row):
        self.ref = ref
        self.n_item, self.n_row, self.n_group = n_item, n_row, n_row * 2
        self.item, self.row, self.pair = (lax.axis_index(a) for a in ("item", "row", "pair"))
        self.sibling = 1 - self.pair
        self.slot = self.row * 2 + self.pair
        self.sends = 0
        self.recvs = 0
        self.pending = []

    def at(self, row=None, pair=None, item=None):
        return (
            self.item if item is None else item,
            self.row if row is None else row,
            self.pair if pair is None else pair,
        )

    def others_in_group(self):
        for step in range(1, self.n_group):
            other = lax.rem(self.slot + step, self.n_group)
            yield other, self.at(lax.div(other, 2), lax.rem(other, 2))

    def others_in_row(self):
        for step in range(1, self.n_row):
            other = lax.rem(self.row + step, self.n_row)
            yield other, self.at(row=other)

    def others_in_item(self):
        for step in range(1, self.n_item):
            other = lax.rem(self.item + step, self.n_item)
            yield other, self.at(item=other)

    def new_recv(self, count=1):
        self.recvs += count
        return self.recvs - count

    def copy(self, source, target, device, send, recv):
        return pltpu.make_async_remote_copy(
            src_ref=source,
            dst_ref=target,
            send_sem=self.ref.send_sem.at[send],
            recv_sem=self.ref.recv_sem.at[recv],
            device_id=device,
            device_id_type=MESH,
        )

    def send(self, source, target, device, recv, when=None):
        index = self.sends
        self.sends += 1

        def make():
            return self.copy(source, target, device, index, recv)

        if when is None:
            make().start()
        else:
            pl.when(when)(lambda: make().start())
        self.pending.append((make, when))

    def send_all(self, copies, size):
        index, recv = self.sends, self.new_recv()
        self.sends += 1
        for source, target, device in copies:
            self.copy(source, target, device, index, recv).start()
        whole = self.copy(size, size, self.at(pair=self.sibling), index, recv)
        self.pending.append((lambda: whole, None))
        return whole.wait_recv

    def arrived(self, target, recv, when=None):
        def wait():
            self.copy(target, target, self.at(pair=self.sibling), 0, recv).wait_recv()

        if when is None:
            wait()
        else:
            pl.when(when)(wait)

    def finish(self):
        for make, when in self.pending:
            if when is None:
                make().wait_send()
            else:
                pl.when(when)(lambda make=make: make().wait_send())

    def greet(self):
        barrier = pltpu.get_barrier_semaphore()
        devices = [d for _, d in self.others_in_group()] + [d for _, d in self.others_in_item()]
        for device in devices:
            pl.semaphore_signal(barrier, inc=1, device_id=device, device_id_type=MESH)
        return lambda: pl.semaphore_wait(barrier, len(devices))

    def share(self, slots):
        mine = slots.at[self.slot]
        copies = [(mine, mine, device) for _, device in self.others_in_group()]
        return self.send_all(copies, slots.at[pl.ds(0, self.n_group - 1)])

    def edge_rows(self, first, last, above, below):
        has_above, has_below = self.row > 0, self.row < self.n_row - 1
        from_above, from_below = self.new_recv(), self.new_recv()
        self.send(first, below, self.at(row=self.row - 1), from_below, has_above)
        self.send(last, above, self.at(row=self.row + 1), from_above, has_below)

        def wait():
            self.arrived(above, from_above, has_above)
            self.arrived(below, from_below, has_below)

            @pl.when(self.row == 0)
            def _():
                above[...] = jnp.zeros(above.shape, above.dtype)

            @pl.when(self.row == self.n_row - 1)
            def _():
                below[...] = jnp.zeros(below.shape, below.dtype)

        return wait

    def edge_columns(self, column, columns):
        has_above, has_below = self.row > 0, self.row < self.n_row - 1
        base = self.new_recv(3)
        self.send(column, columns.at[2], self.at(self.row - 1, self.sibling), base + 2, has_above)
        self.send(column, columns.at[0], self.at(self.row + 1, self.sibling), base, has_below)
        self.send(column, columns.at[1], self.at(pair=self.sibling), base + 1)

        def wait():
            self.arrived(columns.at[1], base + 1)
            self.arrived(columns.at[0], base, has_above)
            self.arrived(columns.at[2], base + 2, has_below)

            @pl.when(self.row == 0)
            def _():
                columns[0] = jnp.zeros(columns.shape[1:], columns.dtype)

            @pl.when(self.row == self.n_row - 1)
            def _():
                columns[2] = jnp.zeros(columns.shape[1:], columns.dtype)

        return wait

    def all_sum(self, part, recv1, recv2, recv3, out):
        half = part.shape[0] // 2
        quarter = half // self.n_item
        chunk = quarter // self.n_row
        mine = self.pair * half
        item_at = mine + self.item * quarter
        own = item_at + self.row * chunk

        def span(ref, start, size):
            return ref.at[pl.ds(start, size)]

        def grow(start, size, arrivals):
            value = part[pl.ds(start, size)].astype(F32)
            for arrival in arrivals:
                value = value + arrival.astype(F32)
            return value.astype(BF16)

        def stage2():
            wait1()
            part[pl.ds(mine, half)] = grow(mine, half, [recv1[...]])
            copies = [
                (span(part, mine + other * quarter, quarter), recv2.at[step], device)
                for step, (other, device) in enumerate(self.others_in_item())
            ]
            wait2 = self.send_all(copies, recv2)

            def stage3():
                wait2()
                part[pl.ds(item_at, quarter)] = grow(item_at, quarter, [recv2[k] for k in range(self.n_item - 1)])
                copies = [
                    (span(part, item_at + other * chunk, chunk), recv3.at[step], device)
                    for step, (other, device) in enumerate(self.others_in_row())
                ]
                wait3 = self.send_all(copies, recv3)

                def stage4():
                    wait3()
                    out[pl.ds(own, chunk)] = grow(own, chunk, [recv3[k] for k in range(self.n_row - 1)])
                    source = span(out, own, chunk)
                    copies = [(source, source, device) for _, device in self.others_in_row()]
                    wait4 = self.send_all(copies, span(out, 0, (self.n_row - 1) * chunk))

                    def stage5():
                        wait4()
                        source = span(out, item_at, quarter)
                        copies = [(source, source, device) for _, device in self.others_in_item()]
                        wait5 = self.send_all(copies, span(out, 0, (self.n_item - 1) * quarter))

                        def stage6():
                            wait5()
                            source = span(out, mine, half)
                            return self.send_all([(source, source, self.at(pair=self.sibling))], span(out, 0, half))

                        return stage6

                    return stage5

                return stage4

            return stage3

        wait1 = self.send_all([(span(part, self.sibling * half, half), recv1, self.at(pair=self.sibling))], recv1)
        return stage2


def norm_terms(sums, squares, count, width):
    size = jnp.maximum(count, 1.0) * width
    grouped = group_total(jnp.concatenate([sums, squares], axis=0), width)
    mean = grouped[0:1] / size
    return mean, lax.rsqrt(grouped[1:2] / size - mean * mean + EPS), size


def chain_order(n_row):
    orders = []
    for row in range(n_row):
        steps = [(row + s, 0, n_row - 1 - s, s) for s in range(n_row - 1) if n_row - 1 - s > row]
        steps += [(n_row - 1 - row + s, 1, s, s) for s in range(n_row - 1) if s < row]
        steps.sort()
        orders.append([(target, 1 - down, down * (n_row - 1) + s) for _, down, target, s in steps])
    return orders


def arrival_order(n_row):
    orders = []
    for row in range(n_row):
        found = [row]
        for step in range(1, n_row):
            found += [r for r in (row - step, row + step) if 0 <= r < n_row]
        orders.append(found)
    return orders


def pick(values, index):
    chosen = jnp.int32(0)
    for k, value in enumerate(values):
        chosen = chosen + jnp.where(index == k, jnp.int32(value), jnp.int32(0))
    return chosen


def main_kernel(n_item, n_row, *refs):
    names = INPUTS + RESULTS + SCRATCH
    ref = SimpleNamespace(**dict(zip(names, refs)))
    link = Links(ref, n_item, n_row)
    height, span, c_in = ref.image.shape
    channels = ref.bias1.shape[-1]
    half = span // 2
    tokens = ref.features.shape[0]
    n_group = link.n_group
    low = height // 2
    side = link.pair.astype(F32)
    width1, width2 = c_in // GROUPS, channels // GROUPS
    slot, item, row, pair, sibling = link.slot, link.item, link.row, link.pair, link.sibling
    factor = channels ** (-0.5)
    zero1 = jnp.zeros((8, c_in), F32)
    zero2 = jnp.zeros((8, channels), F32)

    def lanes(mask, width):
        if width <= mask.shape[1]:
            return mask[:, 0:width]
        return jnp.concatenate([mask] * (width // mask.shape[1]), axis=1)

    def slot_sum(slots):
        value = slots[0]
        for other in range(1, n_group):
            value = value + slots[other]
        return value

    met = link.greet()

    ones = jnp.ones((span, 128), BF16)
    place = iota((span, span), 0)
    place = jnp.where(place < half, 2 * place, 2 * (place - half) + 1)
    spread = place == iota((span, span), 1)

    def land_row(y, carry):
        line = jnp.broadcast_to(ref.land[pl.ds(y, 1), :].astype(F32), (span, span))
        ref.mask[y] = mm(jnp.where(spread, line, 0.0).astype(BF16), ones)
        return carry

    lax.fori_loop(0, height, land_row, 0)

    rows_t, cols_t = ref.token.shape

    def token_mask(flags):
        chosen = iota((rows_t, cols_t, rows_t), 0) == iota((rows_t, cols_t, rows_t), 2)
        lines = mm(chosen.reshape(tokens, rows_t).astype(BF16), flags.astype(F32).astype(BF16))
        keep = (iota((rows_t, cols_t, cols_t), 1) == iota((rows_t, cols_t, cols_t), 2)).reshape(tokens, cols_t)
        return mm(jnp.where(keep, lines, 0.0).astype(BF16), jnp.ones((cols_t, 128), BF16))

    ref.token_mask[...] = token_mask(ref.token[...])

    def split_row(y, line):
        ref.line[...] = line.astype(F32)
        even = ref.line[pl.ds(0, half, stride=2), :]
        odd = ref.line[pl.ds(1, half, stride=2), :]
        ref.normed1[y, 0:half] = even
        ref.normed1[y, half:span] = odd
        return even, odd

    def image_row(y, carry):
        sums, squares, count = carry
        even, odd = split_row(y + 1, ref.image[y])
        value = jnp.concatenate([even, odd], axis=0)
        ref.image_low[y] = value.astype(BF16)
        ref.column1[pl.ds(y, 1), :] = jnp.where(side > 0.5, even[0:1], odd[half - 1 : half])
        mask = ref.mask[y]
        masked = value * mask
        return sums + fold(masked), squares + fold(masked * value), count + fold(mask)

    sums1, squares1, count1 = lax.fori_loop(0, height, image_row, (zero1, zero1, jnp.zeros((8, 128), F32)))
    raw = ref.features[...].astype(F32)
    tmask = ref.token_mask[...]
    tmask2 = lanes(tmask, channels)
    masked = raw * tmask2
    ref.stats1[slot] = jnp.zeros((8, channels), F32)
    ref.stats1[slot, 0:1, 0:c_in] = total(sums1)
    ref.stats1[slot, 0:1, c_in:channels] = total(squares1)
    ref.stats1[slot, 1:2, :] = total(masked)
    ref.stats1[slot, 2:3, :] = total(masked * raw)
    ref.stats1[slot, 3:4, 0:128] = total(count1)
    ref.stats1[slot, 3:4, 128:256] = total(tmask)

    gpre_sum = zero2
    for i in range(low):
        value = (ref.gpool[i].astype(F32) * 0.25 * math.sqrt(0.5)).astype(BF16)
        ref.gpre[i] = value
        ref.gpre_t[:, i * half : (i + 1) * half] = value.T
        wide = value.astype(F32)
        ref.column2[i : i + 1, :] = jnp.where(side > 0.5, wide[0:1], wide[half - 1 : half])
        gpre_sum = gpre_sum + fold(wide)
    ref.flags[slot] = ref.token[...]
    ref.raw[slot] = ref.features[...]

    met()
    wait_stats1 = link.share(ref.stats1)
    wait_image_columns = link.edge_columns(ref.column1, ref.columns1)
    wait_pool_columns = link.edge_columns(ref.column2, ref.columns2)
    wait_image_rows = link.edge_rows(ref.image.at[0], ref.image.at[height - 1], ref.image_up, ref.image_down)
    wait_pool_rows = link.edge_rows(ref.gpool.at[0], ref.gpool.at[low - 1], ref.pool_up, ref.pool_down)
    wait_token = link.share(ref.flags)
    raw_sem = link.new_recv(n_group)

    def raw_send(block, device, when=None):
        index = block * 2 + pair
        link.send(ref.raw.at[index], ref.raw.at[index], device, raw_sem + index, when)

    raw_send(row, link.at(row=row + 1), row < n_row - 1)
    raw_send(row, link.at(row=row - 1), row > 0)
    raw_send(row, link.at(pair=sibling))

    def raw_step(step):
        below, above = row - step, row + step
        link.arrived(ref.raw.at[below * 2 + pair], raw_sem + below * 2 + pair, below >= 0)
        link.arrived(ref.raw.at[above * 2 + pair], raw_sem + above * 2 + pair, above < n_row)
        if step < n_row - 1:
            raw_send(below, link.at(row=row + 1), (below >= 0) & (row < n_row - 1))
            raw_send(above, link.at(row=row - 1), (above < n_row) & (row > 0))
        raw_send(below, link.at(pair=sibling), below >= 0)
        raw_send(above, link.at(pair=sibling), above < n_row)

    coarse = ref.probs if n_group >= 8 and tokens >= 2 * channels else ref.coarse
    upper, lower = {0: (2,), 1: (1, 2)}, {0: (0, 1), 1: (0,)}
    for u in range(2):
        for line, row_taps in enumerate((upper[u], lower[u])):
            tall = []
            for b in range(3):
                tile = sum(ref.kernel2[a, b * channels : (b + 1) * channels, :].astype(F32) for a in row_taps)
                tall.append(tile)
            for v in range(2):
                for place_x, column_taps in enumerate((upper[v], lower[v])):
                    tile = sum(tall[b] for b in column_taps)
                    at = slice(place_x * channels, (place_x + 1) * channels)
                    coarse[u * 4 + v * 2 + line, 0:channels, at] = tile.astype(BF16)

    wait_pool_rows()
    wait_pool_columns()
    first_row = iota((half, channels), 0) == 0
    last_row = iota((half, channels), 0) == half - 1
    for i in range(low + 2):
        if i == 0:
            value, edge = ref.pool_up[...], ref.columns2[0, low - 1 : low, :]
        elif i == low + 1:
            value, edge = ref.pool_down[...], ref.columns2[2, 0:1, :]
        else:
            value, edge = ref.gpre[i - 1], ref.columns2[1, i - 1 : i, :]
        if i in (0, low + 1):
            value = (value.astype(F32) * 0.25 * math.sqrt(0.5)).astype(BF16)
        wide = value.astype(F32)
        left = jnp.where(first_row, edge * side, pltpu.roll(wide, 1, 0))
        right = jnp.where(last_row, edge * (1.0 - side), pltpu.roll(wide, half - 1, 0))
        ref.padded_g[i, :, 0:channels] = left.astype(BF16)
        ref.padded_g[i, :, channels : 2 * channels] = value
        ref.padded_g[i, :, 2 * channels : 3 * channels] = right.astype(BF16)
    for u in range(2):
        for v in range(2):
            value = 0.0
            for line in range(2):
                rows = ref.padded_g[u + line : u + line + low, :, v * channels : (v + 2) * channels]
                taps = coarse[u * 4 + v * 2 + line, 0:channels, 0 : 2 * channels]
                value = value + mm_t(rows.reshape(low * half, 2 * channels), taps)
            for i in range(low):
                ref.grad2[2 * i + u, v * half : (v + 1) * half, :] = value[i * half : (i + 1) * half]

    wait_image_rows()
    wait_image_columns()
    wait_stats1()
    stats1 = slot_sum(ref.stats1)
    count_land = lanes(stats1[3:4, 0:128], channels)
    count_token = lanes(stats1[3:4, 128:256], channels)
    mean1, inv1, size1 = norm_terms(stats1[0:1, 0:c_in], stats1[0:1, c_in:channels], count_land[:, 0:c_in], width1)
    mean3, inv3, size3 = norm_terms(stats1[1:2], stats1[2:3], count_token, width2)
    split_row(0, ref.image_up[...])
    split_row(height + 1, ref.image_down[...])
    gain1, shift1 = ref.gain1[...], ref.shift1[...]

    def write_shifted(target, y, even, odd, edge, size):
        top = iota((half, size), 0) == 0
        end = iota((half, size), 0) == half - 1
        before = jnp.where(top, edge * side, pltpu.roll(odd, 1, 0)).astype(BF16)
        after = jnp.where(end, edge * (1.0 - side), pltpu.roll(even, half - 1, 0)).astype(BF16)
        even, odd = even.astype(BF16), odd.astype(BF16)
        target[y, 0:half, 0:size] = before
        target[y, 0:half, size : 2 * size] = even
        target[y, 0:half, 2 * size : 3 * size] = odd
        target[y, half:span, 0:size] = even
        target[y, half:span, size : 2 * size] = odd
        target[y, half:span, 2 * size : 3 * size] = after

    def act1(value):
        normed = (value - mean1) * inv1
        affine = normed * gain1 + shift1
        gate = sigmoid(affine)
        return normed, affine, gate

    def edge_act(rows):
        _, affine, gate = act1(rows)
        return affine * gate

    has_up = (row > 0).astype(F32)
    has_down = (row < n_row - 1).astype(F32)
    ref.columns1[0] = edge_act(ref.columns1[0]) * has_up
    ref.columns1[1] = edge_act(ref.columns1[1])
    ref.columns1[2] = edge_act(ref.columns1[2]) * has_down

    def act1_edge_row(y, edge, exists):
        _, affine, gate = act1(ref.normed1[y])
        act = affine * gate * exists
        write_shifted(ref.padded1, y, act[0:half], act[half:span], edge, c_in)

    act1_edge_row(0, ref.columns1[0, height - 1 : height, :], has_up)
    act1_edge_row(height + 1, ref.columns1[2, 0:1, :], has_down)

    def act1_row(y, carry):
        normed, affine, gate = act1(ref.normed1[y + 1])
        act = affine * gate
        ref.normed1[y + 1] = normed
        ref.slope1[y] = gate * (1.0 + affine * (1.0 - gate))
        write_shifted(ref.padded1, y + 1, act[0:half], act[half:span], ref.columns1[1, pl.ds(y, 1), :], c_in)
        return carry

    lax.fori_loop(0, height, act1_row, 0)
    raw_step(1)

    def wide_mask(y):
        return lanes(ref.mask[y], channels)

    def conv1_row(y, carry):
        sums, squares = carry
        value = mm(ref.padded1[y], ref.kernel1[0])
        value = value + mm(ref.padded1[y + 1], ref.kernel1[1])
        value = value + mm(ref.padded1[y + 2], ref.kernel1[2])
        value = value + ref.bias1[...]
        ref.hidden[y] = value
        masked = value * wide_mask(y)
        return sums + fold(masked), squares + fold(masked * value)

    sums2, squares2 = lax.fori_loop(0, height, conv1_row, (zero2, zero2))
    ref.stats2[slot] = jnp.zeros((8, channels), F32)
    ref.stats2[slot, 0:1, :] = total(sums2)
    ref.stats2[slot, 1:2, :] = total(squares2)
    wait_stats2 = link.share(ref.stats2)

    scale3 = inv3 * ref.gain3[...]
    shift3 = ref.shift3[...]

    def normalize(index):
        value = ((ref.raw[index].astype(F32) - mean3) * scale3 + shift3).astype(BF16)
        ref.tokens[index] = value
        ref.tokens_t[index] = value.T

    normalize(slot)
    w_query = ref.mix_w[:, 0:channels]
    w_key = ref.mix_w[:, channels : 2 * channels]
    w_value = ref.mix_w[:, 2 * channels : 3 * channels]
    ref.query[...] = (mm(ref.tokens[slot], w_query) + ref.mix_b[:, 0:channels]).astype(BF16)
    ref.query_t[...] = (mm_t(w_key, ref.query[...]) * (factor * LOG2E)).astype(BF16)
    alive = (count_token > 0.0).astype(F32) * factor
    ref.query_k[...] = (mm_t(ref.query[...], w_key) * alive).astype(BF16)
    ref.grad_att[...] = mm_t(ref.gres[...], ref.out_w[...]).astype(BF16)
    ref.grad_t[...] = mm_t(w_value, ref.grad_att[...])

    lines = jnp.broadcast_to(ref.embedding[...], (8, ref.embedding.shape[-1]))
    film = mm(lines, ref.film_w[...])[0:1] + ref.film_b[...]
    film_scale = 1.0 + film[:, 0:channels]
    film_shift = film[:, channels:]

    ref.mixed_t[...] = jnp.zeros((channels, tokens), F32)
    ref.top[...] = jnp.full((8, tokens), -3e38, F32)
    ref.norm[...] = jnp.zeros((8, tokens), F32)

    def attend_block(index):
        mask = lanes(token_mask(ref.flags[index]), tokens)
        scores = mm(ref.tokens[index], ref.query_t[...])
        scores = jnp.where(mask > 0.5, scores, MASKED * LOG2E)
        old = ref.top[0:1]
        new = jnp.max(scores.reshape(tokens // 8, 8, tokens), axis=0)
        new = jnp.maximum(old, jnp.max(new, axis=0, keepdims=True))
        probs = jnp.exp2(scores - new)
        low_probs = probs.astype(BF16)
        ref.probs[index] = low_probs
        ref.tops[index, 0:1] = new
        ref.top[0:1] = new
        shrink = jnp.exp2(old - new)
        ref.norm[0:1] = ref.norm[0:1] * shrink + total(fold(probs))
        ref.mixed_t[...] = ref.mixed_t[...] * shrink + mm(ref.tokens_t[index], low_probs)

    arrivals = arrival_order(n_row)

    def attend(position):
        block = pick([order[position] for order in arrivals], row)

        def body(lane, carry):
            mine = lane == 0
            index = block * 2 + jnp.where(mine, pair, sibling)

            @pl.when(lane == 1)
            def _():
                link.arrived(ref.raw.at[index], raw_sem + index)

            if position == 0:

                @pl.when(lane == 1)
                def _():
                    normalize(index)
            else:
                normalize(index)
            attend_block(index)
            return carry

        lax.fori_loop(0, 2, body, 0)

    wait_token()
    attend(0)
    raw_step(2) if n_row > 2 else None

    wait_stats2()
    stats = slot_sum(ref.stats2)
    mean2, inv2, size2 = norm_terms(stats[0:1], stats[1:2], count_land, width2)
    slope_m = ref.gain2[...] * film_scale
    shift_m = ref.shift2[...] * film_scale + film_shift

    def mid_row(y, carry):
        grad_sum, grad_dot = carry
        normed = (ref.hidden[y] - mean2) * inv2
        affine = normed * slope_m + shift_m
        gate = sigmoid(affine)
        act = affine * gate
        grad = ref.grad2[y] * (gate * (1.0 + affine * (1.0 - gate)))
        ref.hidden[y] = normed
        ref.grad2[y] = grad
        ref.act2[y] = act.astype(BF16)
        ref.column3[pl.ds(y, 1), :] = jnp.where(side > 0.5, act[0:1], act[span - 1 : span])
        return grad_sum + fold(grad), grad_dot + fold(grad * normed)

    grad_sum2, grad_dot2 = lax.fori_loop(0, height, mid_row, (zero2, zero2))
    ref.stats3[slot] = jnp.zeros((8, channels), F32)
    ref.stats3[slot, 0:1, :] = total(grad_sum2)
    ref.stats3[slot, 1:2, :] = total(grad_dot2)
    wait_stats3 = link.share(ref.stats3)
    wait_act_columns = link.edge_columns(ref.column3, ref.columns3)
    wait_act_rows = link.edge_rows(ref.act2.at[0], ref.act2.at[height - 1], ref.act_up, ref.act_down)

    for a in range(3):
        for b in range(3):
            at = slice((2 - b) * channels, (3 - b) * channels)
            ref.kernel1_t[2 - a, :, at] = ref.kernel1[a, b * c_in : (b + 1) * c_in, :]
    attend(1)

    wait_stats3()
    stats = slot_sum(ref.stats3)
    grad_sum2, grad_dot2 = stats[0:1], stats[1:2]
    grouped = group_total(jnp.concatenate([grad_sum2 * slope_m, grad_dot2 * slope_m], axis=0), width2)
    first2, second2 = grouped[0:1] / size2, grouped[1:2] / size2

    def hidden_row(y, carry):
        normed = ref.hidden[y]
        grad = ref.grad2[y] * slope_m - wide_mask(y) * (first2 + normed * second2)
        grad = (grad * inv2).astype(BF16)
        ref.grad_hidden[y] = grad
        ref.grad_hidden_t[y] = grad.T
        wide = grad.astype(F32)
        ref.column4[pl.ds(y, 1), :] = jnp.where(side > 0.5, wide[0:1], wide[span - 1 : span])
        return carry + fold(wide)

    bias1_sum = lax.fori_loop(0, height, hidden_row, zero2)
    wait_hidden_columns = link.edge_columns(ref.column4, ref.columns4)
    wait_hidden_rows = link.edge_rows(
        ref.grad_hidden.at[0], ref.grad_hidden.at[height - 1], ref.hidden_up, ref.hidden_down
    )
    for step in range(3, n_row):
        raw_step(step)

    def pad_rows(target, source, up, down, columns):
        def edge_row(y, line, edge):
            line = line.astype(F32)
            write_shifted(target, y, line[0:half], line[half:span], edge, channels)

        edge_row(0, up[...], columns[0, height - 1 : height, :])
        edge_row(height + 1, down[...], columns[2, 0:1, :])

        def body(y, carry):
            edge_row(y + 1, source[y], columns[1, pl.ds(y, 1), :])
            return carry

        lax.fori_loop(0, height, body, 0)

    wait_act_rows()
    wait_act_columns()
    pad_rows(ref.padded2, ref.act2, ref.act_up, ref.act_down, ref.columns3)

    def box_row(i, carry):
        for a in range(3):
            value = 0.0
            for dy in range(2):
                for side_x in range(2):
                    line = ref.padded2[2 * i + a + dy, side_x * half : (side_x + 1) * half, :]
                    value = value + line.astype(F32)
            ref.padded3[a * (low // 2) + lax.div(i, 2), pl.ds(lax.rem(i, 2) * half, half), :] = value.astype(BF16)
        value = 0.0
        for dy in range(2):
            for side_x in range(2):
                value = value + ref.image_low[2 * i + dy, side_x * half : (side_x + 1) * half, :].astype(F32)
        ref.image_box[i] = value.astype(BF16)
        return carry

    lax.fori_loop(0, low, box_row, 0)

    def put(target, start, stride, value):
        count = value.shape[0] // 16
        for lane in range(value.shape[1] // 128):
            piece = value[:, lane * 128 : (lane + 1) * 128].astype(BF16)
            target[pl.ds(start + lane * stride, count)] = piece.reshape(count, 16, 128)

    rows_a, rows_c = 9 * channels // 16, 10 * c_in // 16

    def kernel2_grad(a, carry):
        boxes = ref.padded3[pl.ds(a * (low // 2), low // 2)].reshape(low * half, 3 * channels)
        value = mm(ref.gpre_t[...], boxes).T
        put(ref.part_a, a * (rows_a // 3), rows_a, value)
        return carry

    lax.fori_loop(0, 3, kernel2_grad, 0)
    next_a = link.all_sum(ref.part_a, ref.recv1_a, ref.recv2_a, ref.recv3_a, ref.sum_a)

    def kernel1_grad(a, carry):
        value = 0.0
        for y in range(height):
            value = value + mm(ref.grad_hidden_t[y], ref.padded1[a + y])
        put(ref.part_c, a * (3 * c_in // 16), rows_c, value.T)
        return carry

    lax.fori_loop(0, 3, kernel1_grad, 0)
    value = mm(ref.gpre_t[...], ref.image_box[...].reshape(low * half, c_in)).T
    put(ref.part_c, 9 * c_in // 16, rows_c, value)
    next_c = link.all_sum(ref.part_c, ref.recv1_c, ref.recv2_c, ref.recv3_c, ref.sum_c)
    next_a = next_a()

    attend(2) if n_row > 2 else None
    next_c = next_c()
    for position in range(3, n_row):
        attend(position)
    next_a = next_a()

    norm = 1.0 / ref.norm[0:1]
    mixed_t = ref.mixed_t[...] * norm
    ref.mixed_t[...] = mixed_t
    grad_t = (ref.grad_t[...] * norm).astype(BF16)
    delta = total(grad_t.astype(F32) * mixed_t)
    ref.grad_low_t[...] = grad_t
    ref.grad_low[...] = grad_t.T
    ref.grad_query_t[...] = jnp.zeros((channels, tokens), F32)
    next_c = next_c()

    last_top = ref.top[0:1]

    def back_block(index, carry):
        grad_sum, grad_dot = carry
        probs = ref.probs[index].astype(F32) * jnp.exp2(ref.tops[index, 0:1] - last_top)
        grad = mm(ref.tokens[index], ref.grad_low_t[...])
        grad = (probs * (grad - delta)).astype(BF16)
        value = mm(grad, ref.query_k[...]) + mm(probs.astype(BF16), ref.grad_low[...])
        ref.grad_tokens[index] = value.astype(BF16)
        ref.grad_query_t[...] += mm(ref.tokens_t[index], grad)
        return grad_sum + fold(value), grad_dot + fold(value * ref.raw[index].astype(F32))

    orders = chain_order(n_row)
    pair_sem = link.new_recv(n_row)
    chain_sem = link.new_recv(2 * (n_row - 1))

    def chain_at(position):
        target, up, index = (pick([order[position][k] for order in orders], row) for k in range(3))
        has_before = jnp.where(up == 1, row, n_row - 1 - row) > 0
        return target, up, index, has_before

    def back(target, carry):
        def body(lane, carry):
            return back_block(target * 2 + jnp.where(lane == 0, sibling, pair), carry)

        carry = body(0, carry)
        index = target * 2 + sibling
        link.send(ref.grad_tokens.at[index], ref.pair_grad.at[target], link.at(pair=sibling), pair_sem + target)
        return body(1, carry)

    def chain_send(position):
        target, up, index, has_before = chain_at(position)
        link.arrived(ref.pair_grad.at[target], pair_sem + target)
        own = ref.pair_grad[target].astype(F32) + ref.grad_tokens[target * 2 + pair].astype(F32)
        ref.chip_grad[position] = own.astype(BF16)

        @pl.when(has_before)
        def _():
            link.arrived(ref.chain_grad.at[index], chain_sem + index)
            ref.chip_grad[position] = (own + ref.chain_grad[index].astype(F32)).astype(BF16)

        link.send(
            ref.chip_grad.at[position], ref.chain_grad.at[index], link.at(row=row + 2 * up - 1), chain_sem + index
        )

    sums3 = (zero2, zero2)
    for position in range(n_row - 1):
        sums3 = back(chain_at(position)[0], sums3)
        if position > 0:
            chain_send(position - 1)
    sums3 = back(row, sums3)
    chain_send(n_row - 2)
    next_a = next_a()

    grad_query_t = (ref.grad_query_t[...] * alive[0:1, 0:1]).astype(BF16)
    grad_query = mm(grad_query_t.T, w_key).astype(BF16)
    attended = (mm(mixed_t.T.astype(BF16), w_value) + ref.mix_b[:, channels:]).astype(BF16)
    rows_b = channels // 16
    put(ref.part_b, 6 * rows_b, rows_b, mm(attended.T, ref.gres[...]))
    put(ref.part_b, 4 * rows_b, rows_b, mm(mixed_t.astype(BF16), ref.grad_att[...]))
    put(ref.part_b, 0, rows_b, mm(ref.tokens_t[slot], grad_query))
    put(ref.part_b, 2 * rows_b, rows_b, mm(grad_query_t, ref.query[...]))
    next_b = link.all_sum(ref.part_b, ref.recv1_b, ref.recv2_b, ref.recv3_b, ref.sum_b)
    next_c = next_c()

    update = mm(attended, ref.out_w[...]) + ref.out_b[...]
    raw = ref.features[...].astype(F32)
    result = raw + update
    ref.result[...] = result.astype(BF16)
    tmask2 = lanes(ref.token_mask[...], channels)
    update_sum = fold(update * update * tmask2)
    result_sum = fold(result * result * tmask2)
    next_b = next_b()
    ref.grad_own[...] = mm_t(grad_query, w_query)
    own_grad = ref.grad_own[...]
    grad_sum3 = total(sums3[0] + fold(own_grad))
    grad_dot3 = total(sums3[1] + fold(own_grad * raw))

    def conv2_rows(i, carry):
        branch_sum, stream_sum = carry
        pooled = 0.0
        for u in range(2):
            y = 2 * i + u
            branch = mm(ref.padded2[y], ref.kernel2[0])
            branch = branch + mm(ref.padded2[y + 1], ref.kernel2[1])
            branch = branch + mm(ref.padded2[y + 2], ref.kernel2[2])
            branch = branch + ref.bias2[...]
            stream = (branch + mm(ref.image_low[y], ref.skip_w[...]) + ref.skip_b[...]) * math.sqrt(0.5)
            mask = wide_mask(y)
            branch_sum = branch_sum + fold(branch * branch * mask)
            stream_sum = stream_sum + fold(stream * stream * mask)
            pooled = pooled + stream[0:half] + stream[half:span]
        ref.pooled[i] = (pooled * 0.25).astype(BF16)
        return branch_sum, stream_sum

    branch_sum, stream_sum = lax.fori_loop(0, low, conv2_rows, (zero2, zero2))
    next_b = next_b()
    next_a = next_a()

    wait_hidden_rows()
    wait_hidden_columns()
    pad_rows(ref.padded3, ref.grad_hidden, ref.hidden_up, ref.hidden_down, ref.columns4)
    next_c = next_c()

    def back1_row(y, carry):
        grad_sum, grad_dot = carry
        value = mm_t(ref.padded3[y], ref.kernel1_t[0])
        value = value + mm_t(ref.padded3[y + 1], ref.kernel1_t[1])
        value = value + mm_t(ref.padded3[y + 2], ref.kernel1_t[2])
        value = value * ref.slope1[y]
        ref.slope1[y] = value
        return grad_sum + fold(value), grad_dot + fold(value * ref.normed1[y + 1])

    grad_sum1, grad_dot1 = lax.fori_loop(0, height, back1_row, (zero1, zero1))
    ref.stats4[slot] = jnp.zeros((16, channels), F32)
    ref.stats4[slot, 11:12, 0:c_in] = total(grad_dot1)
    ref.stats4[slot, 11:12, c_in:channels] = total(grad_sum1)
    for index, value in enumerate((
        grad_sum3,
        (grad_dot3 - mean3 * grad_sum3) * inv3,
        total(bias1_sum),
        4.0 * total(gpre_sum),
        total(fold(ref.gres[...].astype(F32))),
        total(fold(grad_query.astype(F32))),
        total(fold(ref.grad_att[...].astype(F32))),
        total(branch_sum),
        total(stream_sum),
        total(update_sum),
        total(result_sum),
    )):
        ref.stats4[slot, index : index + 1, :] = value
    wait_stats4 = link.share(ref.stats4)
    next_b = next_b()

    last = n_row - 1
    link.arrived(ref.pair_grad.at[row], pair_sem + row)
    ref.grad_own[...] += ref.pair_grad[row].astype(F32) + ref.grad_tokens[slot].astype(F32)
    for index, exists in ((last - row, row > 0), (last + row, row < last)):

        @pl.when(exists)
        def _(index=index):
            link.arrived(ref.chain_grad.at[index], chain_sem + index)
            ref.grad_own[...] += ref.chain_grad[index].astype(F32)

    wait_stats4()
    stats = slot_sum(ref.stats4)
    ref.vectors[item, 0:16, :] = stats
    ref.vectors[item, 16:24, :] = jnp.zeros((8, channels), F32)
    ref.vectors[item, 12:13, :] = grad_dot2 * film_scale
    ref.vectors[item, 13:14, :] = grad_sum2 * film_scale
    ref.vectors[item, 14:15, :] = grad_dot2 * ref.gain2[...] + grad_sum2 * ref.shift2[...]
    ref.vectors[item, 15:16, :] = grad_sum2
    ref.vectors[item, 16:17, :] = ref.embedding[:, 0:channels].astype(F32)
    ref.vectors[item, 17:18, :] = ref.embedding[:, channels : 2 * channels].astype(F32)
    ref.vectors[item, 18:19, 0:c_in] = stats1[0:1, c_in:channels]
    ref.vectors[item, 19:20, :] = stats1[3:4]
    mine = ref.vectors.at[item]
    wait_vectors = link.send_all(
        [(mine, mine, device) for _, device in link.others_in_item()], ref.vectors.at[pl.ds(0, n_item - 1)]
    )
    next_b = next_b()

    grad_sum1, grad_dot1 = stats[11:12, c_in:channels], stats[11:12, 0:c_in]
    grouped = group_total(jnp.concatenate([grad_sum1 * gain1, grad_dot1 * gain1], axis=0), width1)
    first1, second1 = grouped[0:1] / size1, grouped[1:2] / size1

    def image_grad_rows(i, carry):
        skip = mm_t(ref.gpre[i], ref.skip_w[...])
        skip = jnp.concatenate([skip, skip], axis=0)
        for u in range(2):
            y = 2 * i + u
            value = ref.slope1[y] * gain1 - ref.mask[y] * (first1 + ref.normed1[y + 1] * second1)
            value = value * inv1 + skip
            ref.line[pl.ds(0, half, stride=2), :] = value[0:half]
            ref.line[pl.ds(1, half, stride=2), :] = value[half:span]
            ref.image_grad[y] = ref.line[...].astype(BF16)
        return carry

    lax.fori_loop(0, low, image_grad_rows, 0)
    next_b = next_b()

    gain3 = ref.gain3[...]
    grouped = group_total(jnp.concatenate([stats[0:1] * gain3, stats[1:2] * gain3], axis=0), width2)
    first3, second3 = grouped[0:1] / size3, grouped[1:2] / size3
    normed = (ref.features[...].astype(F32) - mean3) * inv3
    value = (ref.grad_own[...] * gain3 - lanes(ref.token_mask[...], channels) * (first3 + normed * second3)) * inv3
    ref.features_grad[...] = (ref.gres[...].astype(F32) + value).astype(BF16)

    wait_vectors()
    for step in (next_a, next_c, next_b):
        while step is not None:
            step = step()
    link.finish()
    assert link.sends <= ref.send_sem.shape[0] and link.recvs <= ref.recv_sem.shape[0], (link.sends, link.recvs)


SCRATCH = (
    "send_sem", "recv_sem", "flags", "raw", "image_up", "image_down", "pool_up", "pool_down", "mask",
    "token_mask", "line", "normed1", "image_low", "column1", "columns1", "stats1", "gpre", "gpre_t",
    "column2", "columns2", "coarse", "padded_g", "grad2", "slope1", "padded1", "hidden", "stats2",
    "tokens", "tokens_t", "query", "query_t", "query_k", "grad_att", "grad_t", "act2", "column3",
    "columns3", "stats3", "act_up", "act_down", "kernel1_t", "grad_hidden", "grad_hidden_t", "column4",
    "columns4", "hidden_up", "hidden_down", "padded2", "image_box", "part_a", "recv1_a",
    "recv2_a", "recv3_a", "part_b", "recv1_b", "recv2_b", "recv3_b", "part_c", "recv1_c", "recv2_c",
    "recv3_c", "padded3", "stats4", "top", "tops", "norm", "probs", "mixed_t", "grad_low_t", "grad_low",
    "grad_query_t", "grad_tokens", "pair_grad", "chip_grad", "chain_grad", "grad_own",
)


def last_kernel(n_item, *refs):
    (pooled, result, image_grad, features_grad, sum_a, sum_b, sum_c, vectors) = refs[:8]
    (o_pooled, o_result, o_image, o_features, o_gain1, o_shift1, o_kernel1, o_bias1, o_film_w, o_film_b,
     o_gain2, o_shift2, o_kernel2, o_bias2, o_skip_w, o_skip_b, o_gain3, o_shift3, o_mix_w, o_mix_b,
     o_out_w, o_out_b, o_rms) = refs[8:]
    o_pooled[...] = pooled[...]
    o_result[...] = result[...]
    o_image[...] = image_grad[...]
    o_features[...] = features_grad[...]
    channels = o_bias1.shape[-1]
    c_in = o_gain1.shape[-1]

    def blocks(ref, start, count):
        return ref[start : start + count].reshape(count * 16, 128).astype(F32)

    lanes = channels // 128
    n_a, n_c, n_k = 9 * channels // 16, 10 * c_in // 16, 9 * c_in // 16
    for lane in range(lanes):
        at = slice(lane * 128, (lane + 1) * 128)
        o_kernel2[:, at] = blocks(sum_a, lane * n_a, n_a)
        o_kernel1[:, at] = blocks(sum_c, lane * n_c, n_k)
        o_skip_w[:, at] = blocks(sum_c, lane * n_c + n_k, n_c - n_k)
    n_b = channels // 16
    for lane in range(3 * lanes):
        o_mix_w[:, lane * 128 : (lane + 1) * 128] = blocks(sum_b, lane * n_b, n_b)
    for lane in range(lanes):
        o_out_w[:, lane * 128 : (lane + 1) * 128] = blocks(sum_b, (3 * lanes + lane) * n_b, n_b)
    value = vectors[0]
    for item in range(1, n_item):
        value = value + vectors[item]
    o_shift3[...] = value[0:1]
    o_gain3[...] = value[1:2]
    o_bias1[...] = value[2:3]
    o_bias2[...] = value[3:4]
    o_skip_b[...] = value[3:4]
    o_out_b[...] = value[4:5]
    o_mix_b[:, 0:channels] = value[5:6]
    o_mix_b[:, channels:] = value[6:7]
    o_gain1[...] = value[11:12, 0:c_in]
    o_shift1[...] = value[11:12, c_in:channels]
    o_gain2[...] = value[12:13]
    o_shift2[...] = value[13:14]
    o_film_b[:, 0:channels] = value[14:15]
    o_film_b[:, channels:] = value[15:16]
    pad = jnp.zeros((8 - n_item, 2 * channels), F32)
    embedding = jnp.concatenate(
        [jnp.concatenate([vectors[i, 16:17, :], vectors[i, 17:18, :]], axis=1) for i in range(n_item)] + [pad], axis=0
    )
    grads = jnp.concatenate(
        [jnp.concatenate([vectors[i, 14:15, :], vectors[i, 15:16, :]], axis=1) for i in range(n_item)] + [pad], axis=0
    )
    o_film_w[...] = lax.dot_general(
        embedding, grads, (((0,), (0,)), ((), ())), precision=HIGHEST, preferred_element_type=F32
    )

    def lane_sum(row):
        return jnp.sum(row, axis=1, keepdims=True)

    land = jnp.maximum(value[19:20, 0:1], 1.0)
    token = jnp.maximum(value[19:20, 128:129], 1.0)
    place = iota((1, 5), 1)
    rms = jnp.zeros((1, 5), F32)
    for index, (square, count) in enumerate((
        (lane_sum(value[18:19, 0:c_in]), land * c_in),
        (lane_sum(value[7:8]), land * channels),
        (lane_sum(value[8:9]), land * channels),
        (lane_sum(value[9:10]), token * channels),
        (lane_sum(value[10:11]), token * channels),
    )):
        rms = jnp.where(place == index, jnp.sqrt(square / count), rms)
    o_rms[...] = rms


def on_device(mesh_shape, *args):
    names = INPUTS
    arg = SimpleNamespace(**dict(zip(names, args)))
    n_item, n_row = mesh_shape["item"], mesh_shape["row"]
    n_group = 2 * n_row
    _, height, span, c_in = arg.image.shape
    channels = arg.bias1.shape[-1]
    _, rows_t, cols_t, _ = arg.features.shape
    tokens = rows_t * cols_t
    low, half = height // 2, span // 2
    inputs = [
        arg.image.reshape(height, span, c_in),
        arg.land_mask.reshape(height, span) if hasattr(arg, "land_mask") else arg.land.reshape(height, span),
        arg.embedding,
        arg.gain1.reshape(1, c_in),
        arg.shift1.reshape(1, c_in),
        arg.kernel1.reshape(3, 3 * c_in, channels),
        arg.bias1.reshape(1, channels),
        arg.film_w,
        arg.film_b.reshape(1, 2 * channels),
        arg.gain2.reshape(1, channels),
        arg.shift2.reshape(1, channels),
        arg.kernel2.reshape(3, 3 * channels, channels),
        arg.bias2.reshape(1, channels),
        arg.skip_w,
        arg.skip_b.reshape(1, channels),
        arg.features.reshape(tokens, channels),
        arg.token.reshape(rows_t, cols_t),
        arg.gain3.reshape(1, channels),
        arg.shift3.reshape(1, channels),
        arg.mix_w,
        arg.mix_b.reshape(1, 2 * channels),
        arg.out_w,
        arg.out_b.reshape(1, channels),
        arg.gpool.reshape(low, half, channels),
        arg.gres.reshape(tokens, channels),
    ]
    share = 2 * n_item * n_row
    blocks_a = -(-9 * channels * channels // 2048 // share) * share
    blocks_b = -(-4 * channels * channels // 2048 // share) * share
    blocks_c = -(-10 * c_in * channels // 2048 // share) * share
    vmem = pltpu.VMEM

    def sums(blocks):
        unit = blocks // 2 // n_item
        return [
            vmem((blocks, 16, 128), BF16),
            vmem((blocks // 2, 16, 128), BF16),
            vmem((n_item - 1, unit, 16, 128), BF16),
            vmem((n_row - 1, unit // n_row, 16, 128), BF16),
        ]

    scratch = [
        pltpu.SemaphoreType.DMA((52 + 6 * n_row,)),
        pltpu.SemaphoreType.DMA((44 + 5 * n_row,)),
        vmem((n_group, rows_t, cols_t), jnp.int32),
        vmem((n_group, tokens, channels), BF16),
        vmem((span, c_in), BF16),
        vmem((span, c_in), BF16),
        vmem((half, channels), BF16),
        vmem((half, channels), BF16),
        vmem((height, span, 128), F32),
        vmem((tokens, 128), F32),
        vmem((span, c_in), F32),
        vmem((height + 2, span, c_in), F32),
        vmem((height, span, c_in), BF16),
        vmem((8, c_in), F32),
        vmem((3, 8, c_in), F32),
        vmem((n_group, 8, channels), F32),
        vmem((low, half, channels), BF16),
        vmem((channels, low * half), BF16),
        vmem((8, channels), F32),
        vmem((3, 8, channels), F32),
        vmem((8, channels, 2 * channels) if n_group < 8 or tokens < 2 * channels else (8, 16, 128), BF16),
        vmem((low + 2, half, 3 * channels), BF16),
        vmem((height, span, channels), F32),
        vmem((height, span, c_in), F32),
        vmem((height + 2, span, 3 * c_in), BF16),
        vmem((height, span, channels), F32),
        vmem((n_group, 8, channels), F32),
        vmem((n_group, tokens, channels), BF16),
        vmem((n_group, channels, tokens), BF16),
        vmem((tokens, channels), BF16),
        vmem((channels, tokens), BF16),
        vmem((tokens, channels), BF16),
        vmem((tokens, channels), BF16),
        vmem((channels, tokens), F32),
        vmem((height, span, channels), BF16),
        vmem((8, channels), F32),
        vmem((3, 8, channels), F32),
        vmem((n_group, 8, channels), F32),
        vmem((span, channels), BF16),
        vmem((span, channels), BF16),
        vmem((3, c_in, 3 * channels), BF16),
        vmem((height, span, channels), BF16),
        vmem((height, channels, span), BF16),
        vmem((8, channels), F32),
        vmem((3, 8, channels), F32),
        vmem((span, channels), BF16),
        vmem((span, channels), BF16),
        vmem((height + 2, span, 3 * channels), BF16),
        vmem((low, half, c_in), BF16),
        *sums(blocks_a),
        *sums(blocks_b),
        *sums(blocks_c),
        vmem((height + 2, span, 3 * channels), BF16),
        vmem((n_group, 16, channels), F32),
        vmem((8, tokens), F32),
        vmem((n_group, 8, tokens), F32),
        vmem((8, tokens), F32),
        vmem((n_group, tokens, tokens), BF16),
        vmem((channels, tokens), F32),
        vmem((channels, tokens), BF16),
        vmem((tokens, channels), BF16),
        vmem((channels, tokens), F32),
        vmem((n_group, tokens, channels), BF16),
        vmem((n_row, tokens, channels), BF16),
        vmem((n_row - 1, tokens, channels), BF16),
        vmem((2 * (n_row - 1), tokens, channels), BF16),
        vmem((tokens, channels), F32),
    ]
    shape = jax.ShapeDtypeStruct
    mid = [
        shape((low, half, channels), BF16),
        shape((tokens, channels), BF16),
        shape((height, span, c_in), BF16),
        shape((tokens, channels), BF16),
        shape((blocks_a, 16, 128), BF16),
        shape((blocks_b, 16, 128), BF16),
        shape((blocks_c, 16, 128), BF16),
        shape((n_item, 24, channels), F32),
    ]
    in_vmem = pl.BlockSpec(memory_space=vmem)
    parts = pl.pallas_call(
        functools.partial(main_kernel, n_item, n_row),
        out_shape=mid,
        in_specs=[in_vmem] * len(inputs),
        out_specs=[in_vmem] * len(mid),
        scratch_shapes=scratch,
        compiler_params=pltpu.CompilerParams(
            collective_id=0, has_side_effects=True, vmem_limit_bytes=int(63.9 * 1024 * 1024)
        ),
    )(*inputs)
    emb = arg.embedding.shape[-1]
    final = [
        *mid[:4],
        shape((1, c_in), F32),
        shape((1, c_in), F32),
        shape((9 * c_in, channels), F32),
        shape((1, channels), F32),
        shape((emb, 2 * channels), F32),
        shape((1, 2 * channels), F32),
        shape((1, channels), F32),
        shape((1, channels), F32),
        shape((9 * channels, channels), F32),
        shape((1, channels), F32),
        shape((c_in, channels), F32),
        shape((1, channels), F32),
        shape((1, channels), F32),
        shape((1, channels), F32),
        shape((channels, 3 * channels), F32),
        shape((1, 2 * channels), F32),
        shape((channels, channels), F32),
        shape((1, channels), F32),
        shape((1, 5), F32),
    ]
    outs = pl.pallas_call(
        functools.partial(last_kernel, n_item),
        out_shape=final,
        in_specs=[in_vmem] * len(mid),
        out_specs=[in_vmem] * len(final),
        compiler_params=pltpu.CompilerParams(vmem_limit_bytes=int(63.9 * 1024 * 1024)),
    )(*parts)
    shapes = (
        (1, low, half, channels),
        (1, rows_t, cols_t, channels),
        (1, height, span, c_in),
        (1, rows_t, cols_t, channels),
        (c_in,),
        (c_in,),
        (3, 3, c_in, channels),
        (channels,),
        (emb, 2 * channels),
        (2 * channels,),
        (channels,),
        (channels,),
        (3, 3, channels, channels),
        (channels,),
        (c_in, channels),
        (channels,),
        (channels,),
        (channels,),
        (channels, 3 * channels),
        (2 * channels,),
        (channels, channels),
        (channels,),
        (5,),
    )
    return tuple(out.reshape(to) for out, to in zip(outs, shapes))


def solution(mesh):
    tiled = P("item", "row", "pair", None)
    mask = P("item", "row", "pair")
    in_specs = [P()] * len(INPUTS)
    for name in ("image", "features", "gpool", "gres"):
        in_specs[INPUTS.index(name)] = tiled
    for name in ("land", "token"):
        in_specs[INPUTS.index(name)] = mask
    in_specs[INPUTS.index("embedding")] = P("item", None)
    return jax.shard_map(
        functools.partial(on_device, dict(mesh.shape)),
        mesh=mesh,
        in_specs=tuple(in_specs),
        out_specs=(tiled,) * 4 + (P(),) * 19,
        check_vma=False,
    )
```

time: 154 us -> 114 us (0.74)
  Pallas kernels: 145 us -> 113 us
  local copies, waits for them, and re-layouts: 8.17 us -> 0 us
    pallas_call x1, Pallas kernels: 141 us -> 107 us  [on_device(): pl.pallas_call(functools.partial(main_kernel, n_item, n_row), out_shape=m...]
    unnamed x16 -> x0, local copies, waits for them, and re-layouts: 8.17 us -> none
    pallas_call x1, Pallas kernels: 3.92 us -> 5.96 us  [on_device(): pl.pallas_call(functools.partial(last_kernel, n_item), out_shape=final, i...]
where the time goes in v1:
time: 114 us
  Pallas kernels  113 us (99%)
    pallas_call x1, Pallas kernels, on_device(): pl.pallas_call(functools.partial(main_kernel, n_item, n_row), out_shape=m...  107 us
    pallas_call x1, Pallas kernels, on_device(): pl.pallas_call(functools.partial(last_kernel, n_item), out_shape=final, i...  5.96 us

profile of v1, /device:TPU:0, one launch (start us, length us, event | category | flops | bytes accessed | tf_op | source)
XLA Modules:
  0.0 113.7 jit_solution(5819047205607897392)
XLA Ops:
  0.7 106.9 %shard_map.416 = (bf16[4,128,256]{2,1,0:T(8,128)(2,1)}, bf16[512,256]{1,0:T(8,128)(2,1)}, bf16[8,256,128]{2,1,0:T(8,128)(2,1)}, bf16[512,256]{1,0:T(8,128)(2,1)}...) custom-call(bf16[8,256,128]{2,1,0:T(8,128)(2,1)} %bitcast.41, ...), custom_call_target="tpu_custom_call" | custom-call | tf_op jit(solution)/shard_map/pallas_call | solution.py:1171
  107.5 6.0 %shard_map.417 = (bf16[4,128,256]{2,1,0:T(8,128)(2,1)}, bf16[512,256]{1,0:T(8,128)(2,1)}, bf16[8,256,128]{2,1,0:T(8,128)(2,1)}, bf16[512,256]{1,0:T(8,128)(2,1)}...) custom-call(bf16[4,128,256]{2,1,0:T(8,128)(2,1)} %get-tuple-element., ...), custom_call_target="tpu_custom_call" | custom-call | tf_op jit(solution)/shard_map/pallas_call | solution.py:1204

commit v2 on v1

v2 whole, which is shorter than its diff:
```python
import functools
import math
from types import SimpleNamespace
from typing import Any, NamedTuple

import jax
import jax.numpy as jnp
from jax import lax
from jax.experimental import pallas as pl
from jax.experimental.pallas import tpu as pltpu
from jax.sharding import PartitionSpec as P

GROUPS = 32
EPS = 1e-05
MASKED = -1000000000.0
LOG2E = 1.4426950408889634
F32 = jnp.float32
BF16 = jnp.bfloat16
MESH = pl.DeviceIdType.MESH
HIGHEST = lax.Precision.HIGHEST


def mm(left, right):
    return jnp.dot(left, right, preferred_element_type=F32)


def mm_t(left, right):
    return lax.dot_general(left, right, (((1,), (1,)), ((), ())), preferred_element_type=F32)


def iota(shape, dim):
    return lax.broadcasted_iota(jnp.int32, shape, dim)


def fold(value):
    rows, width = value.shape
    return jnp.sum(value.reshape(rows // 8, 8, width), axis=0)


def total(value):
    return jnp.sum(value, axis=0, keepdims=True)


def group_total(rows, width):
    channels = rows.shape[-1]
    left = jnp.floor(iota((channels, channels), 0).astype(F32) * (1.0 / width))
    right = jnp.floor(iota((channels, channels), 1).astype(F32) * (1.0 / width))
    same = (left == right).astype(F32)
    padded = jnp.concatenate([rows, jnp.zeros((8 - rows.shape[0], channels), F32)], axis=0)
    return jnp.dot(padded, same, precision=HIGHEST, preferred_element_type=F32)


def sigmoid(value):
    return 0.5 * jnp.tanh(0.5 * value) + 0.5


class Inputs(NamedTuple):
    image: Any
    land: Any
    embedding: Any
    gain1: Any
    shift1: Any
    kernel1: Any
    bias1: Any
    film_w: Any
    film_b: Any
    gain2: Any
    shift2: Any
    kernel2: Any
    bias2: Any
    skip_w: Any
    skip_b: Any
    features: Any
    token: Any
    gain3: Any
    shift3: Any
    mix_w: Any
    mix_b: Any
    out_w: Any
    out_b: Any
    gpool: Any
    gres: Any


class Results(NamedTuple):
    pooled: Any
    result: Any
    image_grad: Any
    features_grad: Any
    sum_a: Any
    sum_b: Any
    sum_c: Any
    vectors: Any


INPUTS, RESULTS = Inputs._fields, Results._fields
FETCHED = ("kernel2", "kernel1", "film_w", "mix_w", "out_w", "skip_w", "gres")


class Links:
    def __init__(self, ref, n_item, n_row):
        self.ref = ref
        self.n_item, self.n_row, self.n_group = n_item, n_row, n_row * 2
        self.item, self.row, self.pair = (lax.axis_index(a) for a in ("item", "row", "pair"))
        self.sibling = 1 - self.pair
        self.slot = self.row * 2 + self.pair
        self.sends = 0
        self.recvs = 0
        self.pending = []

    def at(self, row=None, pair=None, item=None):
        return (
            self.item if item is None else item,
            self.row if row is None else row,
            self.pair if pair is None else pair,
        )

    def others_in_group(self):
        for step in range(1, self.n_group):
            other = lax.rem(self.slot + step, self.n_group)
            yield other, self.at(lax.div(other, 2), lax.rem(other, 2))

    def others_in_row(self):
        for step in range(1, self.n_row):
            other = lax.rem(self.row + step, self.n_row)
            yield other, self.at(row=other)

    def others_in_item(self):
        for step in range(1, self.n_item):
            other = lax.rem(self.item + step, self.n_item)
            yield other, self.at(item=other)

    def new_recv(self, count=1):
        self.recvs += count
        return self.recvs - count

    def copy(self, source, target, device, send, recv):
        return pltpu.make_async_remote_copy(
            src_ref=source,
            dst_ref=target,
            send_sem=self.ref.send_sem.at[send],
            recv_sem=self.ref.recv_sem.at[recv],
            device_id=device,
            device_id_type=MESH,
        )

    def send(self, source, target, device, recv, when=None):
        index = self.sends
        self.sends += 1

        def make():
            return self.copy(source, target, device, index, recv)

        if when is None:
            make().start()
        else:
            pl.when(when)(lambda: make().start())
        self.pending.append((make, when))

    def send_all(self, copies, size):
        index, recv = self.sends, self.new_recv()
        self.sends += 1
        for source, target, device in copies:
            self.copy(source, target, device, index, recv).start()
        whole = self.copy(size, size, self.at(pair=self.sibling), index, recv)
        self.pending.append((lambda: whole, None))
        return whole.wait_recv

    def arrived(self, target, recv, when=None):
        def wait():
            self.copy(target, target, self.at(pair=self.sibling), 0, recv).wait_recv()

        if when is None:
            wait()
        else:
            pl.when(when)(wait)

    def finish(self):
        for make, when in self.pending:
            if when is None:
                make().wait_send()
            else:
                pl.when(when)(lambda make=make: make().wait_send())

    def greet(self):
        barrier = pltpu.get_barrier_semaphore()
        devices = [d for _, d in self.others_in_group()] + [d for _, d in self.others_in_item()]
        for device in devices:
            pl.semaphore_signal(barrier, inc=1, device_id=device, device_id_type=MESH)
        return lambda: pl.semaphore_wait(barrier, len(devices))

    def share(self, slots):
        mine = slots.at[self.slot]
        copies = [(mine, mine, device) for _, device in self.others_in_group()]
        return self.send_all(copies, slots.at[pl.ds(0, self.n_group - 1)])

    def edge_rows(self, first, last, above, below):
        has_above, has_below = self.row > 0, self.row < self.n_row - 1
        from_above, from_below = self.new_recv(), self.new_recv()
        self.send(first, below, self.at(row=self.row - 1), from_below, has_above)
        self.send(last, above, self.at(row=self.row + 1), from_above, has_below)

        def wait():
            self.arrived(above, from_above, has_above)
            self.arrived(below, from_below, has_below)

            @pl.when(self.row == 0)
            def _():
                above[...] = jnp.zeros(above.shape, above.dtype)

            @pl.when(self.row == self.n_row - 1)
            def _():
                below[...] = jnp.zeros(below.shape, below.dtype)

        return wait

    def edge_columns(self, column, columns):
        has_above, has_below = self.row > 0, self.row < self.n_row - 1
        base = self.new_recv(3)
        self.send(column, columns.at[2], self.at(self.row - 1, self.sibling), base + 2, has_above)
        self.send(column, columns.at[0], self.at(self.row + 1, self.sibling), base, has_below)
        self.send(column, columns.at[1], self.at(pair=self.sibling), base + 1)

        def wait():
            self.arrived(columns.at[1], base + 1)
            self.arrived(columns.at[0], base, has_above)
            self.arrived(columns.at[2], base + 2, has_below)

            @pl.when(self.row == 0)
            def _():
                columns[0] = jnp.zeros(columns.shape[1:], columns.dtype)

            @pl.when(self.row == self.n_row - 1)
            def _():
                columns[2] = jnp.zeros(columns.shape[1:], columns.dtype)

        return wait

    def all_sum(self, part, recv1, recv2, recv3, out):
        half = part.shape[0] // 2
        quarter = half // self.n_item
        chunk = quarter // self.n_row
        mine = self.pair * half
        item_at = mine + self.item * quarter
        own = item_at + self.row * chunk

        def span(ref, start, size):
            return ref.at[pl.ds(start, size)]

        def grow(start, size, arrivals):
            value = part[pl.ds(start, size)].astype(F32)
            for arrival in arrivals:
                value = value + arrival.astype(F32)
            return value.astype(BF16)

        def stage2():
            wait1()
            part[pl.ds(mine, half)] = grow(mine, half, [recv1[...]])
            copies = [
                (span(part, mine + other * quarter, quarter), recv2.at[step], device)
                for step, (other, device) in enumerate(self.others_in_item())
            ]
            wait2 = self.send_all(copies, recv2)

            def stage3():
                wait2()
                part[pl.ds(item_at, quarter)] = grow(item_at, quarter, [recv2[k] for k in range(self.n_item - 1)])
                copies = [
                    (span(part, item_at + other * chunk, chunk), recv3.at[step], device)
                    for step, (other, device) in enumerate(self.others_in_row())
                ]
                wait3 = self.send_all(copies, recv3)

                def stage4():
                    wait3()
                    out[pl.ds(own, chunk)] = grow(own, chunk, [recv3[k] for k in range(self.n_row - 1)])
                    source = span(out, own, chunk)
                    copies = [(source, source, device) for _, device in self.others_in_row()]
                    wait4 = self.send_all(copies, span(out, 0, (self.n_row - 1) * chunk))

                    def stage5():
                        wait4()
                        source = span(out, item_at, quarter)
                        copies = [(source, source, device) for _, device in self.others_in_item()]
                        wait5 = self.send_all(copies, span(out, 0, (self.n_item - 1) * quarter))

                        def stage6():
                            wait5()
                            source = span(out, mine, half)
                            return self.send_all([(source, source, self.at(pair=self.sibling))], span(out, 0, half))

                        return stage6

                    return stage5

                return stage4

            return stage3

        wait1 = self.send_all([(span(part, self.sibling * half, half), recv1, self.at(pair=self.sibling))], recv1)
        return stage2


def norm_terms(sums, squares, count, width):
    size = jnp.maximum(count, 1.0) * width
    grouped = group_total(jnp.concatenate([sums, squares], axis=0), width)
    mean = grouped[0:1] / size
    return mean, lax.rsqrt(grouped[1:2] / size - mean * mean + EPS), size


def chain_order(n_row):
    orders = []
    for row in range(n_row):
        steps = [(row + s, 0, n_row - 1 - s, s) for s in range(n_row - 1) if n_row - 1 - s > row]
        steps += [(n_row - 1 - row + s, 1, s, s) for s in range(n_row - 1) if s < row]
        steps.sort()
        orders.append([(target, 1 - down, down * (n_row - 1) + s) for _, down, target, s in steps])
    return orders


def arrival_order(n_row):
    orders = []
    for row in range(n_row):
        found = [row]
        for step in range(1, n_row):
            found += [r for r in (row - step, row + step) if 0 <= r < n_row]
        orders.append(found)
    return orders


def pick(values, index):
    chosen = jnp.int32(0)
    for k, value in enumerate(values):
        chosen = chosen + jnp.where(index == k, jnp.int32(value), jnp.int32(0))
    return chosen


def main_kernel(n_item, n_row, *refs):
    names = INPUTS + RESULTS + SCRATCH
    ref = SimpleNamespace(**dict(zip(names, refs)))
    fetches = []
    for index, name in enumerate(FETCHED):
        fetches.append(pltpu.make_async_copy(getattr(ref, name), getattr(ref, name + "_in"), ref.local_sem.at[index]))
        fetches[-1].start()
        setattr(ref, name, getattr(ref, name + "_in"))
    stores = []
    homes = {name: getattr(ref, name) for name in RESULTS}
    for name in RESULTS:
        setattr(ref, name, getattr(ref, name + "_out"))

    def store(name):
        copy = pltpu.make_async_copy(getattr(ref, name), homes[name], ref.local_sem.at[len(FETCHED) + len(stores)])
        copy.start()
        stores.append(copy)

    link = Links(ref, n_item, n_row)
    height, span, c_in = ref.image.shape
    channels = ref.bias1.shape[-1]
    half = span // 2
    tokens = ref.features.shape[0]
    n_group = link.n_group
    low = height // 2
    side = link.pair.astype(F32)
    width1, width2 = c_in // GROUPS, channels // GROUPS
    slot, item, row, pair, sibling = link.slot, link.item, link.row, link.pair, link.sibling
    has_up = (row > 0).astype(F32)
    has_down = (row < n_row - 1).astype(F32)
    factor = channels ** (-0.5)
    zero1 = jnp.zeros((8, c_in), F32)
    zero2 = jnp.zeros((8, channels), F32)
    rows_t, cols_t = ref.token.shape
    now = SimpleNamespace()

    def lanes(mask, width):
        if width <= mask.shape[1]:
            return mask[:, 0:width]
        return jnp.concatenate([mask] * (width // mask.shape[1]), axis=1)

    def wide_mask(y):
        return lanes(ref.mask[y], channels)

    def inner(y):
        return ((y > 0) & (y < height + 1)).astype(F32)

    def exists(y):
        return jnp.where(y == 0, has_up, jnp.where(y == height + 1, has_down, 1.0))

    def slot_sum(slots):
        value = slots[0]
        for other in range(1, n_group):
            value = value + slots[other]
        return value

    def land_line(line):
        place = iota((span, span), 0)
        place = jnp.where(place < half, 2 * place, 2 * (place - half) + 1)
        line = jnp.broadcast_to(line.astype(F32), (span, span))
        line = jnp.where(place == iota((span, span), 1), line, 0.0).astype(BF16)
        return mm(line, jnp.ones((span, 128), BF16))

    def token_mask(flags):
        chosen = iota((rows_t, cols_t, rows_t), 0) == iota((rows_t, cols_t, rows_t), 2)
        lines = mm(chosen.reshape(tokens, rows_t).astype(BF16), flags)
        keep = (iota((rows_t, cols_t, cols_t), 1) == iota((rows_t, cols_t, cols_t), 2)).reshape(tokens, cols_t)
        return mm(jnp.where(keep, lines, 0.0).astype(BF16), jnp.ones((cols_t, 128), BF16))

    def split_row(y, line):
        ref.line[...] = line.astype(F32)
        even = ref.line[pl.ds(0, half, stride=2), :]
        odd = ref.line[pl.ds(1, half, stride=2), :]
        ref.normed1[y, 0:half] = even
        ref.normed1[y, half:span] = odd
        return even, odd

    def write_shifted(target, y, even, odd, edge, size):
        top = iota((half, size), 0) == 0
        end = iota((half, size), 0) == half - 1
        before = jnp.where(top, edge * side, pltpu.roll(odd, 1, 0)).astype(BF16)
        after = jnp.where(end, edge * (1.0 - side), pltpu.roll(even, half - 1, 0)).astype(BF16)
        even, odd = even.astype(BF16), odd.astype(BF16)
        target[y, 0:half, 0:size] = before
        target[y, 0:half, size : 2 * size] = even
        target[y, 0:half, 2 * size : 3 * size] = odd
        target[y, half:span, 0:size] = even
        target[y, half:span, size : 2 * size] = odd
        target[y, half:span, 2 * size : 3 * size] = after

    def set_edges(target, edges):
        size = channels

        def body(y, carry):
            edge = edges[pl.ds(y, 1), :]

            @pl.when(pair == 1)
            def _():
                tile = target[y, 0:16, 0:size].astype(F32)
                target[y, 0:16, 0:size] = jnp.where(iota((16, size), 0) == 0, edge, tile).astype(BF16)

            @pl.when(pair == 0)
            def _():
                tile = target[y, span - 16 : span, 2 * size : 3 * size].astype(F32)
                tile = jnp.where(iota((16, size), 0) == 15, edge, tile).astype(BF16)
                target[y, span - 16 : span, 2 * size : 3 * size] = tile

            return carry

        lax.fori_loop(0, height + 2, body, 0)

    def put(target, start, stride, value):
        count = value.shape[0] // 16
        for lane in range(value.shape[1] // 128):
            piece = value[:, lane * 128 : (lane + 1) * 128].astype(BF16)
            target[pl.ds(start + lane * stride, count)] = piece.reshape(count, 16, 128)

    rows_a, rows_b, rows_c = 9 * channels // 16, channels // 16, 10 * c_in // 16

    def local():
        def land_row(y, carry):
            ref.mask[y + 1] = land_line(ref.land[pl.ds(y, 1), :])
            return carry

        lax.fori_loop(0, height, land_row, 0)
        ref.token_mask[...] = token_mask(ref.token[...].astype(F32).astype(BF16))

        def image_row(y, carry):
            sums, squares, count = carry
            even, odd = split_row(y + 2, ref.image[y])
            value = jnp.concatenate([even, odd], axis=0)
            ref.image_low[y] = value.astype(BF16)
            ref.column1[pl.ds(y, 1), :] = jnp.where(side > 0.5, even[0:1], odd[half - 1 : half])
            mask = ref.mask[y + 1]
            masked = value * mask
            return sums + fold(masked), squares + fold(masked * value), count + fold(mask)

        sums, squares, count = lax.fori_loop(0, height, image_row, (zero1, zero1, jnp.zeros((8, 128), F32)))
        raw = ref.features[...].astype(F32)
        tmask = ref.token_mask[...]
        masked = raw * lanes(tmask, channels)
        ref.stats1[slot, 0:1, 0:c_in] = total(sums)
        ref.stats1[slot, 0:1, c_in:channels] = total(squares)
        ref.stats1[slot, 1:2, :] = total(masked)
        ref.stats1[slot, 2:3, :] = total(masked * raw)
        ref.stats1[slot, 3:4, 0:128] = total(count)
        ref.stats1[slot, 3:4, 128:256] = total(tmask)
        now.gpre_sum = zero2
        for i in range(low):
            value = (ref.gpool[i].astype(F32) * 0.25 * math.sqrt(0.5)).astype(BF16)
            ref.gpre[i] = value
            ref.gpre_t[:, i * half : (i + 1) * half] = value.T
            wide = value.astype(F32)
            ref.column2[i : i + 1, :] = jnp.where(side > 0.5, wide[0:1], wide[half - 1 : half])
            now.gpre_sum = now.gpre_sum + fold(wide)
        ref.flags[slot, 0:rows_t] = ref.token[...].astype(F32).astype(BF16)
        ref.raw[slot] = ref.features[...]

    def raw_send(block, device, when=None):
        index = block * 2 + pair
        link.send(ref.raw.at[index], ref.raw.at[index], device, now.raw_sem + index, when)

    def first_sends():
        now.wait_stats1 = link.share(ref.stats1)
        now.wait_pool_columns = link.edge_columns(ref.column2, ref.columns2)
        now.wait_image_columns = link.edge_columns(ref.column1, ref.columns1)
        now.wait_pool_rows = link.edge_rows(ref.gpool.at[0], ref.gpool.at[low - 1], ref.pool_up, ref.pool_down)
        now.wait_image_rows = link.edge_rows(
            ref.image.at[pl.ds(0, 2)], ref.image.at[pl.ds(height - 2, 2)], ref.image_up, ref.image_down
        )
        now.wait_land_rows = link.edge_rows(ref.land, ref.land, ref.land_up, ref.land_down)
        now.wait_token = link.share(ref.flags)
        now.raw_sem = link.new_recv(n_group)
        raw_send(row, link.at(row=row + 1), row < n_row - 1)
        raw_send(row, link.at(row=row - 1), row > 0)
        raw_send(row, link.at(pair=sibling))

    def raw_step(step):
        below, above = row - step, row + step
        link.arrived(ref.raw.at[below * 2 + pair], now.raw_sem + below * 2 + pair, below >= 0)
        link.arrived(ref.raw.at[above * 2 + pair], now.raw_sem + above * 2 + pair, above < n_row)
        if step < n_row - 1:
            raw_send(below, link.at(row=row + 1), (below >= 0) & (row < n_row - 1))
            raw_send(above, link.at(row=row - 1), (above < n_row) & (row > 0))
        raw_send(below, link.at(pair=sibling), below >= 0)
        raw_send(above, link.at(pair=sibling), above < n_row)

    coarse = ref.probs if n_group >= 8 and tokens >= 2 * channels else ref.coarse

    def coarse_taps():
        for copy in fetches:
            copy.wait()
        upper, lower = {0: (2,), 1: (1, 2)}, {0: (0, 1), 1: (0,)}
        for u in range(2):
            for line, row_taps in enumerate((upper[u], lower[u])):
                tall = []
                for b in range(3):
                    at = slice(b * channels, (b + 1) * channels)
                    tall.append(sum(ref.kernel2[a, at, :].astype(F32) for a in row_taps))
                for v in range(2):
                    for place_x, column_taps in enumerate((upper[v], lower[v])):
                        tile = sum(tall[b] for b in column_taps)
                        at = slice(place_x * channels, (place_x + 1) * channels)
                        coarse[u * 4 + v * 2 + line, 0:channels, at] = tile.astype(BF16)

    def back2():
        now.wait_pool_rows()
        now.wait_pool_columns()
        first_row = iota((half, channels), 0) == 0
        last_row = iota((half, channels), 0) == half - 1
        for i in range(low + 2):
            if i == 0:
                value, edge = ref.pool_up[...], ref.columns2[0, low - 1 : low, :]
            elif i == low + 1:
                value, edge = ref.pool_down[...], ref.columns2[2, 0:1, :]
            else:
                value, edge = ref.gpre[i - 1], ref.columns2[1, i - 1 : i, :]
            if i in (0, low + 1):
                value = (value.astype(F32) * 0.25 * math.sqrt(0.5)).astype(BF16)
            wide = value.astype(F32)
            left = jnp.where(first_row, edge * side, pltpu.roll(wide, 1, 0))
            right = jnp.where(last_row, edge * (1.0 - side), pltpu.roll(wide, half - 1, 0))
            ref.padded_g[i, :, 0:channels] = left.astype(BF16)
            ref.padded_g[i, :, channels : 2 * channels] = value
            ref.padded_g[i, :, 2 * channels : 3 * channels] = right.astype(BF16)
        for u in range(2):
            for v in range(2):
                value = 0.0
                for line in range(2):
                    rows = ref.padded_g[line : line + low + 1, :, v * channels : (v + 2) * channels]
                    taps = coarse[u * 4 + v * 2 + line, 0:channels, 0 : 2 * channels]
                    value = value + mm_t(rows.reshape((low + 1) * half, 2 * channels), taps)
                for i in range(low + 1):
                    ref.grad2[2 * i + 1 - u, v * half : (v + 1) * half, :] = value[i * half : (i + 1) * half]

    def norm1():
        now.wait_stats1()
        stats = slot_sum(ref.stats1)
        now.stats1 = stats
        now.count_land = lanes(stats[3:4, 0:128], channels)
        now.count_token = lanes(stats[3:4, 128:256], channels)
        mean, inv, now.size1 = norm_terms(
            stats[0:1, 0:c_in], stats[0:1, c_in:channels], now.count_land[:, 0:c_in], width1
        )
        now.inv1 = inv
        now.mean3, now.inv3, now.size3 = norm_terms(stats[1:2], stats[2:3], now.count_token, width2)
        gain, shift = ref.gain1[...], ref.shift1[...]

        def act1(value):
            normed = (value - mean) * inv
            affine = normed * gain + shift
            return normed, affine, sigmoid(affine)

        def edge_act(rows):
            _, affine, gate = act1(rows)
            return affine * gate

        now.wait_image_columns()
        ref.columns1[0] = edge_act(ref.columns1[0]) * has_up
        ref.columns1[1] = edge_act(ref.columns1[1])
        ref.columns1[2] = edge_act(ref.columns1[2]) * has_down

        def edge_row(y, edge, there):
            _, affine, gate = act1(ref.normed1[y])
            act = affine * gate * there
            write_shifted(ref.padded1, y, act[0:half], act[half:span], edge, c_in)

        def act1_row(y, carry):
            normed, affine, gate = act1(ref.normed1[y + 2])
            act = affine * gate
            ref.normed1[y + 2] = normed
            ref.slope1[y] = gate * (1.0 + affine * (1.0 - gate))
            write_shifted(ref.padded1, y + 2, act[0:half], act[half:span], ref.columns1[1, pl.ds(y, 1), :], c_in)
            return carry

        lax.fori_loop(0, height, act1_row, 0)
        now.wait_image_rows()
        for k in range(2):
            split_row(k, ref.image_up[k])
            split_row(height + 2 + k, ref.image_down[k])
        for k in range(2):
            edge_row(k, ref.columns1[0, height - 2 + k : height - 1 + k, :], has_up)
            edge_row(height + 2 + k, ref.columns1[2, k : k + 1, :], has_down)

    def conv1():
        now.wait_land_rows()
        ref.mask[0] = land_line(ref.land_up[height - 1 : height, :])
        ref.mask[height + 1] = land_line(ref.land_down[0:1, :])

        def conv1_row(y, carry):
            sums, squares = carry
            value = mm(ref.padded1[y], ref.kernel1[0])
            value = value + mm(ref.padded1[y + 1], ref.kernel1[1])
            value = value + mm(ref.padded1[y + 2], ref.kernel1[2])
            value = value + ref.bias1[...]
            ref.hidden[y] = value
            masked = value * wide_mask(y)
            keep = inner(y)
            return sums + fold(masked) * keep, squares + fold(masked * value) * keep

        sums, squares = lax.fori_loop(0, height + 2, conv1_row, (zero2, zero2))
        ref.stats2[slot, 0:1, :] = total(sums)
        ref.stats2[slot, 1:2, :] = total(squares)
        now.wait_stats2 = link.share(ref.stats2)

    def normalize(index):
        scale = now.inv3 * ref.gain3[...]
        value = ((ref.raw[index].astype(F32) - now.mean3) * scale + ref.shift3[...]).astype(BF16)
        ref.tokens[index] = value
        ref.tokens_t[index] = value.T

    def weights(k):
        return ref.mix_w[:, k * channels : (k + 1) * channels]

    def queries():
        now.wait_token()
        normalize(slot)
        ref.query[...] = (mm(ref.tokens[slot], weights(0)) + ref.mix_b[:, 0:channels]).astype(BF16)
        ref.query_t[...] = (mm_t(weights(1), ref.query[...]) * (factor * LOG2E)).astype(BF16)
        now.alive = (now.count_token > 0.0).astype(F32) * factor
        ref.query_k[...] = (mm_t(ref.query[...], weights(1)) * now.alive).astype(BF16)
        ref.grad_att[...] = mm_t(ref.gres[...], ref.out_w[...]).astype(BF16)
        ref.grad_t[...] = mm_t(weights(2), ref.grad_att[...])
        ref.mixed_t[...] = jnp.zeros((channels, tokens), F32)
        ref.top[...] = jnp.full((8, tokens), -3e38, F32)
        ref.norm[...] = jnp.zeros((8, tokens), F32)

    def attend_block(index):
        mask = lanes(token_mask(ref.flags[index, 0:rows_t]), tokens)
        scores = mm(ref.tokens[index], ref.query_t[...])
        scores = jnp.where(mask > 0.5, scores, MASKED * LOG2E)
        old = ref.top[0:1]
        new = jnp.max(scores.reshape(tokens // 8, 8, tokens), axis=0)
        new = jnp.maximum(old, jnp.max(new, axis=0, keepdims=True))
        probs = jnp.exp2(scores - new)
        low_probs = probs.astype(BF16)
        ref.probs[index] = low_probs
        ref.tops[index, 0:1] = new
        ref.top[0:1] = new
        shrink = jnp.exp2(old - new)
        ref.norm[0:1] = ref.norm[0:1] * shrink + total(fold(probs))
        ref.mixed_t[...] = ref.mixed_t[...] * shrink + mm(ref.tokens_t[index], low_probs)

    arrivals = arrival_order(n_row)

    def attend(position):
        block = pick([order[position] for order in arrivals], row)

        def body(lane, carry):
            index = block * 2 + jnp.where(lane == 0, pair, sibling)

            @pl.when(lane == 1)
            def _():
                link.arrived(ref.raw.at[index], now.raw_sem + index)

            if position == 0:

                @pl.when(lane == 1)
                def _():
                    normalize(index)
            else:
                normalize(index)
            attend_block(index)
            return carry

        lax.fori_loop(0, 2, body, 0)

    def film():
        lines = jnp.broadcast_to(ref.embedding[...], (8, ref.embedding.shape[-1]))
        value = mm(lines, ref.film_w[...])[0:1] + ref.film_b[...]
        now.film_scale = 1.0 + value[:, 0:channels]
        now.slope_m = ref.gain2[...] * now.film_scale
        now.shift_m = ref.shift2[...] * now.film_scale + value[:, channels:]

    def mid():
        now.wait_stats2()
        stats = slot_sum(ref.stats2)
        mean, inv, now.size2 = norm_terms(stats[0:1], stats[1:2], now.count_land, width2)
        now.inv2 = inv
        slope_m, shift_m = now.slope_m, now.shift_m

        def mid_row(y, carry):
            grad_sum, grad_dot = carry
            normed = (ref.hidden[y] - mean) * inv
            affine = normed * slope_m + shift_m
            gate = sigmoid(affine)
            act = affine * gate
            grad = ref.grad2[y] * (gate * (1.0 + affine * (1.0 - gate)))
            ref.hidden[y] = normed
            ref.grad2[y] = grad
            act = act * exists(y)
            write_shifted(ref.padded2, y, act[0:half], act[half:span], 0.0, channels)
            ref.column3[pl.ds(y, 1), :] = jnp.where(side > 0.5, act[0:1], act[span - 1 : span])
            keep = inner(y)
            return grad_sum + fold(grad) * keep, grad_dot + fold(grad * normed) * keep

        grad_sum, grad_dot = lax.fori_loop(0, height + 2, mid_row, (zero2, zero2))
        ref.stats3[slot, 0:1, :] = total(grad_sum)
        ref.stats3[slot, 1:2, :] = total(grad_dot)
        now.wait_stats3 = link.share(ref.stats3)
        now.wait_act_column = link.send_all([(ref.column3, ref.edge3, link.at(pair=sibling))], ref.edge3)

    def kernel2_grad():
        now.wait_act_column()
        set_edges(ref.padded2, ref.edge3)

        def box_row(i, carry):
            for a in range(3):
                value = 0.0
                for dy in range(2):
                    for side_x in range(2):
                        line = ref.padded2[2 * i + a + dy, side_x * half : (side_x + 1) * half, :]
                        value = value + line.astype(F32)
                at = a * (low // 2) + lax.div(i, 2)
                ref.padded3[at, pl.ds(lax.rem(i, 2) * half, half), :] = value.astype(BF16)
            return carry

        lax.fori_loop(0, low, box_row, 0)

        def body(a, carry):
            boxes = ref.padded3[pl.ds(a * (low // 2), low // 2)].reshape(low * half, 3 * channels)
            value = mm(ref.gpre_t[...], boxes).T
            put(ref.part_a, a * (rows_a // 3), rows_a, value)
            return carry

        lax.fori_loop(0, 3, body, 0)
        now.sum_a = link.all_sum(ref.part_a, ref.recv1_a, ref.recv2_a, ref.recv3_a, ref.sum_a)

    def hidden():
        now.wait_stats3()
        stats = slot_sum(ref.stats3)
        now.grad_sum2, now.grad_dot2 = stats[0:1], stats[1:2]
        slope_m, inv = now.slope_m, now.inv2
        grouped = group_total(jnp.concatenate([now.grad_sum2 * slope_m, now.grad_dot2 * slope_m], axis=0), width2)
        first, second = grouped[0:1] / now.size2, grouped[1:2] / now.size2

        def hidden_row(y, carry):
            normed = ref.hidden[y]
            grad = ref.grad2[y] * slope_m - wide_mask(y) * (first + normed * second)
            grad = (grad * (inv * exists(y))).astype(BF16)
            wide = grad.astype(F32)
            write_shifted(ref.padded3, y, wide[0:half], wide[half:span], 0.0, channels)
            ref.column4[pl.ds(y, 1), :] = jnp.where(side > 0.5, wide[0:1], wide[span - 1 : span])

            @pl.when((y > 0) & (y < height + 1))
            def _():
                ref.grad_hidden_t[y - 1] = grad.T

            return carry + fold(wide) * inner(y)

        now.bias1_sum = lax.fori_loop(0, height + 2, hidden_row, zero2)
        now.wait_hidden_column = link.send_all([(ref.column4, ref.edge4, link.at(pair=sibling))], ref.edge4)

    def image_boxes():
        for i in range(low):
            value = 0.0
            for dy in range(2):
                for side_x in range(2):
                    at = slice(side_x * half, (side_x + 1) * half)
                    value = value + ref.image_low[2 * i + dy, at, :].astype(F32)
            ref.image_box[i] = value.astype(BF16)
        value = mm(ref.gpre_t[...], ref.image_box[...].reshape(low * half, c_in)).T
        put(ref.part_c, 9 * c_in // 16, rows_c, value)

    def kernel1_grad():
        def body(a, carry):
            value = 0.0
            for y in range(height):
                value = value + mm(ref.grad_hidden_t[y], ref.padded1[a + y + 1])
            put(ref.part_c, a * (3 * c_in // 16), rows_c, value.T)
            return carry

        lax.fori_loop(0, 3, body, 0)
        now.sum_c = link.all_sum(ref.part_c, ref.recv1_c, ref.recv2_c, ref.recv3_c, ref.sum_c)

    def attended():
        norm = 1.0 / ref.norm[0:1]
        mixed_t = ref.mixed_t[...] * norm
        ref.mixed_t[...] = mixed_t
        grad_t = (ref.grad_t[...] * norm).astype(BF16)
        now.delta = total(grad_t.astype(F32) * mixed_t)
        ref.grad_low_t[...] = grad_t
        ref.grad_low[...] = grad_t.T
        ref.grad_query_t[...] = jnp.zeros((channels, tokens), F32)
        now.last_top = ref.top[0:1]
        now.sums3 = (zero2, zero2)
        now.pair_sem = link.new_recv(n_row)
        now.chain_sem = link.new_recv(2 * (n_row - 1))
        now.chain_send_sem = link.sends
        link.sends += n_row - 1

    def back_block(index, carry):
        grad_sum, grad_dot = carry
        probs = ref.probs[index].astype(F32) * jnp.exp2(ref.tops[index, 0:1] - now.last_top)
        grad = mm(ref.tokens[index], ref.grad_low_t[...])
        grad = (probs * (grad - now.delta)).astype(BF16)
        value = mm(grad, ref.query_k[...]) + mm(probs.astype(BF16), ref.grad_low[...])
        ref.grad_tokens[index] = value.astype(BF16)
        ref.grad_query_t[...] += mm(ref.tokens_t[index], grad)
        return grad_sum + fold(value), grad_dot + fold(value * ref.raw[index].astype(F32))

    orders = chain_order(n_row)

    def chain_at(position):
        target, up, index = (pick([order[position][k] for order in orders], row) for k in range(3))
        has_before = jnp.where(up == 1, row, n_row - 1 - row) > 0
        return target, up, index, has_before

    def back(position):
        target = row if position == n_row - 1 else chain_at(position)[0]

        def body(lane, carry):
            return back_block(target * 2 + jnp.where(lane == 0, sibling, pair), carry)

        now.sums3 = body(0, now.sums3)
        index = target * 2 + sibling
        link.send(ref.grad_tokens.at[index], ref.pair_grad.at[target], link.at(pair=sibling), now.pair_sem + target)
        now.sums3 = body(1, now.sums3)

    def chain_send(position, first):
        target, up, index, has_before = chain_at(position)
        source, device = ref.chip_grad.at[position], link.at(row=row + 2 * up - 1)
        send_sem = now.chain_send_sem + position

        @pl.when(jnp.logical_not(has_before) if first else has_before)
        def _():
            link.arrived(ref.pair_grad.at[target], now.pair_sem + target)
            own = ref.pair_grad[target].astype(F32) + ref.grad_tokens[target * 2 + pair].astype(F32)
            if not first:
                link.arrived(ref.chain_grad.at[index], now.chain_sem + index)
                own = own + ref.chain_grad[index].astype(F32)
            ref.chip_grad[position] = own.astype(BF16)
            link.copy(source, ref.chain_grad.at[index], device, send_sem, now.chain_sem + index).start()

        if not first:
            link.pending.append((lambda: link.copy(source, source, device, send_sem, 0), None))

    def mix_grads():
        grad_query_t = (ref.grad_query_t[...] * now.alive[0:1, 0:1]).astype(BF16)
        now.grad_query = mm(grad_query_t.T, weights(1)).astype(BF16)
        mixed_t = ref.mixed_t[...]
        now.attended = (mm(mixed_t.T.astype(BF16), weights(2)) + ref.mix_b[:, channels:]).astype(BF16)
        put(ref.part_b, 6 * rows_b, rows_b, mm(now.attended.T, ref.gres[...]))
        put(ref.part_b, 4 * rows_b, rows_b, mm(mixed_t.astype(BF16), ref.grad_att[...]))
        put(ref.part_b, 0, rows_b, mm(ref.tokens_t[slot], now.grad_query))
        put(ref.part_b, 2 * rows_b, rows_b, mm(grad_query_t, ref.query[...]))
        now.sum_b = link.all_sum(ref.part_b, ref.recv1_b, ref.recv2_b, ref.recv3_b, ref.sum_b)

    def result():
        update = mm(now.attended, ref.out_w[...]) + ref.out_b[...]
        raw = ref.features[...].astype(F32)
        value = raw + update
        ref.result[...] = value.astype(BF16)
        store("result")
        tmask2 = lanes(ref.token_mask[...], channels)
        now.update_sum = fold(update * update * tmask2)
        now.result_sum = fold(value * value * tmask2)
        own_grad = mm_t(now.grad_query, weights(0))
        ref.grad_own[...] = own_grad
        now.grad_sum3 = total(now.sums3[0] + fold(own_grad))
        now.grad_dot3 = total(now.sums3[1] + fold(own_grad * raw))

    def conv2():
        def conv2_rows(i, carry):
            branch_sum, stream_sum = carry
            pooled = 0.0
            for u in range(2):
                y = 2 * i + u
                branch = mm(ref.padded2[y], ref.kernel2[0])
                branch = branch + mm(ref.padded2[y + 1], ref.kernel2[1])
                branch = branch + mm(ref.padded2[y + 2], ref.kernel2[2])
                branch = branch + ref.bias2[...]
                stream = (branch + mm(ref.image_low[y], ref.skip_w[...]) + ref.skip_b[...]) * math.sqrt(0.5)
                mask = wide_mask(y + 1)
                branch_sum = branch_sum + fold(branch * branch * mask)
                stream_sum = stream_sum + fold(stream * stream * mask)
                pooled = pooled + stream[0:half] + stream[half:span]
            ref.pooled[i] = (pooled * 0.25).astype(BF16)
            return branch_sum, stream_sum

        now.branch_sum, now.stream_sum = lax.fori_loop(0, low, conv2_rows, (zero2, zero2))
        store("pooled")

    def taps1():
        for a in range(3):
            for b in range(3):
                at = slice((2 - b) * channels, (3 - b) * channels)
                ref.kernel1_t[2 - a, :, at] = ref.kernel1[a, b * c_in : (b + 1) * c_in, :]

    def back1():
        now.wait_hidden_column()
        set_edges(ref.padded3, ref.edge4)

        def back1_row(y, carry):
            grad_sum, grad_dot = carry
            value = mm_t(ref.padded3[y], ref.kernel1_t[0])
            value = value + mm_t(ref.padded3[y + 1], ref.kernel1_t[1])
            value = value + mm_t(ref.padded3[y + 2], ref.kernel1_t[2])
            value = value * ref.slope1[y]
            ref.slope1[y] = value
            return grad_sum + fold(value), grad_dot + fold(value * ref.normed1[y + 2])

        now.grad_sum1, now.grad_dot1 = lax.fori_loop(0, height, back1_row, (zero1, zero1))

    def last_share():
        ref.stats4[slot, 11:12, 0:c_in] = total(now.grad_dot1)
        ref.stats4[slot, 11:12, c_in:channels] = total(now.grad_sum1)
        for index, value in enumerate((
            now.grad_sum3,
            (now.grad_dot3 - now.mean3 * now.grad_sum3) * now.inv3,
            total(now.bias1_sum),
            4.0 * total(now.gpre_sum),
            total(fold(ref.gres[...].astype(F32))),
            total(fold(now.grad_query.astype(F32))),
            total(fold(ref.grad_att[...].astype(F32))),
            total(now.branch_sum),
            total(now.stream_sum),
            total(now.update_sum),
            total(now.result_sum),
        )):
            ref.stats4[slot, index : index + 1, :] = value
        now.wait_stats4 = link.share(ref.stats4)

    def last_sums():
        now.wait_stats4()
        stats = slot_sum(ref.stats4)
        now.stats4 = stats
        ref.vectors[item, 0:12, :] = stats
        ref.vectors[item, 12:13, :] = now.grad_dot2 * now.film_scale
        ref.vectors[item, 13:14, :] = now.grad_sum2 * now.film_scale
        ref.vectors[item, 14:15, :] = now.grad_dot2 * ref.gain2[...] + now.grad_sum2 * ref.shift2[...]
        ref.vectors[item, 15:16, :] = now.grad_sum2
        ref.vectors[item, 16:17, :] = ref.embedding[:, 0:channels].astype(F32)
        ref.vectors[item, 17:18, :] = ref.embedding[:, channels : 2 * channels].astype(F32)
        ref.vectors[item, 18:19, :] = now.stats1[0:1]
        ref.vectors[item, 19:20, :] = now.stats1[3:4]
        mine = ref.vectors.at[item]
        now.wait_vectors = link.send_all(
            [(mine, mine, device) for _, device in link.others_in_item()], ref.vectors.at[pl.ds(0, n_item - 1)]
        )

    def image_grad():
        stats = now.stats4
        gain, inv = ref.gain1[...], now.inv1
        grad_sum, grad_dot = stats[11:12, c_in:channels], stats[11:12, 0:c_in]
        grouped = group_total(jnp.concatenate([grad_sum * gain, grad_dot * gain], axis=0), width1)
        first, second = grouped[0:1] / now.size1, grouped[1:2] / now.size1

        def body(i, carry):
            skip = mm_t(ref.gpre[i], ref.skip_w[...])
            skip = jnp.concatenate([skip, skip], axis=0)
            for u in range(2):
                y = 2 * i + u
                value = ref.slope1[y] * gain - ref.mask[y + 1] * (first + ref.normed1[y + 2] * second)
                value = value * inv + skip
                ref.line[pl.ds(0, half, stride=2), :] = value[0:half]
                ref.line[pl.ds(1, half, stride=2), :] = value[half:span]
                ref.image_grad[y] = ref.line[...].astype(BF16)
            return carry

        lax.fori_loop(0, low, body, 0)
        store("image_grad")

    def features_grad():
        last = n_row - 1
        link.arrived(ref.pair_grad.at[row], now.pair_sem + row)
        ref.grad_own[...] += ref.pair_grad[row].astype(F32) + ref.grad_tokens[slot].astype(F32)
        for index, there in ((last - row, row > 0), (last + row, row < last)):

            @pl.when(there)
            def _(index=index):
                link.arrived(ref.chain_grad.at[index], now.chain_sem + index)
                ref.grad_own[...] += ref.chain_grad[index].astype(F32)

        stats, gain = now.stats4, ref.gain3[...]
        grouped = group_total(jnp.concatenate([stats[0:1] * gain, stats[1:2] * gain], axis=0), width2)
        first, second = grouped[0:1] / now.size3, grouped[1:2] / now.size3
        normed = (ref.features[...].astype(F32) - now.mean3) * now.inv3
        value = ref.grad_own[...] * gain - lanes(ref.token_mask[...], channels) * (first + normed * second)
        ref.features_grad[...] = (ref.gres[...].astype(F32) + value * now.inv3).astype(BF16)
        store("features_grad")

    def step(name):
        stage = getattr(now, name)
        setattr(now, name, stage() if stage is not None else None)

    def step_a():
        step("sum_a")

    def step_b():
        step("sum_b")

    def step_c():
        step("sum_c")

    met = link.greet()
    local()
    met()
    first_sends()
    coarse_taps()
    back2()
    norm1()
    conv1()
    raw_step(1)
    queries()
    film()
    attend(0)
    mid()
    for k in range(2, min(3, n_row)): raw_step(k)
    kernel2_grad()
    taps1()
    step_a()
    hidden()
    attend(1)
    image_boxes()
    kernel1_grad()
    for k in range(3, n_row): raw_step(k)
    for k in range(2, min(3, n_row)): attend(k)
    step_c()
    for k in range(3, n_row): attend(k)
    step_a()
    attended()
    back(0)
    back(1)
    chain_send(0, True)
    step_a()
    for k in range(2, n_row - 1): (back(k), chain_send(k - 1, True))
    back(n_row - 1)
    step_c()
    mix_grads()
    chain_send(n_row - 2, True)
    result()
    step_b()
    chain_send(0, False)
    conv2()
    step_a()
    step_b()
    back1()
    for k in range(1, min(2, n_row - 1)): chain_send(k, False)
    step_c()
    last_share()
    step_a()
    step_b()
    for k in range(2, n_row - 1): chain_send(k, False)
    step_c()
    last_sums()
    step_b()
    image_grad()
    step_c()
    step_b()
    features_grad()
    steps = [now.sum_a, now.sum_c, now.sum_b, now.wait_vectors]
    while steps:
        steps = [stage() for stage in steps if stage is not None]
    for name in ("sum_a", "sum_b", "sum_c", "vectors"):
        store(name)
    link.finish()
    for copy in stores:
        copy.wait()
    assert link.sends <= ref.send_sem.shape[0] and link.recvs <= ref.recv_sem.shape[0], (link.sends, link.recvs)


class Scratch(NamedTuple):
    send_sem: Any
    recv_sem: Any
    flags: Any
    raw: Any
    image_up: Any
    image_down: Any
    land_up: Any
    land_down: Any
    pool_up: Any
    pool_down: Any
    mask: Any
    token_mask: Any
    line: Any
    normed1: Any
    image_low: Any
    column1: Any
    columns1: Any
    stats1: Any
    gpre: Any
    gpre_t: Any
    column2: Any
    columns2: Any
    coarse: Any
    padded_g: Any
    grad2: Any
    slope1: Any
    padded1: Any
    hidden: Any
    stats2: Any
    tokens: Any
    tokens_t: Any
    query: Any
    query_t: Any
    query_k: Any
    grad_att: Any
    grad_t: Any
    column3: Any
    edge3: Any
    stats3: Any
    kernel1_t: Any
    grad_hidden_t: Any
    column4: Any
    edge4: Any
    padded2: Any
    image_box: Any
    part_a: Any
    recv1_a: Any
    recv2_a: Any
    recv3_a: Any
    part_b: Any
    recv1_b: Any
    recv2_b: Any
    recv3_b: Any
    part_c: Any
    recv1_c: Any
    recv2_c: Any
    recv3_c: Any
    padded3: Any
    stats4: Any
    top: Any
    tops: Any
    norm: Any
    probs: Any
    mixed_t: Any
    grad_low_t: Any
    grad_low: Any
    grad_query_t: Any
    grad_tokens: Any
    pair_grad: Any
    chip_grad: Any
    chain_grad: Any
    grad_own: Any
    local_sem: Any


SCRATCH = Scratch._fields + tuple(name + "_in" for name in FETCHED) + tuple(name + "_out" for name in RESULTS)


class LastOut(NamedTuple):
    gain1: Any
    shift1: Any
    kernel1: Any
    bias1: Any
    film_w: Any
    film_b: Any
    gain2: Any
    shift2: Any
    kernel2: Any
    bias2: Any
    skip_w: Any
    skip_b: Any
    gain3: Any
    shift3: Any
    mix_w: Any
    mix_b: Any
    out_w: Any
    out_b: Any
    rms: Any


LAST_OUT = LastOut._fields
LAST_BIG = ("kernel1", "film_w", "kernel2", "skip_w", "mix_w", "out_w")


def last_kernel(n_item, *refs):
    count = len(RESULTS)
    source = dict(zip(RESULTS, refs))
    target = dict(zip(RESULTS[:4] + LAST_OUT, refs[count:]))
    rest = refs[count + 4 + len(LAST_OUT) :]
    held = dict(zip(RESULTS + LAST_BIG, rest))
    in_sem, out_sem = rest[count + len(LAST_BIG) :]
    arrivals = {}
    for index, name in enumerate(("vectors", "sum_c", "sum_b", "sum_a") + RESULTS[:4]):
        arrivals[name] = pltpu.make_async_copy(source[name], held[name], in_sem.at[index])
        arrivals[name].start()
    leaving = []

    def leave(name):
        copy = pltpu.make_async_copy(held[name], target[name], out_sem.at[len(leaving)])
        copy.start()
        leaving.append(copy)

    o = SimpleNamespace(**target)
    channels, c_in = o.bias1.shape[-1], o.gain1.shape[-1]

    arrivals["vectors"].wait()
    vectors = held["vectors"]
    value = vectors[0]
    for item in range(1, n_item):
        value = value + vectors[item]
    o.shift3[...] = value[0:1]
    o.gain3[...] = value[1:2]
    o.bias1[...] = value[2:3]
    o.bias2[...] = value[3:4]
    o.skip_b[...] = value[3:4]
    o.out_b[...] = value[4:5]
    o.mix_b[:, 0:channels] = value[5:6]
    o.mix_b[:, channels:] = value[6:7]
    o.gain1[...] = value[11:12, 0:c_in]
    o.shift1[...] = value[11:12, c_in:channels]
    o.gain2[...] = value[12:13]
    o.shift2[...] = value[13:14]
    o.film_b[:, 0:channels] = value[14:15]
    o.film_b[:, channels:] = value[15:16]
    pad = jnp.zeros((8 - n_item, 2 * channels), F32)

    def stacked(first):
        rows = [
            jnp.concatenate([vectors[i, first : first + 1, :], vectors[i, first + 1 : first + 2, :]], axis=1)
            for i in range(n_item)
        ]
        return jnp.concatenate(rows + [pad], axis=0)

    held["film_w"][...] = lax.dot_general(
        stacked(16), stacked(14), (((0,), (0,)), ((), ())), precision=HIGHEST, preferred_element_type=F32
    )
    leave("film_w")

    def lane_sum(row):
        return jnp.sum(row, axis=1, keepdims=True)

    land = jnp.maximum(value[19:20, 0:1], 1.0)
    token = jnp.maximum(value[19:20, 128:129], 1.0)
    place = iota((1, 5), 1)
    rms = jnp.zeros((1, 5), F32)
    for index, (square, size) in enumerate((
        (lane_sum(value[18:19, c_in:channels]), land * c_in),
        (lane_sum(value[7:8]), land * channels),
        (lane_sum(value[8:9]), land * channels),
        (lane_sum(value[9:10]), token * channels),
        (lane_sum(value[10:11]), token * channels),
    )):
        rms = jnp.where(place == index, jnp.sqrt(square / size), rms)
    o.rms[...] = rms

    def widen(name, blocks, start, stride):
        rows, width = held[name].shape
        for lane in range(width // 128):
            first = start + lane * stride
            piece = held[blocks][first : first + rows // 16].reshape(rows, 128)
            held[name][:, lane * 128 : (lane + 1) * 128] = piece.astype(F32)
        leave(name)

    rows_a, rows_b, rows_c, rows_k = 9 * channels // 16, channels // 16, 10 * c_in // 16, 9 * c_in // 16
    arrivals["sum_c"].wait()
    widen("kernel1", "sum_c", 0, rows_c)
    widen("skip_w", "sum_c", rows_k, rows_c)
    arrivals["sum_b"].wait()
    widen("mix_w", "sum_b", 0, rows_b)
    widen("out_w", "sum_b", 3 * (channels // 128) * rows_b, rows_b)
    arrivals["sum_a"].wait()
    widen("kernel2", "sum_a", 0, rows_a)
    for name in RESULTS[:4]:
        arrivals[name].wait()
        leave(name)
    for copy in leaving:
        copy.wait()


def on_device(mesh_shape, *args):
    names = INPUTS
    arg = SimpleNamespace(**dict(zip(names, args)))
    n_item, n_row = mesh_shape["item"], mesh_shape["row"]
    n_group = 2 * n_row
    _, height, span, c_in = arg.image.shape
    channels = arg.bias1.shape[-1]
    _, rows_t, cols_t, _ = arg.features.shape
    tokens = rows_t * cols_t
    low, half = height // 2, span // 2
    inputs = [
        arg.image.reshape(height, span, c_in),
        arg.land_mask.reshape(height, span) if hasattr(arg, "land_mask") else arg.land.reshape(height, span),
        arg.embedding,
        arg.gain1.reshape(1, c_in),
        arg.shift1.reshape(1, c_in),
        arg.kernel1.reshape(3, 3 * c_in, channels),
        arg.bias1.reshape(1, channels),
        arg.film_w,
        arg.film_b.reshape(1, 2 * channels),
        arg.gain2.reshape(1, channels),
        arg.shift2.reshape(1, channels),
        arg.kernel2.reshape(3, 3 * channels, channels),
        arg.bias2.reshape(1, channels),
        arg.skip_w,
        arg.skip_b.reshape(1, channels),
        arg.features.reshape(tokens, channels),
        arg.token.reshape(rows_t, cols_t),
        arg.gain3.reshape(1, channels),
        arg.shift3.reshape(1, channels),
        arg.mix_w,
        arg.mix_b.reshape(1, 2 * channels),
        arg.out_w,
        arg.out_b.reshape(1, channels),
        arg.gpool.reshape(low, half, channels),
        arg.gres.reshape(tokens, channels),
    ]
    share = 2 * n_item * n_row
    blocks_a = -(-9 * channels * channels // 2048 // share) * share
    blocks_b = -(-4 * channels * channels // 2048 // share) * share
    blocks_c = -(-10 * c_in * channels // 2048 // share) * share
    vmem = pltpu.VMEM

    def sums(blocks):
        unit = blocks // 2 // n_item
        return [
            vmem((blocks, 16, 128), BF16),
            vmem((blocks // 2, 16, 128), BF16),
            vmem((n_item - 1, unit, 16, 128), BF16),
            vmem((n_row - 1, unit // n_row, 16, 128), BF16),
        ]

    scratch = [
        pltpu.SemaphoreType.DMA((52 + 6 * n_row,)),
        pltpu.SemaphoreType.DMA((44 + 5 * n_row,)),
        vmem((n_group, -(-rows_t // 16) * 16, cols_t), BF16),
        vmem((n_group, tokens, channels), BF16),
        vmem((2, span, c_in), BF16),
        vmem((2, span, c_in), BF16),
        vmem((height, span), jnp.int32),
        vmem((height, span), jnp.int32),
        vmem((half, channels), BF16),
        vmem((half, channels), BF16),
        vmem((height + 2, span, 128), F32),
        vmem((tokens, 128), F32),
        vmem((span, c_in), F32),
        vmem((height + 4, span, c_in), F32),
        vmem((height, span, c_in), BF16),
        vmem((8, c_in), F32),
        vmem((3, 8, c_in), F32),
        vmem((n_group, 4, channels), F32),
        vmem((low, half, channels), BF16),
        vmem((channels, low * half), BF16),
        vmem((8, channels), F32),
        vmem((3, 8, channels), F32),
        vmem((8, channels, 2 * channels) if n_group < 8 or tokens < 2 * channels else (8, 16, 128), BF16),
        vmem((low + 2, half, 3 * channels), BF16),
        vmem((height + 2, span, channels), F32),
        vmem((height, span, c_in), F32),
        vmem((height + 4, span, 3 * c_in), BF16),
        vmem((height + 2, span, channels), F32),
        vmem((n_group, 2, channels), F32),
        vmem((n_group, tokens, channels), BF16),
        vmem((n_group, channels, tokens), BF16),
        vmem((tokens, channels), BF16),
        vmem((channels, tokens), BF16),
        vmem((tokens, channels), BF16),
        vmem((tokens, channels), BF16),
        vmem((channels, tokens), F32),
        vmem((16, channels), F32),
        vmem((16, channels), F32),
        vmem((n_group, 2, channels), F32),
        vmem((3, c_in, 3 * channels), BF16),
        vmem((height, channels, span), BF16),
        vmem((16, channels), F32),
        vmem((16, channels), F32),
        vmem((height + 2, span, 3 * channels), BF16),
        vmem((low, half, c_in), BF16),
        *sums(blocks_a),
        *sums(blocks_b),
        *sums(blocks_c),
        vmem((height + 2, span, 3 * channels), BF16),
        vmem((n_group, 12, channels), F32),
        vmem((8, tokens), F32),
        vmem((n_group, 8, tokens), F32),
        vmem((8, tokens), F32),
        vmem((n_group, tokens, tokens), BF16),
        vmem((channels, tokens), F32),
        vmem((channels, tokens), BF16),
        vmem((tokens, channels), BF16),
        vmem((channels, tokens), F32),
        vmem((n_group, tokens, channels), BF16),
        vmem((n_row, tokens, channels), BF16),
        vmem((n_row - 1, tokens, channels), BF16),
        vmem((2 * (n_row - 1), tokens, channels), BF16),
        vmem((tokens, channels), F32),
        pltpu.SemaphoreType.DMA((len(FETCHED) + len(RESULTS),)),
        *[vmem(inputs[INPUTS.index(name)].shape, BF16) for name in FETCHED],
    ]
    shape = jax.ShapeDtypeStruct
    mid = [
        shape((low, half, channels), BF16),
        shape((tokens, channels), BF16),
        shape((height, span, c_in), BF16),
        shape((tokens, channels), BF16),
        shape((blocks_a, 16, 128), BF16),
        shape((blocks_b, 16, 128), BF16),
        shape((blocks_c, 16, 128), BF16),
        shape((n_item, 20, channels), F32),
    ]
    scratch += [vmem(out.shape, out.dtype) for out in mid]
    in_vmem, anywhere = pl.BlockSpec(memory_space=vmem), pl.BlockSpec(memory_space=pl.ANY)
    parts = pl.pallas_call(
        functools.partial(main_kernel, n_item, n_row),
        out_shape=mid,
        in_specs=[anywhere if name in FETCHED else in_vmem for name in INPUTS],
        out_specs=[anywhere] * len(mid),
        scratch_shapes=scratch,
        compiler_params=pltpu.CompilerParams(
            collective_id=0, has_side_effects=True, vmem_limit_bytes=int(63.9 * 1024 * 1024)
        ),
    )(*inputs)
    emb = arg.embedding.shape[-1]
    final = [
        *mid[:4],
        shape((1, c_in), F32),
        shape((1, c_in), F32),
        shape((9 * c_in, channels), F32),
        shape((1, channels), F32),
        shape((emb, 2 * channels), F32),
        shape((1, 2 * channels), F32),
        shape((1, channels), F32),
        shape((1, channels), F32),
        shape((9 * channels, channels), F32),
        shape((1, channels), F32),
        shape((c_in, channels), F32),
        shape((1, channels), F32),
        shape((1, channels), F32),
        shape((1, channels), F32),
        shape((channels, 3 * channels), F32),
        shape((1, 2 * channels), F32),
        shape((channels, channels), F32),
        shape((1, channels), F32),
        shape((1, 5), F32),
    ]
    outs = pl.pallas_call(
        functools.partial(last_kernel, n_item),
        out_shape=final,
        in_specs=[anywhere] * len(mid),
        out_specs=[anywhere] * 4 + [anywhere if name in LAST_BIG else in_vmem for name in LAST_OUT],
        scratch_shapes=[
            *[vmem(out.shape, out.dtype) for out in mid],
            *[vmem(final[4 + LAST_OUT.index(name)].shape, F32) for name in LAST_BIG],
            pltpu.SemaphoreType.DMA((len(mid),)),
            pltpu.SemaphoreType.DMA((4 + len(LAST_BIG),)),
        ],
        compiler_params=pltpu.CompilerParams(vmem_limit_bytes=int(63.9 * 1024 * 1024)),
    )(*parts)
    shapes = (
        (1, low, half, channels),
        (1, rows_t, cols_t, channels),
        (1, height, span, c_in),
        (1, rows_t, cols_t, channels),
        (c_in,),
        (c_in,),
        (3, 3, c_in, channels),
        (channels,),
        (emb, 2 * channels),
        (2 * channels,),
        (channels,),
        (channels,),
        (3, 3, channels, channels),
        (channels,),
        (c_in, channels),
        (channels,),
        (channels,),
        (channels,),
        (channels, 3 * channels),
        (2 * channels,),
        (channels, channels),
        (channels,),
        (5,),
    )
    return tuple(out.reshape(to) for out, to in zip(outs, shapes))


def solution(mesh):
    tiled = P("item", "row", "pair", None)
    mask = P("item", "row", "pair")
    in_specs = [P()] * len(INPUTS)
    for name in ("image", "features", "gpool", "gres"):
        in_specs[INPUTS.index(name)] = tiled
    for name in ("land", "token"):
        in_specs[INPUTS.index(name)] = mask
    in_specs[INPUTS.index("embedding")] = P("item", None)
    return jax.shard_map(
        functools.partial(on_device, dict(mesh.shape)),
        mesh=mesh,
        in_specs=tuple(in_specs),
        out_specs=(tiled,) * 4 + (P(),) * 19,
        check_vma=False,
    )
```

time: 114 us -> 92.7 us (0.81)
  the two profiles are of different devices: /device:TPU:0 before, /device:TPU:27 now
where the time goes in v2:
time: 92.7 us; the launch traced here: 92.6 us
  Pallas kernels  91.7 us (99%)
    pallas_call x1, Pallas kernels, on_device(): pl.pallas_call(functools.partial(main_kernel, n_item, n_row), out_shape=m...  86 us
    pallas_call x1, Pallas kernels, on_device(): pl.pallas_call(functools.partial(last_kernel, n_item), out_shape=final, i...  5.71 us

profile of v2, /device:TPU:27, one launch (start us, length us, event | category | flops | bytes accessed | tf_op | source)
XLA Modules:
  0.0 92.6 jit_solution(11826245492859484114)
XLA Ops:
  0.7 86.0 %shard_map.416 = (bf16[4,128,256]{2,1,0:T(8,128)(2,1)}, bf16[512,256]{1,0:T(8,128)(2,1)}, bf16[8,256,128]{2,1,0:T(8,128)(2,1)}, bf16[512,256]{1,0:T(8,128)(2,1)}...) custom-call(bf16[8,256,128]{2,1,0:T(8,128)(2,1)} %bitcast.41, ...), custom_call_target="tpu_custom_call" | custom-call | tf_op jit(solution)/shard_map/pallas_call | solution.py:1432
  86.7 5.7 %shard_map.417 = (bf16[4,128,256]{2,1,0:T(8,128)(2,1)}, bf16[512,256]{1,0:T(8,128)(2,1)}, bf16[8,256,128]{2,1,0:T(8,128)(2,1)}, bf16[512,256]{1,0:T(8,128)(2,1)}...) custom-call(bf16[4,128,256]{2,1,0:T(8,128)(2,1)} %get-tuple-element., ...), custom_call_target="tpu_custom_call" | custom-call | tf_op jit(solution)/shard_map/pallas_call | solution.py:1465

commit v3 on v2

--- a/solution.py
+++ b/solution.py
@@ -308,16 +308,6 @@
     return mean, lax.rsqrt(grouped[1:2] / size - mean * mean + EPS), size
 
 
-def chain_order(n_row):
-    orders = []
-    for row in range(n_row):
-        steps = [(row + s, 0, n_row - 1 - s, s) for s in range(n_row - 1) if n_row - 1 - s > row]
-        steps += [(n_row - 1 - row + s, 1, s, s) for s in range(n_row - 1) if s < row]
-        steps.sort()
-        orders.append([(target, 1 - down, down * (n_row - 1) + s) for _, down, target, s in steps])
-    return orders
-
-
 def arrival_order(n_row):
     orders = []
     for row in range(n_row):
@@ -493,9 +483,38 @@
         ref.flags[slot, 0:rows_t] = ref.token[...].astype(F32).astype(BF16)
         ref.raw[slot] = ref.features[...]
 
-    def raw_send(block, device, when=None):
-        index = block * 2 + pair
-        link.send(ref.raw.at[index], ref.raw.at[index], device, now.raw_sem + index, when)
+    class Gather:
+        def __init__(self, slots):
+            self.slots, self.base = slots, link.new_recv(n_group)
+            self.pass_on(row, True, row < n_row - 1, row > 0)
+            self.across(row)
+
+        def send(self, block, device, when=None):
+            index = block * 2 + pair
+            link.send(self.slots.at[index], self.slots.at[index], device, self.base + index, when)
+
+        def pass_on(self, block, there, up, down):
+            if up is not None:
+                self.send(block, link.at(row=row + 1), there & up)
+            if down is not None:
+                self.send(block, link.at(row=row - 1), there & down)
+
+        def across(self, block, there=None):
+            self.send(block, link.at(pair=sibling), there)
+
+        def step(self, step):
+            below, above = row - step, row + step
+            for block, there in ((below, below >= 0), (above, above < n_row)):
+                index = block * 2 + pair
+                link.arrived(self.slots.at[index], self.base + index, there)
+            if step < n_row - 1:
+                self.pass_on(below, below >= 0, row < n_row - 1, None)
+                self.pass_on(above, above < n_row, None, row > 0)
+            self.across(below, below >= 0)
+            self.across(above, above < n_row)
+
+        def from_sibling(self, index):
+            link.arrived(self.slots.at[index], self.base + index)
 
     def first_sends():
         now.wait_stats1 = link.share(ref.stats1)
@@ -507,20 +526,17 @@
         )
         now.wait_land_rows = link.edge_rows(ref.land, ref.land, ref.land_up, ref.land_down)
         now.wait_token = link.share(ref.flags)
-        now.raw_sem = link.new_recv(n_group)
-        raw_send(row, link.at(row=row + 1), row < n_row - 1)
-        raw_send(row, link.at(row=row - 1), row > 0)
-        raw_send(row, link.at(pair=sibling))
+        now.raw = Gather(ref.raw)
 
     def raw_step(step):
-        below, above = row - step, row + step
-        link.arrived(ref.raw.at[below * 2 + pair], now.raw_sem + below * 2 + pair, below >= 0)
-        link.arrived(ref.raw.at[above * 2 + pair], now.raw_sem + above * 2 + pair, above < n_row)
-        if step < n_row - 1:
-            raw_send(below, link.at(row=row + 1), (below >= 0) & (row < n_row - 1))
-            raw_send(above, link.at(row=row - 1), (above < n_row) & (row > 0))
-        raw_send(below, link.at(pair=sibling), below >= 0)
-        raw_send(above, link.at(pair=sibling), above < n_row)
+        now.raw.step(step)
+
+    def gres_first():
+        ref.gres_all[slot] = ref.gres[...]
+        now.gres = Gather(ref.gres_all)
+
+    def gres_step(step):
+        now.gres.step(step)
 
     coarse = ref.probs if n_group >= 8 and tokens >= 2 * channels else ref.coarse
 
@@ -652,55 +668,56 @@
     def queries():
         now.wait_token()
         normalize(slot)
-        ref.query[...] = (mm(ref.tokens[slot], weights(0)) + ref.mix_b[:, 0:channels]).astype(BF16)
+        mine = ref.tokens[slot]
+        now.alive = (now.count_token > 0.0).astype(F32) * factor
+        query_of(slot, ref.query)
         ref.query_t[...] = (mm_t(weights(1), ref.query[...]) * (factor * LOG2E)).astype(BF16)
-        now.alive = (now.count_token > 0.0).astype(F32) * factor
-        ref.query_k[...] = (mm_t(ref.query[...], weights(1)) * now.alive).astype(BF16)
+        ref.mix_vo[...] = mm(weights(2), ref.out_w[...]).astype(BF16)
+        ref.key[...] = (mm(mine, weights(1)) * (factor * LOG2E)).astype(BF16)
+        ref.value[...] = mm(mine, ref.mix_vo[...]).astype(BF16)
         ref.grad_att[...] = mm_t(ref.gres[...], ref.out_w[...]).astype(BF16)
-        ref.grad_t[...] = mm_t(weights(2), ref.grad_att[...])
+        ref.grad_low_t[...] = mm_t(ref.mix_vo[...], ref.gres[...]).astype(BF16)
         ref.mixed_t[...] = jnp.zeros((channels, tokens), F32)
         ref.top[...] = jnp.full((8, tokens), -3e38, F32)
         ref.norm[...] = jnp.zeros((8, tokens), F32)
 
-    def attend_block(index):
-        mask = lanes(token_mask(ref.flags[index, 0:rows_t]), tokens)
-        scores = mm(ref.tokens[index], ref.query_t[...])
-        scores = jnp.where(mask > 0.5, scores, MASKED * LOG2E)
-        old = ref.top[0:1]
-        new = jnp.max(scores.reshape(tokens // 8, 8, tokens), axis=0)
-        new = jnp.maximum(old, jnp.max(new, axis=0, keepdims=True))
-        probs = jnp.exp2(scores - new)
-        low_probs = probs.astype(BF16)
-        ref.probs[index] = low_probs
-        ref.tops[index, 0:1] = new
+    def query_of(index, target):
+        target[...] = (mm(ref.tokens[index], weights(0)) + ref.mix_b[:, 0:channels]).astype(BF16)
+
+    arrivals = arrival_order(n_row)
+
+    def blocks_at(position):
+        block = pick([order[position] for order in arrivals], row)
+        return block * 2 + pair, block * 2 + sibling
+
+    def attend(position):
+        blocks = blocks_at(position)
+        if position > 0:
+            normalize(blocks[0])
+        now.raw.from_sibling(blocks[1])
+        normalize(blocks[1])
+        old = new = ref.top[0:1]
+        scores = []
+        for index in blocks:
+            mask = lanes(token_mask(ref.flags[index, 0:rows_t]), tokens)
+            score = mm(ref.tokens[index], ref.query_t[...])
+            score = jnp.where(mask > 0.5, score, MASKED * LOG2E)
+            best = jnp.max(score.reshape(tokens // 8, 8, tokens), axis=0)
+            new = jnp.maximum(new, jnp.max(best, axis=0, keepdims=True))
+            scores.append(score)
+        shrink = jnp.exp2(old - new)
+        norm = ref.norm[0:1] * shrink
+        mixed = ref.mixed_t[...] * shrink
+        for index, score in zip(blocks, scores):
+            probs = jnp.exp2(score - new)
+            low_probs = probs.astype(BF16)
+            ref.probs[index] = low_probs
+            ref.tops[index, 0:1] = new
+            norm = norm + total(fold(probs))
+            mixed = mixed + mm(ref.tokens_t[index], low_probs)
         ref.top[0:1] = new
-        shrink = jnp.exp2(old - new)
-        ref.norm[0:1] = ref.norm[0:1] * shrink + total(fold(probs))
-        ref.mixed_t[...] = ref.mixed_t[...] * shrink + mm(ref.tokens_t[index], low_probs)
-
-    arrivals = arrival_order(n_row)
-
-    def attend(position):
-        block = pick([order[position] for order in arrivals], row)
-
-        def body(lane, carry):
-            index = block * 2 + jnp.where(lane == 0, pair, sibling)
-
-            @pl.when(lane == 1)
-            def _():
-                link.arrived(ref.raw.at[index], now.raw_sem + index)
-
-            if position == 0:
-
-                @pl.when(lane == 1)
-                def _():
-                    normalize(index)
-            else:
-                normalize(index)
-            attend_block(index)
-            return carry
-
-        lax.fori_loop(0, 2, body, 0)
+        ref.norm[0:1] = norm
+        ref.mixed_t[...] = mixed
 
     def film():
         lines = jnp.broadcast_to(ref.embedding[...], (8, ref.embedding.shape[-1]))
@@ -814,63 +831,48 @@
         norm = 1.0 / ref.norm[0:1]
         mixed_t = ref.mixed_t[...] * norm
         ref.mixed_t[...] = mixed_t
-        grad_t = (ref.grad_t[...] * norm).astype(BF16)
-        now.delta = total(grad_t.astype(F32) * mixed_t)
-        ref.grad_low_t[...] = grad_t
-        ref.grad_low[...] = grad_t.T
+        ref.query_stats[slot, 0:1] = ref.top[0:1]
+        ref.query_stats[slot, 1:2] = norm
+        ref.query_stats[slot, 2:3] = total(ref.grad_low_t[...].astype(F32) * mixed_t)
         ref.grad_query_t[...] = jnp.zeros((channels, tokens), F32)
-        now.last_top = ref.top[0:1]
-        now.sums3 = (zero2, zero2)
-        now.pair_sem = link.new_recv(n_row)
-        now.chain_sem = link.new_recv(2 * (n_row - 1))
-        now.chain_send_sem = link.sends
-        link.sends += n_row - 1
-
-    def back_block(index, carry):
-        grad_sum, grad_dot = carry
-        probs = ref.probs[index].astype(F32) * jnp.exp2(ref.tops[index, 0:1] - now.last_top)
-        grad = mm(ref.tokens[index], ref.grad_low_t[...])
-        grad = (probs * (grad - now.delta)).astype(BF16)
-        value = mm(grad, ref.query_k[...]) + mm(probs.astype(BF16), ref.grad_low[...])
-        ref.grad_tokens[index] = value.astype(BF16)
-        ref.grad_query_t[...] += mm(ref.tokens_t[index], grad)
-        return grad_sum + fold(value), grad_dot + fold(value * ref.raw[index].astype(F32))
-
-    orders = chain_order(n_row)
-
-    def chain_at(position):
-        target, up, index = (pick([order[position][k] for order in orders], row) for k in range(3))
-        has_before = jnp.where(up == 1, row, n_row - 1 - row) > 0
-        return target, up, index, has_before
-
-    def back(position):
-        target = row if position == n_row - 1 else chain_at(position)[0]
-
-        def body(lane, carry):
-            return back_block(target * 2 + jnp.where(lane == 0, sibling, pair), carry)
-
-        now.sums3 = body(0, now.sums3)
-        index = target * 2 + sibling
-        link.send(ref.grad_tokens.at[index], ref.pair_grad.at[target], link.at(pair=sibling), now.pair_sem + target)
-        now.sums3 = body(1, now.sums3)
-
-    def chain_send(position, first):
-        target, up, index, has_before = chain_at(position)
-        source, device = ref.chip_grad.at[position], link.at(row=row + 2 * up - 1)
-        send_sem = now.chain_send_sem + position
-
-        @pl.when(jnp.logical_not(has_before) if first else has_before)
-        def _():
-            link.arrived(ref.pair_grad.at[target], now.pair_sem + target)
-            own = ref.pair_grad[target].astype(F32) + ref.grad_tokens[target * 2 + pair].astype(F32)
-            if not first:
-                link.arrived(ref.chain_grad.at[index], now.chain_sem + index)
-                own = own + ref.chain_grad[index].astype(F32)
-            ref.chip_grad[position] = own.astype(BF16)
-            link.copy(source, ref.chain_grad.at[index], device, send_sem, now.chain_sem + index).start()
-
-        if not first:
-            link.pending.append((lambda: link.copy(source, source, device, send_sem, 0), None))
+        ref.key_grad[...] = jnp.zeros((tokens, channels), F32)
+        ref.value_grad[...] = jnp.zeros((tokens, channels), F32)
+        now.wait_query_stats = link.share(ref.query_stats)
+
+    def query_back(first, last):
+        top, norm, delta = (ref.query_stats[slot, k : k + 1] for k in range(3))
+
+        def body(step, carry):
+            value = ref.grad_query_t[...]
+            for index in (2 * step, 2 * step + 1):
+                probs = ref.probs[index].astype(F32) * (jnp.exp2(ref.tops[index, 0:1] - top) * norm)
+                grad = mm(ref.tokens[index], ref.grad_low_t[...])
+                grad = (probs * (grad - delta)).astype(BF16)
+                value = value + mm(ref.tokens_t[index], grad)
+            ref.grad_query_t[...] = value
+            return carry
+
+        lax.fori_loop(first, last, body, 0)
+
+    def key_back(position):
+        blocks = blocks_at(position)
+        if position == 0:
+            now.wait_query_stats()
+        now.gres.from_sibling(blocks[1])
+        key_sum, value_sum = ref.key_grad[...], ref.value_grad[...]
+        for lane, index in enumerate(blocks):
+            top, norm, delta = (ref.query_stats[index, k : k + 1] for k in range(3))
+            query = ref.query_all.at[lane]
+            query_of(index, query)
+            scores = mm_t(ref.key[...], query[...])
+            scores = jnp.where(lanes(ref.token_mask[...], tokens) > 0.5, scores, MASKED * LOG2E)
+            probs = jnp.exp2(scores - top) * norm
+            grad = mm_t(ref.value[...], ref.gres_all[index])
+            grad = (probs * (grad - delta)).astype(BF16)
+            key_sum = key_sum + mm(grad, query[...])
+            value_sum = value_sum + mm(probs.astype(BF16), ref.gres_all[index])
+        ref.key_grad[...] = key_sum
+        ref.value_grad[...] = value_sum
 
     def mix_grads():
         grad_query_t = (ref.grad_query_t[...] * now.alive[0:1, 0:1]).astype(BF16)
@@ -892,10 +894,14 @@
         tmask2 = lanes(ref.token_mask[...], channels)
         now.update_sum = fold(update * update * tmask2)
         now.result_sum = fold(value * value * tmask2)
-        own_grad = mm_t(now.grad_query, weights(0))
-        ref.grad_own[...] = own_grad
-        now.grad_sum3 = total(now.sums3[0] + fold(own_grad))
-        now.grad_dot3 = total(now.sums3[1] + fold(own_grad * raw))
+
+    def own_grad():
+        value = mm_t(now.grad_query, weights(0))
+        value = value + mm_t((ref.key_grad[...] * now.alive).astype(BF16), weights(1))
+        value = value + mm_t(ref.value_grad[...].astype(BF16), ref.mix_vo[...])
+        ref.grad_own[...] = value
+        now.grad_sum3 = total(fold(value))
+        now.grad_dot3 = total(fold(value * ref.features[...].astype(F32)))
 
     def conv2():
         def conv2_rows(i, carry):
@@ -999,16 +1005,6 @@
         store("image_grad")
 
     def features_grad():
-        last = n_row - 1
-        link.arrived(ref.pair_grad.at[row], now.pair_sem + row)
-        ref.grad_own[...] += ref.pair_grad[row].astype(F32) + ref.grad_tokens[slot].astype(F32)
-        for index, there in ((last - row, row > 0), (last + row, row < last)):
-
-            @pl.when(there)
-            def _(index=index):
-                link.arrived(ref.chain_grad.at[index], now.chain_sem + index)
-                ref.grad_own[...] += ref.chain_grad[index].astype(F32)
-
         stats, gain = now.stats4, ref.gain3[...]
         grouped = group_total(jnp.concatenate([stats[0:1] * gain, stats[1:2] * gain], axis=0), width2)
         first, second = grouped[0:1] / now.size3, grouped[1:2] / now.size3
@@ -1039,6 +1035,7 @@
     norm1()
     conv1()
     raw_step(1)
+    gres_first()
     queries()
     film()
     attend(0)
@@ -1048,6 +1045,7 @@
     taps1()
     step_a()
     hidden()
+    gres_step(1)
     attend(1)
     image_boxes()
     kernel1_grad()
@@ -1057,34 +1055,33 @@
     for k in range(3, n_row): attend(k)
     step_a()
     attended()
-    back(0)
-    back(1)
-    chain_send(0, True)
+    for k in range(2, min(3, n_row)): gres_step(k)
+    query_back(0, n_row)
+    mix_grads()
     step_a()
-    for k in range(2, n_row - 1): (back(k), chain_send(k - 1, True))
-    back(n_row - 1)
     step_c()
-    mix_grads()
-    chain_send(n_row - 2, True)
-    result()
+    key_back(0)
     step_b()
-    chain_send(0, False)
-    conv2()
+    key_back(1)
+    for k in range(3, n_row): gres_step(k)
+    for k in range(2, min(3, n_row)): key_back(k)
     step_a()
     step_b()
+    for k in range(3, n_row): key_back(k)
+    step_c()
+    result()
+    conv2()
+    step_b()
+    step_c()
     back1()
-    for k in range(1, min(2, n_row - 1)): chain_send(k, False)
-    step_c()
+    own_grad()
     last_share()
     step_a()
     step_b()
-    for k in range(2, n_row - 1): chain_send(k, False)
     step_c()
     last_sums()
     step_b()
     image_grad()
-    step_c()
-    step_b()
     features_grad()
     steps = [now.sum_a, now.sum_c, now.sum_b, now.wait_vectors]
     while steps:
@@ -1131,9 +1128,7 @@
     tokens_t: Any
     query: Any
     query_t: Any
-    query_k: Any
     grad_att: Any
-    grad_t: Any
     column3: Any
     edge3: Any
     stats3: Any
@@ -1163,13 +1158,16 @@
     probs: Any
     mixed_t: Any
     grad_low_t: Any
-    grad_low: Any
     grad_query_t: Any
-    grad_tokens: Any
-    pair_grad: Any
-    chip_grad: Any
-    chain_grad: Any
     grad_own: Any
+    gres_all: Any
+    query_stats: Any
+    mix_vo: Any
+    key: Any
+    value: Any
+    key_grad: Any
+    value_grad: Any
+    query_all: Any
     local_sem: Any
 
 
@@ -1350,8 +1348,8 @@
         ]
 
     scratch = [
-        pltpu.SemaphoreType.DMA((52 + 6 * n_row,)),
-        pltpu.SemaphoreType.DMA((44 + 5 * n_row,)),
+        pltpu.SemaphoreType.DMA((8 * n_row + 33,)),
+        pltpu.SemaphoreType.DMA((4 * n_row + 39,)),
         vmem((n_group, -(-rows_t // 16) * 16, cols_t), BF16),
         vmem((n_group, tokens, channels), BF16),
         vmem((2, span, c_in), BF16),
@@ -1384,8 +1382,6 @@
         vmem((tokens, channels), BF16),
         vmem((channels, tokens), BF16),
         vmem((tokens, channels), BF16),
-        vmem((tokens, channels), BF16),
-        vmem((channels, tokens), F32),
         vmem((16, channels), F32),
         vmem((16, channels), F32),
         vmem((n_group, 2, channels), F32),
@@ -1406,13 +1402,16 @@
         vmem((n_group, tokens, tokens), BF16),
         vmem((channels, tokens), F32),
         vmem((channels, tokens), BF16),
+        vmem((channels, tokens), F32),
+        vmem((tokens, channels), F32),
+        vmem((n_group, tokens, channels), BF16),
+        vmem((n_group, 4, tokens), F32),
+        vmem((channels, channels), BF16),
         vmem((tokens, channels), BF16),
-        vmem((channels, tokens), F32),
-        vmem((n_group, tokens, channels), BF16),
-        vmem((n_row, tokens, channels), BF16),
-        vmem((n_row - 1, tokens, channels), BF16),
-        vmem((2 * (n_row - 1), tokens, channels), BF16),
+        vmem((tokens, channels), BF16),
         vmem((tokens, channels), F32),
+        vmem((tokens, channels), F32),
+        vmem((2, tokens, channels), BF16),
         pltpu.SemaphoreType.DMA((len(FETCHED) + len(RESULTS),)),
         *[vmem(inputs[INPUTS.index(name)].shape, BF16) for name in FETCHED],
     ]

time: 92.7 us -> 86.9 us (0.937)
  the two profiles are of different devices: /device:TPU:27 before, /device:TPU:0 now
where the time goes in v3:
time: 86.9 us; the launch traced here: 86.8 us
  Pallas kernels  85.9 us (99%)
    pallas_call x1, Pallas kernels, on_device(): pl.pallas_call(functools.partial(main_kernel, n_item, n_row), out_shape=m...  80.2 us
    pallas_call x1, Pallas kernels, on_device(): pl.pallas_call(functools.partial(last_kernel, n_item), out_shape=final, i...  5.71 us

profile of v3, /device:TPU:0, one launch (start us, length us, event | category | flops | bytes accessed | tf_op | source)
XLA Modules:
  0.0 86.8 jit_solution(3546076311449437426)
XLA Ops:
  0.7 80.2 %shard_map.416 = (bf16[4,128,256]{2,1,0:T(8,128)(2,1)}, bf16[512,256]{1,0:T(8,128)(2,1)}, bf16[8,256,128]{2,1,0:T(8,128)(2,1)}, bf16[512,256]{1,0:T(8,128)(2,1)}...) custom-call(bf16[8,256,128]{2,1,0:T(8,128)(2,1)} %bitcast.41, ...), custom_call_target="tpu_custom_call" | custom-call | tf_op jit(solution)/shard_map/pallas_call | solution.py:1431
  80.9 5.7 %shard_map.417 = (bf16[4,128,256]{2,1,0:T(8,128)(2,1)}, bf16[512,256]{1,0:T(8,128)(2,1)}, bf16[8,256,128]{2,1,0:T(8,128)(2,1)}, bf16[512,256]{1,0:T(8,128)(2,1)}...) custom-call(bf16[4,128,256]{2,1,0:T(8,128)(2,1)} %get-tuple-element., ...), custom_call_target="tpu_custom_call" | custom-call | tf_op jit(solution)/shard_map/pallas_call | solution.py:1464

commit v4 on v3

--- a/solution.py
+++ b/solution.py
@@ -1044,9 +1044,9 @@
     kernel2_grad()
     taps1()
     step_a()
+    attend(1)
     hidden()
     gres_step(1)
-    attend(1)
     image_boxes()
     kernel1_grad()
     for k in range(3, n_row): raw_step(k)
@@ -1208,7 +1208,7 @@
     held = dict(zip(RESULTS + LAST_BIG, rest))
     in_sem, out_sem = rest[count + len(LAST_BIG) :]
     arrivals = {}
-    for index, name in enumerate(("vectors", "sum_c", "sum_b", "sum_a") + RESULTS[:4]):
+    for index, name in enumerate(("sum_a", "sum_c", "sum_b", "vectors") + RESULTS[:4]):
         arrivals[name] = pltpu.make_async_copy(source[name], held[name], in_sem.at[index])
         arrivals[name].start()
     leaving = []
@@ -1221,6 +1221,26 @@
     o = SimpleNamespace(**target)
     channels, c_in = o.bias1.shape[-1], o.gain1.shape[-1]
 
+    def widen(name, blocks, start, stride):
+        rows, width = held[name].shape
+        for lane in range(width // 128):
+            first = start + lane * stride
+            piece = held[blocks][first : first + rows // 16].reshape(rows, 128)
+            held[name][:, lane * 128 : (lane + 1) * 128] = piece.astype(F32)
+        leave(name)
+
+    rows_a, rows_b, rows_c, rows_k = 9 * channels // 16, channels // 16, 10 * c_in // 16, 9 * c_in // 16
+    arrivals["sum_a"].wait()
+    widen("kernel2", "sum_a", 0, rows_a)
+    arrivals["sum_c"].wait()
+    widen("kernel1", "sum_c", 0, rows_c)
+    widen("skip_w", "sum_c", rows_k, rows_c)
+    arrivals["sum_b"].wait()
+    widen("mix_w", "sum_b", 0, rows_b)
+    widen("out_w", "sum_b", 3 * (channels // 128) * rows_b, rows_b)
+    for name in RESULTS[:4]:
+        arrivals[name].wait()
+        leave(name)
     arrivals["vectors"].wait()
     vectors = held["vectors"]
     value = vectors[0]
@@ -1249,8 +1269,14 @@
         ]
         return jnp.concatenate(rows + [pad], axis=0)
 
+    grads, parts = stacked(14), []
+    for _ in range(3):
+        parts.append(grads.astype(BF16).astype(F32))
+        grads = grads - parts[-1]
+    parts.append(jnp.zeros_like(grads))
+    embedding = jnp.concatenate([stacked(16)] * 4, axis=0).astype(BF16)
     held["film_w"][...] = lax.dot_general(
-        stacked(16), stacked(14), (((0,), (0,)), ((), ())), precision=HIGHEST, preferred_element_type=F32
+        embedding, jnp.concatenate(parts, axis=0).astype(BF16), (((0,), (0,)), ((), ())), preferred_element_type=F32
     )
     leave("film_w")
 
@@ -1271,26 +1297,6 @@
         rms = jnp.where(place == index, jnp.sqrt(square / size), rms)
     o.rms[...] = rms
 
-    def widen(name, blocks, start, stride):
-        rows, width = held[name].shape
-        for lane in range(width // 128):
-            first = start + lane * stride
-            piece = held[blocks][first : first + rows // 16].reshape(rows, 128)
-            held[name][:, lane * 128 : (lane + 1) * 128] = piece.astype(F32)
-        leave(name)
-
-    rows_a, rows_b, rows_c, rows_k = 9 * channels // 16, channels // 16, 10 * c_in // 16, 9 * c_in // 16
-    arrivals["sum_c"].wait()
-    widen("kernel1", "sum_c", 0, rows_c)
-    widen("skip_w", "sum_c", rows_k, rows_c)
-    arrivals["sum_b"].wait()
-    widen("mix_w", "sum_b", 0, rows_b)
-    widen("out_w", "sum_b", 3 * (channels // 128) * rows_b, rows_b)
-    arrivals["sum_a"].wait()
-    widen("kernel2", "sum_a", 0, rows_a)
-    for name in RESULTS[:4]:
-        arrivals[name].wait()
-        leave(name)
     for copy in leaving:
         copy.wait()
 

time: 86.9 us -> 86.5 us (level)
  no operation moved by 1% of the time
where the time goes in v4:
time: 86.5 us; the launch traced here: 86.4 us
  Pallas kernels  85.5 us (99%)
    pallas_call x1, Pallas kernels, on_device(): pl.pallas_call(functools.partial(main_kernel, n_item, n_row), out_shape=m...  80.4 us
    pallas_call x1, Pallas kernels, on_device(): pl.pallas_call(functools.partial(last_kernel, n_item), out_shape=final, i...  5.18 us

profile of v4, /device:TPU:0, one launch (start us, length us, event | category | flops | bytes accessed | tf_op | source)
XLA Modules:
  0.0 86.4 jit_solution(17590576688830711912)
XLA Ops:
  0.7 80.4 %shard_map.416 = (bf16[4,128,256]{2,1,0:T(8,128)(2,1)}, bf16[512,256]{1,0:T(8,128)(2,1)}, bf16[8,256,128]{2,1,0:T(8,128)(2,1)}, bf16[512,256]{1,0:T(8,128)(2,1)}...) custom-call(bf16[8,256,128]{2,1,0:T(8,128)(2,1)} %bitcast.41, ...), custom_call_target="tpu_custom_call" | custom-call | tf_op jit(solution)/shard_map/pallas_call | solution.py:1437
  81.0 5.2 %shard_map.417 = (bf16[4,128,256]{2,1,0:T(8,128)(2,1)}, bf16[512,256]{1,0:T(8,128)(2,1)}, bf16[8,256,128]{2,1,0:T(8,128)(2,1)}, bf16[512,256]{1,0:T(8,128)(2,1)}...) custom-call(bf16[4,128,256]{2,1,0:T(8,128)(2,1)} %get-tuple-element., ...), custom_call_target="tpu_custom_call" | custom-call | tf_op jit(solution)/shard_map/pallas_call | solution.py:1470
